TPU v7x, 256 devices: a whole 4x4x8 slice. The times are simulated.
256 devices in a mesh: section: 32 (over x, y, z_hi), expert: 8 (over z_lo, core).
Axes of the slice: x: 4, y: 4, z: 8 (z_hi: 2, z_lo: 4; z = z_hi * 4 + z_lo), core: 2. Of those that a mesh axis runs over, the one named last changes fastest.
Arguments:
- tokens_in: bfloat16 [8, 128, 2048], P(None, 'expert'), may hold values from -6 to 6
- expert_ids: int32 [32, 8, 128, 2], P('section'), may hold values from 0 to 7, all different within a row; in each aligned block of 16 rows (0 to 15, 16 to 31, ..., all dimensions but the last counted through in order) at most 5 rows name the same one
- router: bfloat16 [32, 2048, 8], P('section'), may hold values from -0.125 to 0.125
- norm_gain: float32 [32, 2048], P('section'), may hold values from 0.25 to 1.75
- w_gate: bfloat16 [32, 8, 2048, 512], P('section', 'expert'), may hold values from -0.125 to 0.125
- w_up: bfloat16 [32, 8, 2048, 512], P('section', 'expert'), may hold values from -0.125 to 0.125
- w_down: bfloat16 [32, 8, 512, 2048], P('section', 'expert'), may hold values from -0.25 to 0.25
Outputs:
- layer_states: float32 [32, 8, 128, 2048], P('section', None, 'expert')
Inputs may be any that keep to these rules, and one draw needn't show every extreme that they name: `expert_ids`: each token names 2 different experts. Within one layer and micro-batch, each aligned block of 16 tokens (the rows of one device) names any one expert at most 5 times.
All inputs are finite; a program needn't handle non-finite values.
Results may differ from a plain program's by a relative error of at most 0.04.
Values may be sent and summed in bfloat16 or wider, within the bound.
No kernel may reach another device: no remote copies, remote signals or barrier semaphores. Data moves between devices by JAX's collectives and lax.ppermute only.
A program may use at most 64 MiB of HBM per device.

v0:
```python
import jax
import jax.numpy as jnp
from jax import lax
from jax.sharding import PartitionSpec as P

norm_epsilon = 1e-06


def passed_along(value, axis, by):
    length = lax.axis_size(axis)
    pairs = [(i, i + by) for i in range(length) if 0 <= i + by < length]
    return lax.ppermute(value, axis, pairs)


def root_mean_norm(hidden, norm_scale):
    mean_square = jnp.mean(hidden * hidden, axis=-1, keepdims=True)
    return (hidden * lax.rsqrt(mean_square + norm_epsilon) * norm_scale).astype(jnp.bfloat16)


def expert_rows(row_block, gate_matrix, up_matrix, down_matrix):
    gate_part = jnp.dot(row_block, gate_matrix, preferred_element_type=jnp.float32)
    up_part = jnp.dot(row_block, up_matrix, preferred_element_type=jnp.float32)
    act = (jax.nn.silu(gate_part) * up_part).astype(jnp.bfloat16)
    return jnp.dot(act, down_matrix, preferred_element_type=jnp.float32).astype(jnp.bfloat16)


def send_back(outputs):
    return lax.all_to_all(outputs, "expert", split_axis=0, concat_axis=0, tiled=True)


def shards(tokens_in, expert_ids, router, norm_gain, w_gate, w_up, w_down):
    sections = lax.axis_size("section")
    experts = lax.axis_size("expert")
    section_id = lax.axis_index("section")
    expert_id = lax.axis_index("expert")
    micro_count, tok_rows, model_width = tokens_in.shape
    top_count = expert_ids.shape[3]
    capacity = min(tok_rows, (5 * tok_rows * top_count + 4 * experts - 1) // (4 * experts))
    slots_all = experts * capacity
    tick_count = micro_count + sections - 1
    gate_matrix = w_gate[0, 0]
    up_matrix = w_up[0, 0]
    down_matrix = w_down[0, 0]
    router_matrix = router[0]
    norm_scale = norm_gain[0]
    columns = jnp.arange(slots_all, dtype=jnp.int32)
    expert_range = jnp.arange(experts, dtype=jnp.int32)

    def slot_targets(route_ids):
        source_count = route_ids.shape[0] // tok_rows
        one_hot = (route_ids[:, :, None] == expert_range[None, None, :]).astype(jnp.int32)
        one_hot = one_hot.reshape(source_count, tok_rows * top_count, experts)
        before = jnp.cumsum(one_hot, axis=1) - one_hot
        slot_index = jnp.sum(before * one_hot, axis=2).reshape(source_count * tok_rows, top_count)
        return route_ids * capacity + slot_index

    def run_experts(received, is_active):
        row_block = received.reshape(-1, model_width)
        produced = lax.cond(
            is_active,
            lambda block_rows: expert_rows(block_rows, gate_matrix, up_matrix, down_matrix),
            lambda block_rows: jnp.zeros_like(block_rows),
            row_block,
        )
        return produced.reshape(received.shape)

    def tick(tick_step, state_pair):
        incoming, stored = state_pair
        micro_index = tick_step - section_id
        is_active = (micro_index >= 0) & (micro_index < micro_count)
        chosen = jnp.clip(micro_index, 0, micro_count - 1)
        entering = lax.dynamic_index_in_dim(tokens_in, chosen, 0, keepdims=False).astype(
            jnp.float32
        )
        hidden = jnp.where(section_id == 0, entering, incoming)
        ids_all = lax.dynamic_index_in_dim(expert_ids[0], chosen, 0, keepdims=False)
        normed = root_mean_norm(hidden, norm_scale)
        logits = jnp.dot(normed, router_matrix, preferred_element_type=jnp.float32)
        targets_all = slot_targets(ids_all)
        ids_own = lax.dynamic_slice_in_dim(ids_all, expert_id * tok_rows, tok_rows, 0)
        targets_own = lax.dynamic_slice_in_dim(targets_all, expert_id * tok_rows, tok_rows, 0)
        picked = jnp.take_along_axis(logits, ids_own, axis=1)
        scores = jax.nn.sigmoid(picked)
        gate_values = scores / jnp.sum(scores, axis=1, keepdims=True)
        match = targets_own[:, :, None] == columns[None, None, :]
        combine_table = jnp.sum(gate_values[:, :, None] * match.astype(jnp.float32), axis=1)
        everyone = lax.all_gather(normed, "expert", axis=0, tiled=True)
        source = jnp.arange(experts * tok_rows, dtype=jnp.int32) // tok_rows
        local_slot = targets_all - ids_all * capacity
        wanted = jnp.where(ids_all == expert_id, source[:, None] * capacity + local_slot, -1)
        pick_table = jnp.sum(
            (wanted[:, :, None] == columns[None, None, :]).astype(jnp.bfloat16), axis=1
        ).T
        received = jnp.dot(pick_table, everyone, preferred_element_type=jnp.float32).astype(
            jnp.bfloat16
        )
        received = received.reshape(experts, capacity, model_width)
        returned = send_back(run_experts(received, is_active))
        mixture = jnp.dot(
            combine_table,
            returned.reshape(slots_all, model_width).astype(jnp.float32),
            precision=lax.Precision.HIGHEST,
        )
        output = hidden + mixture
        written = jnp.where(
            is_active, output, lax.dynamic_index_in_dim(stored, chosen, 0, keepdims=False)
        )
        stored = lax.dynamic_update_index_in_dim(stored, written, chosen, 0)
        incoming = passed_along(output, "section", 1)
        return (incoming, stored)

    start_pair = (
        jnp.zeros((tok_rows, model_width), jnp.float32),
        jnp.zeros((micro_count, tok_rows, model_width), jnp.float32),
    )
    _, stored = lax.fori_loop(0, tick_count, tick, start_pair)
    return stored[None]


def solution(mesh):
    return jax.shard_map(
        shards,
        mesh=mesh,
        in_specs=(
            P(None, "expert", None),
            P("section", None, None, None),
            P("section", None, None),
            P("section", None),
            P("section", "expert", None, None),
            P("section", "expert", None, None),
            P("section", "expert", None, None),
        ),
        out_specs=P("section", None, "expert", None),
        check_vma=False,
    )
```

profile of v0, /device:TPU:31, one launch (start us, length us, event | category | flops | bytes accessed | tf_op | source)
XLA Modules:
  0.0 1938.6 jit_solution(3871352424238341552)
XLA Ops:
  2.0 1936.6 %while.20 = (s32[]{:T(128)}, f32[16,2048]{1,0:T(8,128)S(1)}, f32[8,16,2048]{2,1,0:T(8,128)}, pred[]{:T(512)}, s32[]{:T(128)}, /*index=5*/bf16[8,16,2048]{2,1,0:T...) while((s32[]{:T(128)}, f32[16,2048]{1,0:T(8,128)S(1)}, ...), condition=%wide.region_9.10_spmd.clone.clone, body=%wide.region_0.9_spmd.clone.clone.sunk | while | flops 289702592 | bytes 20245064 | solution.py:116
  5.4 16.5 all_gather.14
  56.7 15.3 all_gather.14
  104.0 15.4 all_gather.14
  152.1 15.2 all_gather.14
  199.5 15.4 all_gather.14
  247.0 15.5 all_gather.14
  295.0 15.2 all_gather.14
  342.4 15.4 all_gather.14
  390.0 15.5 all_gather.14
  438.0 15.2 all_gather.14
  485.4 15.4 all_gather.14
  533.7 15.1 all_gather.14
  582.0 15.1 all_gather.14
  630.3 15.2 all_gather.14
  678.9 15.1 all_gather.14
  726.4 15.4 all_gather.14
  774.6 15.1 all_gather.14
  823.0 15.0 all_gather.14
  871.3 15.1 all_gather.14
  919.8 15.0 all_gather.14
  952.6 12.4 collective-permute-done
  968.4 15.0 all_gather.14
  1000.9 12.9 collective-permute-done
  1017.2 15.2 all_gather.14
  1049.3 12.7 collective-permute-done
  1065.4 15.6 all_gather.14
  1112.9 15.4 all_gather.14
  1160.8 15.4 all_gather.14
  1208.8 15.1 all_gather.14
  1242.0 12.6 collective-permute-done
  1258.0 15.2 all_gather.14
  1290.5 12.4 collective-permute-done
  1306.3 15.8 all_gather.14
  1354.6 15.9 all_gather.14
  1399.5 17.0 all_gather.14
  1434.3 30.7 %collective-permute-done = f32[16,2048]{1,0:T(8,128)S(1)} collective-permute-done((f32[16,2048]{1,0:T(8,128)S(1)}, f32[16,2048]{1,0:T(8,128)S(1)}, u32[]{:S(2)}, u32[]{:S(2)}) %collective-permute-start) | collective-permute-done | bytes 131104 | tf_op jit(solution)/shard_map/while/body/eval_jaxpr/ppermute | solution.py:12
  1468.4 16.5 all_gather.14
  1520.7 16.4 all_gather.14
  1558.7 13.5 collective-permute-done
  1575.5 16.5 all_gather.14
  1626.1 16.5 all_gather.14
  1679.1 16.5 all_gather.14
  1731.2 16.5 all_gather.14
  1769.3 18.7 collective-permute-done
  1791.4 16.5 all_gather.14
  1843.6 19.1 all_gather.14
  1895.2 17.0 all_gather.14
  (1641 shorter events, 1224.0 us)
Async XLA Ops:
  22.9 13.8 all-to-all-start
  38.5 14.8 collective-permute-start
  87.0 13.7 collective-permute-start
  120.4 13.2 all-to-all-start
  135.4 13.3 collective-permute-start
  263.6 13.0 all-to-all-start
  278.4 13.3 collective-permute-start
  406.5 13.0 all-to-all-start
  421.3 13.3 collective-permute-start
  501.9 13.1 all-to-all-start
  516.7 13.6 collective-permute-start
  549.8 13.4 all-to-all-start
  565.0 13.6 collective-permute-start
  598.1 13.4 all-to-all-start
  613.3 13.7 collective-permute-start
  646.5 13.4 all-to-all-start
  661.7 13.8 collective-permute-start
  695.0 13.5 all-to-all-start
  742.9 13.2 all-to-all-start
  757.9 13.4 collective-permute-start
  790.8 13.2 all-to-all-start
  805.7 13.9 collective-permute-start
  839.0 13.2 all-to-all-start
  854.0 13.9 collective-permute-start
  902.3 14.2 collective-permute-start
  935.9 13.0 all-to-all-start
  950.7 14.3 collective-permute-start
  999.0 14.8 collective-permute-start
  1047.4 14.6 collective-permute-start
  1096.0 13.6 collective-permute-start
  1129.4 13.3 all-to-all-start
  1192.1 13.4 collective-permute-start
  1224.9 13.4 all-to-all-start
  1240.1 14.5 collective-permute-start
  1288.6 14.3 collective-permute-start
  1337.1 14.2 collective-permute-start
  1417.6 13.1 all-to-all-start
  1432.4 32.6 %collective-permute-start = (f32[16,2048]{1,0:T(8,128)S(1)}, f32[16,2048]{1,0:T(8,128)S(1)}, u32[]{:S(2)}, u32[]{:S(2)}) collective-permute-start(f32[16,2048]{1,0:T(8,128)S(1)} %get-tuple-element.693), channel_id=1, source_target_pairs={{0,8},{8,16},{16,24},{24,32},{32,40},{40,48},{48,56},{56,64},{64,7... | collective-permute-start | bytes 393224 | tf_op jit(solution)/shard_map/while/body/eval_jaxpr/ppermute | solution.py:12
  1489.5 13.2 all-to-all-start
  1541.8 13.2 all-to-all-start
  1556.7 15.4 collective-permute-start
  1596.6 13.2 all-to-all-start
  1647.3 13.2 all-to-all-start
  1662.2 13.5 collective-permute-start
  1700.2 13.2 all-to-all-start
  1752.3 13.3 all-to-all-start
  1767.4 20.6 %collective-permute-start = (f32[16,2048]{1,0:T(8,128)S(1)}, f32[16,2048]{1,0:T(8,128)S(1)}, u32[]{:S(2)}, u32[]{:S(2)}) collective-permute-start(f32[16,2048]{1,0:T(8,128)S(1)} %get-tuple-element.693), channel_id=1, source_target_pairs={{0,8},{8,16},{16,24},{24,32},{32,40},{40,48},{48,56},{56,64},{64,7... | collective-permute-start | bytes 393224 | tf_op jit(solution)/shard_map/while/body/eval_jaxpr/ppermute | solution.py:12
  1812.5 13.2 all-to-all-start
  (108 other events, 1366.0 us)
where the time goes:
time: 1960 us; the launch traced here: 1940 us
  waiting for transfers between devices  708 us (36%)
  blocking collectives  613 us (31%)
  starting transfers between devices  250 us (13%)
  local copies, waits for them, and re-layouts  133 us (7%)
  other arithmetic  120 us (6%)
  matrix products  109 us (6%)
    all_gather x39, blocking collectives, tick(): everyone = lax.all_gather(normed, 'expert', axis=0, tiled=True)  613 us
    ppermute x39, waiting for transfers between devices, passed_along(): return lax.ppermute(value, axis, pairs)  463 us
    all_to_all x39, waiting for transfers between devices, send_back(): lax.all_to_all(outputs, 'expert', split_axis=0, concat_axis=0, tiled=True)  245 us
    all_to_all x39, starting transfers between devices, send_back(): lax.all_to_all(outputs, 'expert', split_axis=0, concat_axis=0, tiled=True)  167 us
    ppermute x39, starting transfers between devices, passed_along(): return lax.ppermute(value, axis, pairs)  82.6 us
    dot_general x39, matrix products, tick(): jnp.dot(combine_table, returned.reshape(slots_all, model_width).astype(jn...  66.6 us
    reduce_sum x39, other arithmetic, root_mean_norm(): mean_square = jnp.mean(hidden * hidden, axis=-1, keepdims=True)  43.6 us
    gather x195, local copies, waits for them, and re-layouts, tick(): picked = jnp.take_along_axis(logits, ids_own, axis=1)  39.9 us
  transfers between devices with their start and end apart: 78, of which 78 were waited for; matrix products, arithmetic and copies ran while one was open for 5% of the time, Pallas kernels for 0%

commit v1 on v0

v1 whole, which is shorter than its diff:
```python
import functools

import jax
import jax.numpy as jnp
from jax import lax
from jax.experimental import pallas as pl
from jax.experimental.pallas import tpu as pltpu
from jax.sharding import PartitionSpec as P

norm_epsilon = 1e-06
both = ("section", "expert")
z_size = 8
lanes = 128


def normed_of(hidden, norm_scale):
    mean_square = jnp.mean(hidden * hidden, axis=-1, keepdims=True)
    return (hidden * lax.rsqrt(mean_square + norm_epsilon) * norm_scale).astype(jnp.bfloat16)


def norm_kernel(hidden_ref, scale_ref, normed_ref):
    normed_ref[...] = normed_of(hidden_ref[...], scale_ref[...])


def add_norm_kernel(hidden_ref, own_ref, other_ref, scale_ref, sum_ref, normed_ref):
    total = hidden_ref[...] + (own_ref[...] + other_ref[...])
    sum_ref[...] = total
    normed_ref[...] = normed_of(total, scale_ref[...])


def add_kernel(hidden_ref, own_ref, other_ref, sum_ref):
    sum_ref[...] = hidden_ref[...] + (own_ref[...] + other_ref[...])


def experts_kernel(layer_half, place_ref, own_ref, other_ref, ids_ref, router_ref, *refs):
    kept, arrived = refs[:3], refs[3 : 3 + (z_size - 1) * 6]
    own_out, other_out, gates, ups, downs, rows, sems = refs[3 + (z_size - 1) * 6 :]
    active, my_z, my_core = place_ref[0], place_ref[1], place_ref[2]
    held = gates.shape[0]
    width, hidden_units = gates.shape[1:]
    own_rows = own_ref.shape[0]

    def halves_of(ref, *before):
        middle = ref.shape[len(before)] // 2
        return [ref.at[*before, pl.ds(0, middle)], ref.at[*before, pl.ds(middle, middle)]]

    def targets(i):
        return [half for ref in (gates, ups, downs) for half in halves_of(ref, i)]

    sources = [half for ref in kept for half in halves_of(ref)] + list(arrived)

    @pl.when(active == 1)
    def _():
        @pl.loop(0, held)
        def _(i):
            offset = lax.rem(my_z - (layer_half * held + i) + 2 * z_size, z_size)
            for r in range(z_size):

                @pl.when(offset == r)
                def _(r=r):
                    for m, target in enumerate(targets(i)):
                        pltpu.make_async_copy(sources[r * 6 + m], target, sems.at[i, m]).start()

        rows[pl.ds(0, own_rows)] = own_ref[...]
        rows[pl.ds(own_rows, own_rows)] = other_ref[...]
        logits = jnp.dot(rows[...], router_ref[...], preferred_element_type=jnp.float32)
        lane = lax.broadcasted_iota(jnp.int32, logits.shape, 1)
        first = lane == ids_ref[:, 0:1]
        second = lane == ids_ref[:, 1:2]
        zero = jnp.zeros_like(logits)
        score_first = jax.nn.sigmoid(jnp.sum(jnp.where(first, logits, zero), axis=1, keepdims=True))
        score_second = jax.nn.sigmoid(jnp.sum(jnp.where(second, logits, zero), axis=1, keepdims=True))
        score_sum = score_first + score_second
        table = jnp.where(first, score_first / score_sum, zero) + jnp.where(
            second, score_second / score_sum, zero
        )
        own_out[...] = jnp.zeros_like(own_out)
        other_out[...] = jnp.zeros_like(other_out)

        @pl.loop(0, held)
        def _(i):
            for m, target in enumerate(targets(i)):
                pltpu.make_async_copy(sources[m], target, sems.at[i, m]).wait()
            weight = jnp.sum(
                jnp.where(lane == 2 * i + my_core, table, zero), axis=1, keepdims=True
            )
            gate_part = jnp.dot(rows[...], gates[i], preferred_element_type=jnp.float32)
            up_part = jnp.dot(rows[...], ups[i], preferred_element_type=jnp.float32)
            act = (jax.nn.silu(gate_part) * up_part).astype(jnp.bfloat16)
            produced = jnp.dot(act, downs[i], preferred_element_type=jnp.float32)
            part = produced.astype(jnp.bfloat16).astype(jnp.float32) * weight
            own_out[...] += part[:own_rows]
            other_out[...] += part[own_rows:]


def vmem(count):
    return [pl.BlockSpec(memory_space=pltpu.VMEM)] * count


def run_norm(hidden, scale):
    return pl.pallas_call(
        norm_kernel,
        out_shape=jax.ShapeDtypeStruct(hidden.shape, jnp.bfloat16),
        in_specs=vmem(2),
        out_specs=vmem(1)[0],
    )(hidden, scale)


def run_add_norm(hidden, own, other, scale):
    return pl.pallas_call(
        add_norm_kernel,
        out_shape=(
            jax.ShapeDtypeStruct(hidden.shape, jnp.float32),
            jax.ShapeDtypeStruct(hidden.shape, jnp.bfloat16),
        ),
        in_specs=vmem(4),
        out_specs=tuple(vmem(2)),
    )(hidden, own, other, scale)


def run_add(hidden, own, other):
    return pl.pallas_call(
        add_kernel,
        out_shape=jax.ShapeDtypeStruct(hidden.shape, jnp.float32),
        in_specs=vmem(3),
        out_specs=vmem(1)[0],
    )(hidden, own, other)


def run_experts(layer_half, place, own, other, ids, router, sources):
    rows, width = own.shape
    units = sources[0].shape[1]
    held = z_size // 2
    return pl.pallas_call(
        functools.partial(experts_kernel, layer_half),
        out_shape=(jax.ShapeDtypeStruct(own.shape, jnp.float32),) * 2,
        in_specs=[pl.BlockSpec(memory_space=pltpu.SMEM)]
        + vmem(4)
        + [pl.BlockSpec(memory_space=pl.ANY)] * len(sources),
        out_specs=tuple(vmem(2)),
        scratch_shapes=[
            pltpu.VMEM((held, width, units), jnp.bfloat16),
            pltpu.VMEM((held, width, units), jnp.bfloat16),
            pltpu.VMEM((held, units, width), jnp.bfloat16),
            pltpu.VMEM((2 * rows, width), jnp.bfloat16),
            pltpu.SemaphoreType.DMA((held, 6)),
        ],
        compiler_params=pltpu.CompilerParams(vmem_limit_bytes=44 << 20),
    )(place, own, other, ids, router, *sources)


def device_at(ring, z, core):
    half = z_size // 2
    return (ring * 2 + z // half) * z_size + (z % half) * 2 + core


def around(rings, by):
    return [
        (device_at(ring, z, core), device_at(ring, (z + by) % z_size, core))
        for ring in range(rings)
        for z in range(z_size)
        for core in range(2)
    ]


def gather_ring(pieces, rings):
    forward, backward = around(rings, 1), around(rings, -1)
    slots = [[None] * len(pieces) for _ in range(z_size)]
    travelling = list(pieces)
    for step in range(1, z_size):
        for m in range(len(pieces)):
            travelling[m] = lax.ppermute(travelling[m], both, forward if m % 2 == 0 else backward)
            slots[step if m % 2 == 0 else z_size - step][m] = travelling[m]
    return [piece for slot in slots[1:] for piece in slot]


def shards(tokens_in, expert_ids, router, norm_gain, w_gate, w_up, w_down):
    sections = lax.axis_size("section")
    rings = sections // 2
    section_id = lax.axis_index("section")
    expert_id = lax.axis_index("expert")
    ring_id, upper = section_id // 2, section_id % 2
    my_z, my_core = upper * (z_size // 2) + expert_id // 2, expert_id % 2
    micro_count, tok_rows, width = tokens_in.shape
    own_micros = micro_count // 2
    row_count = own_micros * tok_rows
    other_core = [(e, e ^ 1) for e in range(z_size)]
    other_half = [(s, s ^ 1) for s in range(sections)]
    next_ring = [(s, s + 2) for s in range(sections - 2)]

    def halves(matrix):
        middle = matrix.shape[0] // 2
        return [matrix[:middle], matrix[middle:]]

    def both_layers(value):
        theirs = lax.ppermute(value, "section", other_half)
        return jnp.where(upper == 0, value, theirs), jnp.where(upper == 0, theirs, value)

    def rows_of(ids):
        mine = lax.dynamic_slice_in_dim(ids, upper * own_micros, own_micros, 0)
        blocks = [
            lax.dynamic_slice_in_dim(mine, block * tok_rows, tok_rows, 1)
            for block in (expert_id, expert_id ^ 1)
        ]
        return jnp.concatenate([b.reshape(row_count, -1) for b in blocks], axis=0)

    ids = [rows_of(layer) for layer in both_layers(expert_ids[0])]
    scales = both_layers(norm_gain)
    routers = [
        jnp.pad(layer, ((0, 0), (0, lanes - layer.shape[1]))) for layer in both_layers(router[0])
    ]
    matrices = [w_gate[0, 0], w_up[0, 0], w_down[0, 0]]
    sources = matrices + gather_ring([half for matrix in matrices for half in halves(matrix)], rings)
    entering = lax.dynamic_slice_in_dim(tokens_in, upper * own_micros, own_micros, 0)
    hidden = entering.reshape(row_count, width).astype(jnp.float32)

    def exchange(value):
        return lax.ppermute(value, "expert", other_core)

    def ring_step(step, state):
        hidden, stored_first, stored_second = state
        active = ring_id == step
        place = jnp.stack([active.astype(jnp.int32), my_z, my_core])
        normed = run_norm(hidden, scales[0])
        own, lent = run_experts(0, place, normed, exchange(normed), ids[0], routers[0], sources)
        middle, normed = run_add_norm(hidden, own, exchange(lent), scales[1])
        own, lent = run_experts(1, place, normed, exchange(normed), ids[1], routers[1], sources)
        leaving = run_add(middle, own, exchange(lent))
        stored_first = jnp.where(active, middle, stored_first)
        stored_second = jnp.where(active, leaving, stored_second)
        return lax.ppermute(leaving, "section", next_ring), stored_first, stored_second

    blank = jnp.zeros_like(hidden)
    _, stored_first, stored_second = lax.fori_loop(0, rings, ring_step, (hidden, blank, blank))
    kept = jnp.where(upper == 0, stored_first, stored_second)
    given = jnp.where(upper == 0, stored_second, stored_first)
    taken = lax.ppermute(given, "section", other_half)
    low = jnp.where(upper == 0, kept, taken)
    high = jnp.where(upper == 0, taken, kept)
    return jnp.concatenate([low, high], axis=0).reshape(1, micro_count, tok_rows, width)


def solution(mesh):
    return jax.shard_map(
        shards,
        mesh=mesh,
        in_specs=(
            P(None, "expert", None),
            P("section", None, None, None),
            P("section", None, None),
            P("section", None),
            P("section", "expert", None, None),
            P("section", "expert", None, None),
            P("section", "expert", None, None),
        ),
        out_specs=P("section", None, "expert", None),
        check_vma=False,
    )
```

time: 1960 us -> 1450 us (0.74)
  blocking collectives: 613 us -> 0 us
  waiting for transfers between devices: 708 us -> 971 us
  Pallas kernels: 0 us -> 144 us
  matrix products: 109 us -> 0 us
  starting transfers between devices: 250 us -> 175 us
  other arithmetic: 120 us -> 64.9 us
  local copies, waits for them, and re-layouts: 133 us -> 78.2 us
    all_gather x39 -> x0, blocking collectives: 613 us -> none  [tick(): everyone = lax.all_gather(normed, 'expert', axis=0, tiled=True)]
    ppermute x39 -> x126, waiting for transfers between devices: 463 us -> 971 us  [the longest x16 430 us: ring_step(): lax.ppermute(leaving, 'section', next_ring)]
    all_to_all x39 -> x0, waiting for transfers between devices: 245 us -> none  [send_back(): lax.all_to_all(outputs, 'expert', split_axis=0, concat_axis=0, tiled=True)]
    all_to_all x39 -> x0, starting transfers between devices: 167 us -> none  [send_back(): lax.all_to_all(outputs, 'expert', split_axis=0, concat_axis=0, tiled=True)]
    pallas_call x0 -> x80, Pallas kernels: none -> 144 us  [the longest x32 59 us: run_experts(): pl.pallas_call(functools.partial(experts_kernel, layer_half), out_shape=(...]
    dot_general x133 -> x0, matrix products: 109 us -> none  [the longest x39 66.6 us: tick(): jnp.dot(combine_table, returned.reshape(slots_all, model_width).astype(jn...]
    ppermute x39 -> x126, starting transfers between devices: 82.6 us -> 175 us  [the longest x42 108 us: gather_ring(): lax.ppermute(travelling[m], both, forward if m % 2 == 0 else backward)]
    while x156 -> x192, local copies, waits for them, and re-layouts: 0.39 us -> 69.5 us
  transfers between devices with their start and end apart: 78 -> 126, of which waited for: 78 -> 103; matrix products, arithmetic and copies ran while one was open for 5% -> 5% of each run, Pallas kernels for 0% -> 0%
where the time goes in v1:
time: 1450 us; the launch traced here: 1440 us
  waiting for transfers between devices  971 us (67%)
  starting transfers between devices  175 us (12%)
  Pallas kernels  144 us (10%)
  local copies, waits for them, and re-layouts  78.2 us (5%)
  other arithmetic  64.9 us (4%)
    ppermute x16, waiting for transfers between devices, ring_step(): lax.ppermute(leaving, 'section', next_ring)  430 us
    ppermute x42, waiting for transfers between devices, gather_ring(): lax.ppermute(travelling[m], both, forward if m % 2 == 0 else backward)  424 us
    ppermute x42, starting transfers between devices, gather_ring(): lax.ppermute(travelling[m], both, forward if m % 2 == 0 else backward)  108 us
    ppermute x64, waiting for transfers between devices, exchange(): return lax.ppermute(value, 'expert', other_core)  94 us
    while x192, local copies, waits for them, and re-layouts  69.5 us
    pallas_call x32, Pallas kernels, run_experts(): pl.pallas_call(functools.partial(experts_kernel, layer_half), out_shape=(...  59 us
    pallas_call x16, Pallas kernels, run_add(): pl.pallas_call(add_kernel, out_shape=jax.ShapeDtypeStruct(hidden.shape, j...  36 us
    ppermute x64, starting transfers between devices, exchange(): return lax.ppermute(value, 'expert', other_core)  35.4 us
  transfers between devices with their start and end apart: 126, of which 103 were waited for; matrix products, arithmetic and copies ran while one was open for 5% of the time, Pallas kernels for 0%

profile of v1, /device:TPU:31, one launch (start us, length us, event | category | flops | bytes accessed | tf_op | source)
XLA Modules:
  0.0 1435.2 jit_solution(9891184595462244285)
XLA Ops:
  3.2 5.7 collective-permute-start.9
  12.1 4.8 collective-permute-start.7
  17.7 39.1 %collective-permute-start.25 = (bf16[256,2048]{1,0:T(8,128)(2,1)S(1)}, bf16[256,2048]{1,0:T(8,128)(2,1)S(1)}, u32[]{:S(2)}, u32[]{:S(2)}) collective-permute-start(bf16[256,2048]{1,0:T(8,128)(2,1)S(1)} %get-tuple-element.1155), channel_id=1, source_target_pairs={{0,14},{1,15},{2,0},{3,1},{4,2},{5,3},{6,4},{7,5},{8,6},{9,7},{10,... | collective-permute-start | bytes 3145736 | tf_op jit(solution)/shard_map/ppermute | solution.py:172
  56.8 14.9 %collective-permute-start.8 = (bf16[1024,512]{1,0:T(8,128)(2,1)S(1)}, bf16[1024,512]{1,0:T(8,128)(2,1)S(1)}, u32[]{:S(2)}, u32[]{:S(2)}) collective-permute-start(bf16[1024,512]{1,0:T(8,128)(2,1)S(1)} %copy-done.35), channel_id=1, source_target_pairs={{0,2},{1,3},{2,4},{3,5},{4,6},{5,7},{6,8},{7,9},{8,10},{9,11},{10,... | collective-permute-start | bytes 3145736 | tf_op jit(solution)/shard_map/ppermute | solution.py:172
  71.9 9.8 collective-permute-start.24
  81.6 17.4 %collective-permute-done.25 = bf16[256,2048]{1,0:T(8,128)(2,1)S(1)} collective-permute-done((bf16[256,2048]{1,0:T(8,128)(2,1)S(1)}, bf16[256,2048]{1,0:T(8,128)(2,1)S(1)}, u32[]{:S(2)}, u32[]{:S(2)}) %collective-permute-start.25) | collective-permute-done | bytes 1048608 | tf_op jit(solution)/shard_map/ppermute | solution.py:172
  103.4 18.8 %collective-permute-done.16 = bf16[1024,512]{1,0:T(8,128)(2,1)S(1)} collective-permute-done((bf16[1024,512]{1,0:T(8,128)(2,1)S(1)}, bf16[1024,512]{1,0:T(8,128)(2,1)S(1)}, u32[]{:S(2)}, u32[]{:S(2)}) %collective-permute-start.16) | collective-permute-done | bytes 1048608 | tf_op jit(solution)/shard_map/ppermute | solution.py:172
  122.2 22.5 %collective-permute-done.24 = bf16[256,2048]{1,0:T(8,128)(2,1)S(1)} collective-permute-done((bf16[256,2048]{1,0:T(8,128)(2,1)S(1)}, bf16[256,2048]{1,0:T(8,128)(2,1)S(1)}, u32[]{:S(2)}, u32[]{:S(2)}) %collective-permute-start.24) | collective-permute-done | bytes 1048608 | tf_op jit(solution)/shard_map/ppermute | solution.py:172
  147.6 18.8 %collective-permute-done.26 = bf16[256,2048]{1,0:T(8,128)(2,1)S(1)} collective-permute-done((bf16[256,2048]{1,0:T(8,128)(2,1)S(1)}, bf16[256,2048]{1,0:T(8,128)(2,1)S(1)}, u32[]{:S(2)}, u32[]{:S(2)}) %collective-permute-start.26) | collective-permute-done | bytes 1048608 | tf_op jit(solution)/shard_map/ppermute | solution.py:172
  169.9 19.7 %collective-permute-done.33 = bf16[1024,512]{1,0:T(8,128)(2,1)S(1)} collective-permute-done((bf16[1024,512]{1,0:T(8,128)(2,1)S(1)}, bf16[1024,512]{1,0:T(8,128)(2,1)S(1)}, u32[]{:S(2)}, u32[]{:S(2)}) %collective-permute-start.33) | collective-permute-done | bytes 1048608 | tf_op jit(solution)/shard_map/ppermute | solution.py:172
  189.6 22.5 %collective-permute-done.34 = bf16[256,2048]{1,0:T(8,128)(2,1)S(1)} collective-permute-done((bf16[256,2048]{1,0:T(8,128)(2,1)S(1)}, bf16[256,2048]{1,0:T(8,128)(2,1)S(1)}, u32[]{:S(2)}, u32[]{:S(2)}) %collective-permute-start.34) | collective-permute-done | bytes 1048608 | tf_op jit(solution)/shard_map/ppermute | solution.py:172
  215.0 18.9 %collective-permute-done.27 = bf16[256,2048]{1,0:T(8,128)(2,1)S(1)} collective-permute-done((bf16[256,2048]{1,0:T(8,128)(2,1)S(1)}, bf16[256,2048]{1,0:T(8,128)(2,1)S(1)}, u32[]{:S(2)}, u32[]{:S(2)}) %collective-permute-start.27) | collective-permute-done | bytes 1048608 | tf_op jit(solution)/shard_map/ppermute | solution.py:172
  237.4 19.7 %collective-permute-done.36 = bf16[1024,512]{1,0:T(8,128)(2,1)S(1)} collective-permute-done((bf16[1024,512]{1,0:T(8,128)(2,1)S(1)}, bf16[1024,512]{1,0:T(8,128)(2,1)S(1)}, u32[]{:S(2)}, u32[]{:S(2)}) %collective-permute-start.36) | collective-permute-done | bytes 1048608 | tf_op jit(solution)/shard_map/ppermute | solution.py:172
  257.0 22.5 %collective-permute-done.37 = bf16[256,2048]{1,0:T(8,128)(2,1)S(1)} collective-permute-done((bf16[256,2048]{1,0:T(8,128)(2,1)S(1)}, bf16[256,2048]{1,0:T(8,128)(2,1)S(1)}, u32[]{:S(2)}, u32[]{:S(2)}) %collective-permute-start.37) | collective-permute-done | bytes 1048608 | tf_op jit(solution)/shard_map/ppermute | solution.py:172
  282.4 18.9 %collective-permute-done.28 = bf16[256,2048]{1,0:T(8,128)(2,1)S(1)} collective-permute-done((bf16[256,2048]{1,0:T(8,128)(2,1)S(1)}, bf16[256,2048]{1,0:T(8,128)(2,1)S(1)}, u32[]{:S(2)}, u32[]{:S(2)}) %collective-permute-start.28) | collective-permute-done | bytes 1048608 | tf_op jit(solution)/shard_map/ppermute | solution.py:172
  301.3 3.4 collective-permute-start.21
  304.8 19.7 %collective-permute-done.39 = bf16[1024,512]{1,0:T(8,128)(2,1)S(1)} collective-permute-done((bf16[1024,512]{1,0:T(8,128)(2,1)S(1)}, bf16[1024,512]{1,0:T(8,128)(2,1)S(1)}, u32[]{:S(2)}, u32[]{:S(2)}) %collective-permute-start.39) | collective-permute-done | bytes 1048608 | tf_op jit(solution)/shard_map/ppermute | solution.py:172
  324.5 22.6 %collective-permute-done.40 = bf16[256,2048]{1,0:T(8,128)(2,1)} collective-permute-done((bf16[256,2048]{1,0:T(8,128)(2,1)S(1)}, bf16[256,2048]{1,0:T(8,128)(2,1)}, u32[]{:S(2)}, u32[]{:S(2)}) %collective-permute-start.40) | collective-permute-done | bytes 1048608 | tf_op jit(solution)/shard_map/ppermute | solution.py:172
  350.0 18.7 %collective-permute-done.29 = bf16[256,2048]{1,0:T(8,128)(2,1)S(1)} collective-permute-done((bf16[256,2048]{1,0:T(8,128)(2,1)S(1)}, bf16[256,2048]{1,0:T(8,128)(2,1)S(1)}, u32[]{:S(2)}, u32[]{:S(2)}) %collective-permute-start.29) | collective-permute-done | bytes 1048608 | tf_op jit(solution)/shard_map/ppermute | solution.py:172
  373.2 18.8 %collective-permute-done.42 = bf16[1024,512]{1,0:T(8,128)(2,1)} collective-permute-done((bf16[1024,512]{1,0:T(8,128)(2,1)S(1)}, bf16[1024,512]{1,0:T(8,128)(2,1)}, u32[]{:S(2)}, u32[]{:S(2)}) %collective-permute-start.42) | collective-permute-done | bytes 1048608 | tf_op jit(solution)/shard_map/ppermute | solution.py:172
  392.0 22.5 %collective-permute-done.43 = bf16[256,2048]{1,0:T(8,128)(2,1)} collective-permute-done((bf16[256,2048]{1,0:T(8,128)(2,1)}, bf16[256,2048]{1,0:T(8,128)(2,1)}, u32[]{:S(2)}, u32[]{:S(2)}) %collective-permute-start.43) | collective-permute-done | bytes 1048608 | tf_op jit(solution)/shard_map/ppermute | solution.py:172
  417.8 18.4 %collective-permute-done.30 = bf16[256,2048]{1,0:T(8,128)(2,1)} collective-permute-done((bf16[256,2048]{1,0:T(8,128)(2,1)}, bf16[256,2048]{1,0:T(8,128)(2,1)}, u32[]{:S(2)}, u32[]{:S(2)}) %collective-permute-start.30) | collective-permute-done | bytes 1048608 | tf_op jit(solution)/shard_map/ppermute | solution.py:172
  439.6 19.7 %collective-permute-done.45 = bf16[1024,512]{1,0:T(8,128)(2,1)} collective-permute-done((bf16[1024,512]{1,0:T(8,128)(2,1)}, bf16[1024,512]{1,0:T(8,128)(2,1)}, u32[]{:S(2)}, u32[]{:S(2)}) %collective-permute-start.45) | collective-permute-done | bytes 1048608 | tf_op jit(solution)/shard_map/ppermute | solution.py:172
  459.4 22.5 %collective-permute-done.46 = bf16[256,2048]{1,0:T(8,128)(2,1)} collective-permute-done((bf16[256,2048]{1,0:T(8,128)(2,1)}, bf16[256,2048]{1,0:T(8,128)(2,1)}, u32[]{:S(2)}, u32[]{:S(2)}) %collective-permute-start.46) | collective-permute-done | bytes 1048608 | tf_op jit(solution)/shard_map/ppermute | solution.py:172
  487.2 16.4 %collective-permute-done.31 = bf16[256,2048]{1,0:T(8,128)(2,1)} collective-permute-done((bf16[256,2048]{1,0:T(8,128)(2,1)}, bf16[256,2048]{1,0:T(8,128)(2,1)}, u32[]{:S(2)}, u32[]{:S(2)}) %collective-permute-start.31) | collective-permute-done | bytes 1048608 | tf_op jit(solution)/shard_map/ppermute | solution.py:172
  504.3 22.5 %collective-permute-done.48 = bf16[1024,512]{1,0:T(8,128)(2,1)} collective-permute-done((bf16[1024,512]{1,0:T(8,128)(2,1)}, bf16[1024,512]{1,0:T(8,128)(2,1)}, u32[]{:S(2)}, u32[]{:S(2)}) %collective-permute-start.48) | collective-permute-done | bytes 1048608 | tf_op jit(solution)/shard_map/ppermute | solution.py:172
  526.8 22.5 %collective-permute-done.49 = bf16[256,2048]{1,0:T(8,128)(2,1)} collective-permute-done((bf16[256,2048]{1,0:T(8,128)(2,1)}, bf16[256,2048]{1,0:T(8,128)(2,1)}, u32[]{:S(2)}, u32[]{:S(2)}) %collective-permute-start.49) | collective-permute-done | bytes 1048608 | tf_op jit(solution)/shard_map/ppermute | solution.py:172
  549.3 854.2 %while.18 = (s32[]{:T(128)}, f32[64,2048]{1,0:T(8,128)S(1)}, f32[64,2048]{1,0:T(8,128)}, f32[64,2048]{1,0:T(8,128)}, s32[]{:T(128)}, /*index=5*/s32[]{:T(128)}, ...) while((s32[]{:T(128)}, f32[64,2048]{1,0:T(8,128)S(1)}, ...), condition=%wide.region_1.2_spmd.clone, body=%wide.region_0.1_spmd.clone.sunk | while | flops 524299 | bytes 22021016 | solution.py:234
  574.5 12.2 collective-permute-done.4
  612.3 10.1 collective-permute-done.4
  648.0 10.1 collective-permute-done.4
  683.8 10.1 collective-permute-done.4
  719.5 11.1 collective-permute-done.4
  755.9 12.6 collective-permute-done.4
  793.7 12.6 collective-permute-done.4
  831.5 12.6 collective-permute-done.4
  869.4 12.6 collective-permute-done.4
  907.2 12.6 collective-permute-done.4
  945.0 12.6 collective-permute-done.4
  982.9 12.6 collective-permute-done.4
  1020.7 12.6 collective-permute-done.4
  1058.5 12.6 collective-permute-done.4
  1096.4 253.4 %collective-permute-done.4 = f32[64,2048]{1,0:T(8,128)S(1)} collective-permute-done((f32[64,2048]{1,0:T(8,128)}, f32[64,2048]{1,0:T(8,128)S(1)}, u32[]{:S(2)}, u32[]{:S(2)}) %collective-permute-start.4) | collective-permute-done | bytes 524320 | tf_op jit(solution)/shard_map/while/body/eval_jaxpr/ppermute | solution.py:231
  1353.8 10.2 eval_jaxpr.22
  1372.4 10.6 eval_jaxpr.24
  1393.4 10.0 collective-permute-done.4
  1404.6 5.1 collective-permute-start.50
  1409.6 22.9 %collective-permute-done.50 = f32[64,2048]{1,0:T(8,128)S(1)} collective-permute-done((f32[64,2048]{1,0:T(8,128)S(1)}, f32[64,2048]{1,0:T(8,128)S(1)}, u32[]{:S(2)}, u32[]{:S(2)}) %collective-permute-start.50) | collective-permute-done | bytes 524320 | tf_op jit(solution)/shard_map/ppermute | solution.py:237
  (622 shorter events, 453.4 us)
Async XLA Ops:
  3.2 68.6 %collective-permute-start.9 = (bf16[1024,512]{1,0:T(8,128)(2,1)}, bf16[1024,512]{1,0:T(8,128)(2,1)}, u32[]{:S(2)}, u32[]{:S(2)}) collective-permute-start(bf16[1024,512]{1,0:T(8,128)(2,1)} %get-tuple-element.1159), channel_id=1, source_target_pairs={{0,14},{1,15},{2,0},{3,1},{4,2},{5,3},{6,4},{7,5},{8,6},{9,7},{10,... | collective-permute-start | bytes 3145736 | tf_op jit(solution)/shard_map/ppermute | solution.py:172
  10.4 71.3 %collective-permute-start.17 = (bf16[1024,512]{1,0:T(8,128)(2,1)}, bf16[1024,512]{1,0:T(8,128)(2,1)}, u32[]{:S(2)}, u32[]{:S(2)}) collective-permute-start(bf16[1024,512]{1,0:T(8,128)(2,1)} %get-tuple-element.1157), channel_id=1, source_target_pairs={{0,14},{1,15},{2,0},{3,1},{4,2},{5,3},{6,4},{7,5},{8,6},{9,7},{10,... | collective-permute-start | bytes 3145736 | tf_op jit(solution)/shard_map/ppermute | solution.py:172
  12.1 59.7 %collective-permute-start.7 = (bf16[2048,8]{1,0:T(8,128)(2,1)S(1)}, bf16[2048,8]{1,0:T(8,128)(2,1)S(1)}, u32[]{:S(2)}, u32[]{:S(2)}) collective-permute-start(bf16[2048,8]{1,0:T(8,128)(2,1)S(1)} %bitcast.45), channel_id=1, source_target_pairs={{0,8},{8,0},{16,24},{24,16},{32,40},{40,32},{48,56},{56,48},{64,72... | collective-permute-start | bytes 98312 | tf_op jit(solution)/shard_map/ppermute | solution.py:196
  16.9 39.9 %collective-permute-start.5 = (f32[1,2048]{1,0:T(1,128)S(1)}, f32[1,2048]{1,0:T(1,128)S(1)}, u32[]{:S(2)}, u32[]{:S(2)}) collective-permute-start(f32[1,2048]{1,0:T(1,128)S(1)} %copy-done.39), channel_id=1, source_target_pairs={{0,8},{8,0},{16,24},{24,16},{32,40},{40,32},{48,56},{56,48},{64,72... | collective-permute-start | bytes 24584 | tf_op jit(solution)/shard_map/ppermute | solution.py:196
  17.7 81.3 %collective-permute-start.25 = (bf16[256,2048]{1,0:T(8,128)(2,1)S(1)}, bf16[256,2048]{1,0:T(8,128)(2,1)S(1)}, u32[]{:S(2)}, u32[]{:S(2)}) collective-permute-start(bf16[256,2048]{1,0:T(8,128)(2,1)S(1)} %get-tuple-element.1155), channel_id=1, source_target_pairs={{0,14},{1,15},{2,0},{3,1},{4,2},{5,3},{6,4},{7,5},{8,6},{9,7},{10,... | collective-permute-start | bytes 3145736 | tf_op jit(solution)/shard_map/ppermute | solution.py:172
  56.8 45.6 %collective-permute-start.8 = (bf16[1024,512]{1,0:T(8,128)(2,1)S(1)}, bf16[1024,512]{1,0:T(8,128)(2,1)S(1)}, u32[]{:S(2)}, u32[]{:S(2)}) collective-permute-start(bf16[1024,512]{1,0:T(8,128)(2,1)S(1)} %copy-done.35), channel_id=1, source_target_pairs={{0,2},{1,3},{2,4},{3,5},{4,6},{5,7},{6,8},{7,9},{8,10},{9,11},{10,... | collective-permute-start | bytes 3145736 | tf_op jit(solution)/shard_map/ppermute | solution.py:172
  71.8 50.5 %collective-permute-start.16 = (bf16[1024,512]{1,0:T(8,128)(2,1)S(1)}, bf16[1024,512]{1,0:T(8,128)(2,1)S(1)}, u32[]{:S(2)}, u32[]{:S(2)}) collective-permute-start(bf16[1024,512]{1,0:T(8,128)(2,1)S(1)} %copy-done.34), channel_id=1, source_target_pairs={{0,2},{1,3},{2,4},{3,5},{4,6},{5,7},{6,8},{7,9},{8,10},{9,11},{10,... | collective-permute-start | bytes 3145736 | tf_op jit(solution)/shard_map/ppermute | solution.py:172
  71.9 72.8 %collective-permute-start.24 = (bf16[256,2048]{1,0:T(8,128)(2,1)S(1)}, bf16[256,2048]{1,0:T(8,128)(2,1)S(1)}, u32[]{:S(2)}, u32[]{:S(2)}) collective-permute-start(bf16[256,2048]{1,0:T(8,128)(2,1)S(1)} %get-tuple-element.1156), channel_id=1, source_target_pairs={{0,2},{1,3},{2,4},{3,5},{4,6},{5,7},{6,8},{7,9},{8,10},{9,11},{10,... | collective-permute-start | bytes 3145736 | tf_op jit(solution)/shard_map/ppermute | solution.py:172
  81.6 63.0 %collective-permute-start.10 = (bf16[1024,512]{1,0:T(8,128)(2,1)}, bf16[1024,512]{1,0:T(8,128)(2,1)S(1)}, u32[]{:S(2)}, u32[]{:S(2)}) collective-permute-start(bf16[1024,512]{1,0:T(8,128)(2,1)} %collective-permute-done.9), channel_id=1, source_target_pairs={{0,14},{1,15},{2,0},{3,1},{4,2},{5,3},{6,4},{7,5},{8,6},{9,7},{10,... | collective-permute-start | bytes 3145736 | tf_op jit(solution)/shard_map/ppermute | solution.py:172
  99.0 47.2 %collective-permute-start.18 = (bf16[1024,512]{1,0:T(8,128)(2,1)}, bf16[1024,512]{1,0:T(8,128)(2,1)S(1)}, u32[]{:S(2)}, u32[]{:S(2)}) collective-permute-start(bf16[1024,512]{1,0:T(8,128)(2,1)} %collective-permute-done.17), channel_id=1, source_target_pairs={{0,14},{1,15},{2,0},{3,1},{4,2},{5,3},{6,4},{7,5},{8,6},{9,7},{10,... | collective-permute-start | bytes 3145736 | tf_op jit(solution)/shard_map/ppermute | solution.py:172
  102.4 64.0 %collective-permute-start.26 = (bf16[256,2048]{1,0:T(8,128)(2,1)S(1)}, bf16[256,2048]{1,0:T(8,128)(2,1)S(1)}, u32[]{:S(2)}, u32[]{:S(2)}) collective-permute-start(bf16[256,2048]{1,0:T(8,128)(2,1)S(1)} %collective-permute-done.25), channel_id=1, source_target_pairs={{0,14},{1,15},{2,0},{3,1},{4,2},{5,3},{6,4},{7,5},{8,6},{9,7},{10,... | collective-permute-start | bytes 3145736 | tf_op jit(solution)/shard_map/ppermute | solution.py:172
  122.2 47.6 %collective-permute-start.32 = (bf16[1024,512]{1,0:T(8,128)(2,1)S(1)}, bf16[1024,512]{1,0:T(8,128)(2,1)S(1)}, u32[]{:S(2)}, u32[]{:S(2)}) collective-permute-start(bf16[1024,512]{1,0:T(8,128)(2,1)S(1)} %collective-permute-done.8), channel_id=1, source_target_pairs={{0,2},{1,3},{2,4},{3,5},{4,6},{5,7},{6,8},{7,9},{8,10},{9,11},{10,... | collective-permute-start | bytes 3145736 | tf_op jit(solution)/shard_map/ppermute | solution.py:172
  144.7 44.9 %collective-permute-start.33 = (bf16[1024,512]{1,0:T(8,128)(2,1)S(1)}, bf16[1024,512]{1,0:T(8,128)(2,1)S(1)}, u32[]{:S(2)}, u32[]{:S(2)}) collective-permute-start(bf16[1024,512]{1,0:T(8,128)(2,1)S(1)} %collective-permute-done.16), channel_id=1, source_target_pairs={{0,2},{1,3},{2,4},{3,5},{4,6},{5,7},{6,8},{7,9},{8,10},{9,11},{10,... | collective-permute-start | bytes 3145736 | tf_op jit(solution)/shard_map/ppermute | solution.py:172
  144.7 67.4 %collective-permute-start.34 = (bf16[256,2048]{1,0:T(8,128)(2,1)S(1)}, bf16[256,2048]{1,0:T(8,128)(2,1)S(1)}, u32[]{:S(2)}, u32[]{:S(2)}) collective-permute-start(bf16[256,2048]{1,0:T(8,128)(2,1)S(1)} %collective-permute-done.24), channel_id=1, source_target_pairs={{0,2},{1,3},{2,4},{3,5},{4,6},{5,7},{6,8},{7,9},{8,10},{9,11},{10,... | collective-permute-start | bytes 3145736 | tf_op jit(solution)/shard_map/ppermute | solution.py:172
  146.3 65.8 %collective-permute-start.11 = (bf16[1024,512]{1,0:T(8,128)(2,1)S(1)}, bf16[1024,512]{1,0:T(8,128)(2,1)S(1)}, u32[]{:S(2)}, u32[]{:S(2)}) collective-permute-start(bf16[1024,512]{1,0:T(8,128)(2,1)S(1)} %collective-permute-done.10), channel_id=1, source_target_pairs={{0,14},{1,15},{2,0},{3,1},{4,2},{5,3},{6,4},{7,5},{8,6},{9,7},{10,... | collective-permute-start | bytes 3145736 | tf_op jit(solution)/shard_map/ppermute | solution.py:172
  166.4 47.3 %collective-permute-start.19 = (bf16[1024,512]{1,0:T(8,128)(2,1)S(1)}, bf16[1024,512]{1,0:T(8,128)(2,1)S(1)}, u32[]{:S(2)}, u32[]{:S(2)}) collective-permute-start(bf16[1024,512]{1,0:T(8,128)(2,1)S(1)} %collective-permute-done.18), channel_id=1, source_target_pairs={{0,14},{1,15},{2,0},{3,1},{4,2},{5,3},{6,4},{7,5},{8,6},{9,7},{10,... | collective-permute-start | bytes 3145736 | tf_op jit(solution)/shard_map/ppermute | solution.py:172
  169.8 64.0 %collective-permute-start.27 = (bf16[256,2048]{1,0:T(8,128)(2,1)S(1)}, bf16[256,2048]{1,0:T(8,128)(2,1)S(1)}, u32[]{:S(2)}, u32[]{:S(2)}) collective-permute-start(bf16[256,2048]{1,0:T(8,128)(2,1)S(1)} %collective-permute-done.26), channel_id=1, source_target_pairs={{0,14},{1,15},{2,0},{3,1},{4,2},{5,3},{6,4},{7,5},{8,6},{9,7},{10,... | collective-permute-start | bytes 3145736 | tf_op jit(solution)/shard_map/ppermute | solution.py:172
  189.6 47.6 %collective-permute-start.35 = (bf16[1024,512]{1,0:T(8,128)(2,1)S(1)}, bf16[1024,512]{1,0:T(8,128)(2,1)S(1)}, u32[]{:S(2)}, u32[]{:S(2)}) collective-permute-start(bf16[1024,512]{1,0:T(8,128)(2,1)S(1)} %collective-permute-done.32), channel_id=1, source_target_pairs={{0,2},{1,3},{2,4},{3,5},{4,6},{5,7},{6,8},{7,9},{8,10},{9,11},{10,... | collective-permute-start | bytes 3145736 | tf_op jit(solution)/shard_map/ppermute | solution.py:172
  212.1 44.9 %collective-permute-start.36 = (bf16[1024,512]{1,0:T(8,128)(2,1)S(1)}, bf16[1024,512]{1,0:T(8,128)(2,1)S(1)}, u32[]{:S(2)}, u32[]{:S(2)}) collective-permute-start(bf16[1024,512]{1,0:T(8,128)(2,1)S(1)} %collective-permute-done.33), channel_id=1, source_target_pairs={{0,2},{1,3},{2,4},{3,5},{4,6},{5,7},{6,8},{7,9},{8,10},{9,11},{10,... | collective-permute-start | bytes 3145736 | tf_op jit(solution)/shard_map/ppermute | solution.py:172
  212.1 67.4 %collective-permute-start.37 = (bf16[256,2048]{1,0:T(8,128)(2,1)S(1)}, bf16[256,2048]{1,0:T(8,128)(2,1)S(1)}, u32[]{:S(2)}, u32[]{:S(2)}) collective-permute-start(bf16[256,2048]{1,0:T(8,128)(2,1)S(1)} %collective-permute-done.34), channel_id=1, source_target_pairs={{0,2},{1,3},{2,4},{3,5},{4,6},{5,7},{6,8},{7,9},{8,10},{9,11},{10,... | collective-permute-start | bytes 3145736 | tf_op jit(solution)/shard_map/ppermute | solution.py:172
  213.8 65.8 %collective-permute-start.12 = (bf16[1024,512]{1,0:T(8,128)(2,1)S(1)}, bf16[1024,512]{1,0:T(8,128)(2,1)S(1)}, u32[]{:S(2)}, u32[]{:S(2)}) collective-permute-start(bf16[1024,512]{1,0:T(8,128)(2,1)S(1)} %collective-permute-done.11), channel_id=1, source_target_pairs={{0,14},{1,15},{2,0},{3,1},{4,2},{5,3},{6,4},{7,5},{8,6},{9,7},{10,... | collective-permute-start | bytes 3145736 | tf_op jit(solution)/shard_map/ppermute | solution.py:172
  233.8 47.3 %collective-permute-start.20 = (bf16[1024,512]{1,0:T(8,128)(2,1)S(1)}, bf16[1024,512]{1,0:T(8,128)(2,1)S(1)}, u32[]{:S(2)}, u32[]{:S(2)}) collective-permute-start(bf16[1024,512]{1,0:T(8,128)(2,1)S(1)} %collective-permute-done.19), channel_id=1, source_target_pairs={{0,14},{1,15},{2,0},{3,1},{4,2},{5,3},{6,4},{7,5},{8,6},{9,7},{10,... | collective-permute-start | bytes 3145736 | tf_op jit(solution)/shard_map/ppermute | solution.py:172
  237.3 64.0 %collective-permute-start.28 = (bf16[256,2048]{1,0:T(8,128)(2,1)S(1)}, bf16[256,2048]{1,0:T(8,128)(2,1)S(1)}, u32[]{:S(2)}, u32[]{:S(2)}) collective-permute-start(bf16[256,2048]{1,0:T(8,128)(2,1)S(1)} %collective-permute-done.27), channel_id=1, source_target_pairs={{0,14},{1,15},{2,0},{3,1},{4,2},{5,3},{6,4},{7,5},{8,6},{9,7},{10,... | collective-permute-start | bytes 3145736 | tf_op jit(solution)/shard_map/ppermute | solution.py:172
  257.0 47.6 %collective-permute-start.38 = (bf16[1024,512]{1,0:T(8,128)(2,1)S(1)}, bf16[1024,512]{1,0:T(8,128)(2,1)S(1)}, u32[]{:S(2)}, u32[]{:S(2)}) collective-permute-start(bf16[1024,512]{1,0:T(8,128)(2,1)S(1)} %collective-permute-done.35), channel_id=1, source_target_pairs={{0,2},{1,3},{2,4},{3,5},{4,6},{5,7},{6,8},{7,9},{8,10},{9,11},{10,... | collective-permute-start | bytes 3145736 | tf_op jit(solution)/shard_map/ppermute | solution.py:172
  279.5 44.9 %collective-permute-start.39 = (bf16[1024,512]{1,0:T(8,128)(2,1)S(1)}, bf16[1024,512]{1,0:T(8,128)(2,1)S(1)}, u32[]{:S(2)}, u32[]{:S(2)}) collective-permute-start(bf16[1024,512]{1,0:T(8,128)(2,1)S(1)} %collective-permute-done.36), channel_id=1, source_target_pairs={{0,2},{1,3},{2,4},{3,5},{4,6},{5,7},{6,8},{7,9},{8,10},{9,11},{10,... | collective-permute-start | bytes 3145736 | tf_op jit(solution)/shard_map/ppermute | solution.py:172
  279.5 67.5 %collective-permute-start.40 = (bf16[256,2048]{1,0:T(8,128)(2,1)S(1)}, bf16[256,2048]{1,0:T(8,128)(2,1)}, u32[]{:S(2)}, u32[]{:S(2)}) collective-permute-start(bf16[256,2048]{1,0:T(8,128)(2,1)S(1)} %collective-permute-done.37), channel_id=1, source_target_pairs={{0,2},{1,3},{2,4},{3,5},{4,6},{5,7},{6,8},{7,9},{8,10},{9,11},{10,... | collective-permute-start | bytes 3145736 | tf_op jit(solution)/shard_map/ppermute | solution.py:172
  281.2 66.1 %collective-permute-start.13 = (bf16[1024,512]{1,0:T(8,128)(2,1)S(1)}, bf16[1024,512]{1,0:T(8,128)(2,1)}, u32[]{:S(2)}, u32[]{:S(2)}) collective-permute-start(bf16[1024,512]{1,0:T(8,128)(2,1)S(1)} %collective-permute-done.12), channel_id=1, source_target_pairs={{0,14},{1,15},{2,0},{3,1},{4,2},{5,3},{6,4},{7,5},{8,6},{9,7},{10,... | collective-permute-start | bytes 3145736 | tf_op jit(solution)/shard_map/ppermute | solution.py:172
  301.3 47.4 %collective-permute-start.21 = (bf16[1024,512]{1,0:T(8,128)(2,1)S(1)}, bf16[1024,512]{1,0:T(8,128)(2,1)}, u32[]{:S(2)}, u32[]{:S(2)}) collective-permute-start(bf16[1024,512]{1,0:T(8,128)(2,1)S(1)} %collective-permute-done.20), channel_id=1, source_target_pairs={{0,14},{1,15},{2,0},{3,1},{4,2},{5,3},{6,4},{7,5},{8,6},{9,7},{10,... | collective-permute-start | bytes 3145736 | tf_op jit(solution)/shard_map/ppermute | solution.py:172
  304.7 64.0 %collective-permute-start.29 = (bf16[256,2048]{1,0:T(8,128)(2,1)S(1)}, bf16[256,2048]{1,0:T(8,128)(2,1)S(1)}, u32[]{:S(2)}, u32[]{:S(2)}) collective-permute-start(bf16[256,2048]{1,0:T(8,128)(2,1)S(1)} %collective-permute-done.28), channel_id=1, source_target_pairs={{0,14},{1,15},{2,0},{3,1},{4,2},{5,3},{6,4},{7,5},{8,6},{9,7},{10,... | collective-permute-start | bytes 3145736 | tf_op jit(solution)/shard_map/ppermute | solution.py:172
  324.4 48.6 %collective-permute-start.41 = (bf16[1024,512]{1,0:T(8,128)(2,1)S(1)}, bf16[1024,512]{1,0:T(8,128)(2,1)}, u32[]{:S(2)}, u32[]{:S(2)}) collective-permute-start(bf16[1024,512]{1,0:T(8,128)(2,1)S(1)} %collective-permute-done.38), channel_id=1, source_target_pairs={{0,2},{1,3},{2,4},{3,5},{4,6},{5,7},{6,8},{7,9},{8,10},{9,11},{10,... | collective-permute-start | bytes 3145736 | tf_op jit(solution)/shard_map/ppermute | solution.py:172
  347.0 44.9 %collective-permute-start.42 = (bf16[1024,512]{1,0:T(8,128)(2,1)S(1)}, bf16[1024,512]{1,0:T(8,128)(2,1)}, u32[]{:S(2)}, u32[]{:S(2)}) collective-permute-start(bf16[1024,512]{1,0:T(8,128)(2,1)S(1)} %collective-permute-done.39), channel_id=1, source_target_pairs={{0,2},{1,3},{2,4},{3,5},{4,6},{5,7},{6,8},{7,9},{8,10},{9,11},{10,... | collective-permute-start | bytes 3145736 | tf_op jit(solution)/shard_map/ppermute | solution.py:172
  347.2 67.2 %collective-permute-start.43 = (bf16[256,2048]{1,0:T(8,128)(2,1)}, bf16[256,2048]{1,0:T(8,128)(2,1)}, u32[]{:S(2)}, u32[]{:S(2)}) collective-permute-start(bf16[256,2048]{1,0:T(8,128)(2,1)} %collective-permute-done.40), channel_id=1, source_target_pairs={{0,2},{1,3},{2,4},{3,5},{4,6},{5,7},{6,8},{7,9},{8,10},{9,11},{10,... | collective-permute-start | bytes 3145736 | tf_op jit(solution)/shard_map/ppermute | solution.py:172
  348.7 65.7 %collective-permute-start.14 = (bf16[1024,512]{1,0:T(8,128)(2,1)}, bf16[1024,512]{1,0:T(8,128)(2,1)}, u32[]{:S(2)}, u32[]{:S(2)}) collective-permute-start(bf16[1024,512]{1,0:T(8,128)(2,1)} %collective-permute-done.13), channel_id=1, source_target_pairs={{0,14},{1,15},{2,0},{3,1},{4,2},{5,3},{6,4},{7,5},{8,6},{9,7},{10,... | collective-permute-start | bytes 3145736 | tf_op jit(solution)/shard_map/ppermute | solution.py:172
  369.6 46.4 %collective-permute-start.22 = (bf16[1024,512]{1,0:T(8,128)(2,1)}, bf16[1024,512]{1,0:T(8,128)(2,1)}, u32[]{:S(2)}, u32[]{:S(2)}) collective-permute-start(bf16[1024,512]{1,0:T(8,128)(2,1)} %collective-permute-done.21), channel_id=1, source_target_pairs={{0,14},{1,15},{2,0},{3,1},{4,2},{5,3},{6,4},{7,5},{8,6},{9,7},{10,... | collective-permute-start | bytes 3145736 | tf_op jit(solution)/shard_map/ppermute | solution.py:172
  373.1 63.1 %collective-permute-start.30 = (bf16[256,2048]{1,0:T(8,128)(2,1)}, bf16[256,2048]{1,0:T(8,128)(2,1)}, u32[]{:S(2)}, u32[]{:S(2)}) collective-permute-start(bf16[256,2048]{1,0:T(8,128)(2,1)} %copy-done.30), channel_id=1, source_target_pairs={{0,14},{1,15},{2,0},{3,1},{4,2},{5,3},{6,4},{7,5},{8,6},{9,7},{10,... | collective-permute-start | bytes 3145736 | tf_op jit(solution)/shard_map/ppermute | solution.py:172
  392.0 47.6 %collective-permute-start.44 = (bf16[1024,512]{1,0:T(8,128)(2,1)}, bf16[1024,512]{1,0:T(8,128)(2,1)}, u32[]{:S(2)}, u32[]{:S(2)}) collective-permute-start(bf16[1024,512]{1,0:T(8,128)(2,1)} %collective-permute-done.41), channel_id=1, source_target_pairs={{0,2},{1,3},{2,4},{3,5},{4,6},{5,7},{6,8},{7,9},{8,10},{9,11},{10,... | collective-permute-start | bytes 3145736 | tf_op jit(solution)/shard_map/ppermute | solution.py:172
  414.4 44.9 %collective-permute-start.45 = (bf16[1024,512]{1,0:T(8,128)(2,1)}, bf16[1024,512]{1,0:T(8,128)(2,1)}, u32[]{:S(2)}, u32[]{:S(2)}) collective-permute-start(bf16[1024,512]{1,0:T(8,128)(2,1)} %collective-permute-done.42), channel_id=1, source_target_pairs={{0,2},{1,3},{2,4},{3,5},{4,6},{5,7},{6,8},{7,9},{8,10},{9,11},{10,... | collective-permute-start | bytes 3145736 | tf_op jit(solution)/shard_map/ppermute | solution.py:172
  414.4 67.4 %collective-permute-start.46 = (bf16[256,2048]{1,0:T(8,128)(2,1)}, bf16[256,2048]{1,0:T(8,128)(2,1)}, u32[]{:S(2)}, u32[]{:S(2)}) collective-permute-start(bf16[256,2048]{1,0:T(8,128)(2,1)} %collective-permute-done.43), channel_id=1, source_target_pairs={{0,2},{1,3},{2,4},{3,5},{4,6},{5,7},{6,8},{7,9},{8,10},{9,11},{10,... | collective-permute-start | bytes 3145736 | tf_op jit(solution)/shard_map/ppermute | solution.py:172
  416.0 65.8 %collective-permute-start.15 = (bf16[1024,512]{1,0:T(8,128)(2,1)}, bf16[1024,512]{1,0:T(8,128)(2,1)}, u32[]{:S(2)}, u32[]{:S(2)}) collective-permute-start(bf16[1024,512]{1,0:T(8,128)(2,1)} %collective-permute-done.14), channel_id=1, source_target_pairs={{0,14},{1,15},{2,0},{3,1},{4,2},{5,3},{6,4},{7,5},{8,6},{9,7},{10,... | collective-permute-start | bytes 3145736 | tf_op jit(solution)/shard_map/ppermute | solution.py:172
  436.2 51.0 %collective-permute-start.23 = (bf16[1024,512]{1,0:T(8,128)(2,1)}, bf16[1024,512]{1,0:T(8,128)(2,1)}, u32[]{:S(2)}, u32[]{:S(2)}) collective-permute-start(bf16[1024,512]{1,0:T(8,128)(2,1)} %collective-permute-done.22), channel_id=1, source_target_pairs={{0,14},{1,15},{2,0},{3,1},{4,2},{5,3},{6,4},{7,5},{8,6},{9,7},{10,... | collective-permute-start | bytes 3145736 | tf_op jit(solution)/shard_map/ppermute | solution.py:172
  439.6 64.0 %collective-permute-start.31 = (bf16[256,2048]{1,0:T(8,128)(2,1)}, bf16[256,2048]{1,0:T(8,128)(2,1)}, u32[]{:S(2)}, u32[]{:S(2)}) collective-permute-start(bf16[256,2048]{1,0:T(8,128)(2,1)} %collective-permute-done.30), channel_id=1, source_target_pairs={{0,14},{1,15},{2,0},{3,1},{4,2},{5,3},{6,4},{7,5},{8,6},{9,7},{10,... | collective-permute-start | bytes 3145736 | tf_op jit(solution)/shard_map/ppermute | solution.py:172
  459.4 44.9 %collective-permute-start.47 = (bf16[1024,512]{1,0:T(8,128)(2,1)}, bf16[1024,512]{1,0:T(8,128)(2,1)}, u32[]{:S(2)}, u32[]{:S(2)}) collective-permute-start(bf16[1024,512]{1,0:T(8,128)(2,1)} %collective-permute-done.44), channel_id=1, source_target_pairs={{0,2},{1,3},{2,4},{3,5},{4,6},{5,7},{6,8},{7,9},{8,10},{9,11},{10,... | collective-permute-start | bytes 3145736 | tf_op jit(solution)/shard_map/ppermute | solution.py:172
  481.8 44.9 %collective-permute-start.48 = (bf16[1024,512]{1,0:T(8,128)(2,1)}, bf16[1024,512]{1,0:T(8,128)(2,1)}, u32[]{:S(2)}, u32[]{:S(2)}) collective-permute-start(bf16[1024,512]{1,0:T(8,128)(2,1)} %collective-permute-done.45), channel_id=1, source_target_pairs={{0,2},{1,3},{2,4},{3,5},{4,6},{5,7},{6,8},{7,9},{8,10},{9,11},{10,... | collective-permute-start | bytes 3145736 | tf_op jit(solution)/shard_map/ppermute | solution.py:172
  481.8 67.4 %collective-permute-start.49 = (bf16[256,2048]{1,0:T(8,128)(2,1)}, bf16[256,2048]{1,0:T(8,128)(2,1)}, u32[]{:S(2)}, u32[]{:S(2)}) collective-permute-start(bf16[256,2048]{1,0:T(8,128)(2,1)} %collective-permute-done.46), channel_id=1, source_target_pairs={{0,2},{1,3},{2,4},{3,5},{4,6},{5,7},{6,8},{7,9},{8,10},{9,11},{10,... | collective-permute-start | bytes 3145736 | tf_op jit(solution)/shard_map/ppermute | solution.py:172
  750.8 17.7 %collective-permute-start.4 = (f32[64,2048]{1,0:T(8,128)}, f32[64,2048]{1,0:T(8,128)S(1)}, u32[]{:S(2)}, u32[]{:S(2)}) collective-permute-start(f32[64,2048]{1,0:T(8,128)} %eval_jaxpr.25), channel_id=1, source_target_pairs={{0,16},{8,24},{16,32},{24,40},{32,48},{40,56},{48,64},{56,72},{64,... | collective-permute-start | bytes 1572872 | tf_op jit(solution)/shard_map/while/body/eval_jaxpr/ppermute | solution.py:231
  1015.6 17.7 %collective-permute-start.4 = (f32[64,2048]{1,0:T(8,128)}, f32[64,2048]{1,0:T(8,128)S(1)}, u32[]{:S(2)}, u32[]{:S(2)}) collective-permute-start(f32[64,2048]{1,0:T(8,128)} %eval_jaxpr.25), channel_id=1, source_target_pairs={{0,16},{8,24},{16,32},{24,40},{32,48},{40,56},{48,64},{56,72},{64,... | collective-permute-start | bytes 1572872 | tf_op jit(solution)/shard_map/while/body/eval_jaxpr/ppermute | solution.py:231
  1091.3 258.5 %collective-permute-start.4 = (f32[64,2048]{1,0:T(8,128)}, f32[64,2048]{1,0:T(8,128)S(1)}, u32[]{:S(2)}, u32[]{:S(2)}) collective-permute-start(f32[64,2048]{1,0:T(8,128)} %eval_jaxpr.25), channel_id=1, source_target_pairs={{0,16},{8,24},{16,32},{24,40},{32,48},{40,56},{48,64},{56,72},{64,... | collective-permute-start | bytes 1572872 | tf_op jit(solution)/shard_map/while/body/eval_jaxpr/ppermute | solution.py:231
  1404.6 28.0 %collective-permute-start.50 = (f32[64,2048]{1,0:T(8,128)S(1)}, f32[64,2048]{1,0:T(8,128)S(1)}, u32[]{:S(2)}, u32[]{:S(2)}) collective-permute-start(f32[64,2048]{1,0:T(8,128)S(1)} %broadcast_select_fusion.4), channel_id=1, source_target_pairs={{0,8},{8,0},{16,24},{24,16},{32,40},{40,32},{48,56},{56,48},{64,72... | collective-permute-start | bytes 1572872 | tf_op jit(solution)/shard_map/ppermute | solution.py:237
  (208 other events, 2845.7 us)

commit v2 on v1

v2 whole, which is shorter than its diff:
```python
import functools

import jax
import jax.numpy as jnp
from jax import lax
from jax.experimental import pallas as pl
from jax.experimental.pallas import tpu as pltpu
from jax.sharding import PartitionSpec as P

norm_epsilon = 1e-06
both = ("section", "expert")
z_size = 8
source_count = 3 + (z_size - 1) * 6
lanes = 128


def normed_of(hidden, norm_scale):
    mean_square = jnp.mean(hidden * hidden, axis=-1, keepdims=True)
    return (hidden * lax.rsqrt(mean_square + norm_epsilon) * norm_scale).astype(jnp.bfloat16)


def layer_copies(layer_half, my_z, refs, loaded, sems):
    kept, arrived = refs[:3], refs[3:]
    held = z_size // 2

    def halves_of(ref, *before):
        middle = ref.shape[len(before)] // 2
        return [ref.at[*before, pl.ds(0, middle)], ref.at[*before, pl.ds(middle, middle)]]

    def targets(i):
        return [half for ref in loaded for half in halves_of(ref, i)]

    sources = [half for ref in kept for half in halves_of(ref)] + list(arrived)

    def start():
        @pl.loop(0, held)
        def _(i):
            offset = lax.rem(my_z - (layer_half * held + i) + 2 * z_size, z_size)
            for r in range(z_size):

                @pl.when(offset == r)
                def _(r=r):
                    for m, target in enumerate(targets(i)):
                        pltpu.make_async_copy(sources[r * 6 + m], target, sems.at[i, m]).start()

    def wait(i):
        for m, target in enumerate(targets(i)):
            pltpu.make_async_copy(sources[m], target, sems.at[i, m]).wait()

    return start, wait


def load_kernel(place_ref, *refs):
    sources, loaded, sems = refs[:source_count], refs[source_count:-1], refs[-1]
    start, wait = layer_copies(0, place_ref[1], sources, loaded, sems)

    @pl.when(place_ref[0] == 1)
    def _():
        start()
        pl.loop(0, z_size // 2)(wait)


def experts_sum(my_core, rows, ids_ref, router_ref, gates, ups, downs, total, wait=None):
    logits = jnp.dot(rows[...], router_ref[...], preferred_element_type=jnp.float32)
    lane = lax.broadcasted_iota(jnp.int32, logits.shape, 1)
    first = lane == ids_ref[:, 0:1]
    second = lane == ids_ref[:, 1:2]
    zero = jnp.zeros_like(logits)
    score_first = jax.nn.sigmoid(jnp.sum(jnp.where(first, logits, zero), axis=1, keepdims=True))
    score_second = jax.nn.sigmoid(jnp.sum(jnp.where(second, logits, zero), axis=1, keepdims=True))
    score_sum = score_first + score_second
    table = jnp.where(first, score_first / score_sum, zero) + jnp.where(
        second, score_second / score_sum, zero
    )
    total[...] = jnp.zeros_like(total)

    @pl.loop(0, gates.shape[0])
    def _(i):
        if wait is not None:
            wait(i)
        weight = jnp.sum(jnp.where(lane == 2 * i + my_core, table, zero), axis=1, keepdims=True)
        gate_part = jnp.dot(rows[...], gates[i], preferred_element_type=jnp.float32)
        up_part = jnp.dot(rows[...], ups[i], preferred_element_type=jnp.float32)
        act = (jax.nn.silu(gate_part) * up_part).astype(jnp.bfloat16)
        produced = jnp.dot(act, downs[i], preferred_element_type=jnp.float32)
        total[...] += produced.astype(jnp.bfloat16).astype(jnp.float32) * weight


def first_kernel(
    place_ref, mine_ref, other_ref, scale_ref, ids_ref, router_ref, gates, ups, downs,
    part_ref, lent_ref, rows,
):
    count = mine_ref.shape[0]

    @pl.when(place_ref[0] == 1)
    def _():
        rows[pl.ds(0, count)] = normed_of(mine_ref[...].astype(jnp.float32), scale_ref[...])
        rows[pl.ds(count, count)] = normed_of(other_ref[...].astype(jnp.float32), scale_ref[...])
        experts_sum(place_ref[2], rows, ids_ref, router_ref, gates, ups, downs, part_ref)
        lent_ref[...] = part_ref[...].astype(jnp.bfloat16)


def second_kernel(
    place_ref, mine_ref, other_ref, part_ref, back_ref, scale_ref, ids_ref, router_ref, stored_ref, *refs
):
    sources = refs[:source_count]
    middle_ref, own_ref, lent_ref, gates, ups, downs, rows, total, sems = refs[source_count:]
    count = mine_ref.shape[0]
    start, wait = layer_copies(1, place_ref[1], sources, (gates, ups, downs), sems)

    @pl.when(place_ref[0] == 1)
    def _():
        start()
        middle = mine_ref[...].astype(jnp.float32) + (
            part_ref[:count] + back_ref[count:].astype(jnp.float32)
        )
        middle_ref[...] = middle
        rows[pl.ds(0, count)] = normed_of(middle, scale_ref[...])
        beside = other_ref[...].astype(jnp.float32) + (
            part_ref[count:] + back_ref[:count].astype(jnp.float32)
        )
        rows[pl.ds(count, count)] = normed_of(beside, scale_ref[...])
        experts_sum(place_ref[2], rows, ids_ref, router_ref, gates, ups, downs, total, wait)
        own_ref[...] = total[:count]
        lent_ref[...] = total[count:].astype(jnp.bfloat16)

    @pl.when(place_ref[0] == 0)
    def _():
        middle_ref[...] = stored_ref[...]


def add_kernel(place_ref, middle_ref, own_ref, back_ref, stored_ref, sum_ref, sent_ref):
    @pl.when(place_ref[0] == 1)
    def _():
        total = middle_ref[...] + (own_ref[...] + back_ref[...].astype(jnp.float32))
        sum_ref[...] = total
        sent_ref[...] = total.astype(jnp.bfloat16)

    @pl.when(place_ref[0] == 0)
    def _():
        sum_ref[...] = stored_ref[...]


def vmem(count):
    return [pl.BlockSpec(memory_space=pltpu.VMEM)] * count


def like(shape, kind):
    return jax.ShapeDtypeStruct(shape, kind)


def layer_shapes(sources):
    width, units = sources[0].shape
    held = z_size // 2
    return [(held, width, units), (held, width, units), (held, units, width)]


def copy_sems():
    return pltpu.SemaphoreType.DMA((z_size // 2, 6))


def in_hbm(sources):
    return [pl.BlockSpec(memory_space=pltpu.HBM)] * len(sources)


def load_first(place, sources):
    width, units = sources[0].shape
    return pl.pallas_call(
        load_kernel,
        out_shape=tuple(pltpu.VMEM(shape, jnp.bfloat16) for shape in layer_shapes(sources)),
        in_specs=[pl.BlockSpec(memory_space=pltpu.SMEM)] + in_hbm(sources),
        out_specs=tuple(vmem(3)),
        scratch_shapes=[copy_sems()],
        compiler_params=pltpu.CompilerParams(vmem_limit_bytes=1 << 20),
        cost_estimate=pl.CostEstimate(
            flops=0, bytes_accessed=3 * z_size * width * units, transcendentals=0
        ),
    )(place, *sources)


def run_first(place, mine, other, scale, ids, router, weights):
    count, width = mine.shape
    return pl.pallas_call(
        first_kernel,
        out_shape=(like((2 * count, width), jnp.float32), like((2 * count, width), jnp.bfloat16)),
        in_specs=[pl.BlockSpec(memory_space=pltpu.SMEM)] + vmem(8),
        out_specs=tuple(vmem(2)),
        scratch_shapes=[pltpu.VMEM((2 * count, width), jnp.bfloat16)],
        compiler_params=pltpu.CompilerParams(vmem_limit_bytes=8 << 20),
    )(place, mine, other, scale, ids, router, *weights)


def run_second(place, mine, other, part, back, scale, ids, router, stored, sources):
    count, width = mine.shape
    return pl.pallas_call(
        second_kernel,
        out_shape=(
            like((count, width), jnp.float32),
            like((count, width), jnp.float32),
            like((count, width), jnp.bfloat16),
        ),
        in_specs=[pl.BlockSpec(memory_space=pltpu.SMEM)] + vmem(8) + in_hbm(sources),
        out_specs=tuple(vmem(3)),
        scratch_shapes=[pltpu.VMEM(shape, jnp.bfloat16) for shape in layer_shapes(sources)]
        + [
            pltpu.VMEM((2 * count, width), jnp.bfloat16),
            pltpu.VMEM((2 * count, width), jnp.float32),
            copy_sems(),
        ],
        input_output_aliases={8: 0},
        compiler_params=pltpu.CompilerParams(vmem_limit_bytes=34 << 20),
    )(place, mine, other, part, back, scale, ids, router, stored, *sources)


def run_add(place, middle, own, back, stored):
    return pl.pallas_call(
        add_kernel,
        out_shape=(like(middle.shape, jnp.float32), like(middle.shape, jnp.bfloat16)),
        in_specs=[pl.BlockSpec(memory_space=pltpu.SMEM)] + vmem(4),
        out_specs=tuple(vmem(2)),
        input_output_aliases={4: 0},
        compiler_params=pltpu.CompilerParams(vmem_limit_bytes=4 << 20),
    )(place, middle, own, back, stored)


def device_at(ring, z, core):
    half = z_size // 2
    return (ring * 2 + z // half) * z_size + (z % half) * 2 + core


def around(rings, by):
    return [
        (device_at(ring, z, core), device_at(ring, (z + by) % z_size, core))
        for ring in range(rings)
        for z in range(z_size)
        for core in range(2)
    ]


def gather_ring(pieces, rings):
    forward, backward = around(rings, 1), around(rings, -1)
    slots = [[None] * len(pieces) for _ in range(z_size)]
    travelling = list(pieces)
    for step in range(1, z_size):
        for m in range(len(pieces)):
            travelling[m] = lax.ppermute(travelling[m], both, forward if m % 2 == 0 else backward)
            slots[step if m % 2 == 0 else z_size - step][m] = travelling[m]
    return [piece for slot in slots[1:] for piece in slot]


def shards(tokens_in, expert_ids, router, norm_gain, w_gate, w_up, w_down):
    sections = lax.axis_size("section")
    rings = sections // 2
    section_id = lax.axis_index("section")
    expert_id = lax.axis_index("expert")
    ring_id, upper = section_id // 2, section_id % 2
    my_z, my_core = upper * (z_size // 2) + expert_id // 2, expert_id % 2
    micro_count, tok_rows, width = tokens_in.shape
    own_micros = micro_count // 2
    row_count = own_micros * tok_rows
    other_core = [(e, e ^ 1) for e in range(z_size)]
    other_half = [(s, s ^ 1) for s in range(sections)]
    next_ring = [(s, (s + 2) % sections) for s in range(sections)]

    def halves(matrix):
        middle = matrix.shape[0] // 2
        return [matrix[:middle], matrix[middle:]]

    def both_layers(value):
        theirs = lax.ppermute(value, "section", other_half)
        return jnp.where(upper == 0, value, theirs), jnp.where(upper == 0, theirs, value)

    def rows_of(ids):
        mine = lax.dynamic_slice_in_dim(ids, upper * own_micros, own_micros, 0)
        blocks = [
            lax.dynamic_slice_in_dim(mine, block * tok_rows, tok_rows, 1)
            for block in (expert_id, expert_id ^ 1)
        ]
        return jnp.concatenate([b.reshape(row_count, -1) for b in blocks], axis=0)

    ids = [rows_of(layer) for layer in both_layers(expert_ids[0])]
    scales = both_layers(norm_gain)
    routers = [
        jnp.pad(layer, ((0, 0), (0, lanes - layer.shape[1]))) for layer in both_layers(router[0])
    ]
    matrices = [w_gate[0, 0], w_up[0, 0], w_down[0, 0]]
    sources = matrices + gather_ring([half for matrix in matrices for half in halves(matrix)], rings)
    entering = lax.dynamic_slice_in_dim(tokens_in, upper * own_micros, own_micros, 0)
    entering = entering.reshape(row_count, width)

    def exchange(value):
        return lax.ppermute(value, "expert", other_core)

    def ring_step(step, state):
        sent, stored_first, stored_second = state
        place = jnp.stack([(ring_id == step).astype(jnp.int32), my_z, my_core])
        mine = lax.ppermute(sent, "section", next_ring)
        mine, weights = lax.optimization_barrier((mine, load_first(place, sources)))
        other = exchange(mine)
        part, lent = run_first(place, mine, other, scales[0], ids[0], routers[0], weights)
        back = exchange(lent)
        stored_first, own, lent = run_second(
            place, mine, other, part, back, scales[1], ids[1], routers[1], stored_first, sources
        )
        back = exchange(lent)
        stored_second, sent = run_add(place, stored_first, own, back, stored_second)
        return sent, stored_first, stored_second

    blank = jnp.zeros(entering.shape, jnp.float32)
    _, stored_first, stored_second = lax.fori_loop(0, rings, ring_step, (entering, blank, blank))
    kept = jnp.where(upper == 0, stored_first, stored_second)
    given = jnp.where(upper == 0, stored_second, stored_first)
    taken = lax.ppermute(given.astype(jnp.bfloat16), "section", other_half).astype(jnp.float32)
    low = jnp.where(upper == 0, kept, taken)
    high = jnp.where(upper == 0, taken, kept)
    return jnp.concatenate([low, high], axis=0).reshape(1, micro_count, tok_rows, width)


def solution(mesh):
    return jax.shard_map(
        shards,
        mesh=mesh,
        in_specs=(
            P(None, "expert", None),
            P("section", None, None, None),
            P("section", None, None),
            P("section", None),
            P("section", "expert", None, None),
            P("section", "expert", None, None),
            P("section", "expert", None, None),
        ),
        out_specs=P("section", None, "expert", None),
        check_vma=False,
    )
```

time: 1450 us -> 1030 us (0.71)
  waiting for transfers between devices: 971 us -> 641 us
  other arithmetic: 64.9 us -> 5.75 us
  Pallas kernels: 144 us -> 106 us
  local copies, waits for them, and re-layouts: 78.2 us -> 97.7 us
  starting transfers between devices: 175 us -> 157 us
    ppermute x17, waiting for transfers between devices: 453 us -> 115 us  [the longest x16 105 us: ring_step(): mine = lax.ppermute(sent, 'section', next_ring)]
    ppermute x42, starting transfers between devices: 108 us -> 25.9 us  [gather_ring(): lax.ppermute(travelling[m], both, forward if m % 2 == 0 else backward)]
    ppermute x17, starting transfers between devices: 25.5 us -> 89.2 us  [the longest x16 87.3 us: ring_step(): mine = lax.ppermute(sent, 'section', next_ring)]
    select_n x33 -> x0, other arithmetic: 59.9 us -> none  [the longest x16 29.7 us: ring_step(): stored_second = jnp.where(active, leaving, stored_second)]
    ppermute x3, waiting for transfers between devices: 0.01 us -> 38.4 us  [both_layers(): theirs = lax.ppermute(value, 'section', other_half)]
    pallas_call x80 -> x64, Pallas kernels: 144 us -> 106 us  [the longest x16 32.9 us: run_add(): pl.pallas_call(add_kernel, out_shape=(like(middle.shape, jnp.float32), li...]
    ppermute x64 -> x48, waiting for transfers between devices: 94 us -> 61.8 us  [exchange(): return lax.ppermute(value, 'expert', other_core)]
    while x192 -> x770, local copies, waits for them, and re-layouts: 69.5 us -> 88.9 us
  transfers between devices with their start and end apart: 126 -> 110, of which waited for: 103 -> 107; matrix products, arithmetic and copies ran while one was open for 5% -> 1% of each run, Pallas kernels for 0% -> 2%
where the time goes in v2:
time: 1030 us; the launch traced here: 1010 us
  waiting for transfers between devices  641 us (62%)
  starting transfers between devices  157 us (15%)
  Pallas kernels  106 us (10%)
  local copies, waits for them, and re-layouts  97.7 us (9%)
    ppermute x42, waiting for transfers between devices, gather_ring(): lax.ppermute(travelling[m], both, forward if m % 2 == 0 else backward)  426 us
    ppermute x16, waiting for transfers between devices, ring_step(): mine = lax.ppermute(sent, 'section', next_ring)  105 us
    while x768, local copies, waits for them, and re-layouts  88.7 us
    ppermute x16, starting transfers between devices, ring_step(): mine = lax.ppermute(sent, 'section', next_ring)  87.3 us
    ppermute x48, waiting for transfers between devices, exchange(): return lax.ppermute(value, 'expert', other_core)  61.8 us
    ppermute x3, waiting for transfers between devices, both_layers(): theirs = lax.ppermute(value, 'section', other_half)  38.4 us
    ppermute x48, starting transfers between devices, exchange(): return lax.ppermute(value, 'expert', other_core)  33.1 us
    pallas_call x16, Pallas kernels, run_add(): pl.pallas_call(add_kernel, out_shape=(like(middle.shape, jnp.float32), li...  32.9 us
  transfers between devices with their start and end apart: 110, of which 107 were waited for; matrix products, arithmetic and copies ran while one was open for 1% of the time, Pallas kernels for 2%

profile of v2, /device:TPU:31, one launch (start us, length us, event | category | flops | bytes accessed | tf_op | source)
XLA Modules:
  0.0 1010.9 jit_solution(4943215655443486204)
XLA Ops:
  3.2 5.6 collective-permute-start.5
  17.6 17.0 %collective-permute-done.47 = s32[8,128,2]{1,2,0:T(2,128)S(1)} collective-permute-done((s32[8,128,2]{1,2,0:T(2,128)S(1)}, s32[8,128,2]{1,2,0:T(2,128)S(1)}, u32[]{:S(2)}, u32[]{:S(2)}) %collective-permute-start.47) | collective-permute-done | bytes 8224 | tf_op jit(solution)/shard_map/ppermute | solution.py:270
  36.1 21.1 %collective-permute-done.48 = bf16[2048,8]{1,0:T(8,128)(2,1)S(1)} collective-permute-done((bf16[2048,8]{1,0:T(8,128)(2,1)S(1)}, bf16[2048,8]{1,0:T(8,128)(2,1)S(1)}, u32[]{:S(2)}, u32[]{:S(2)}) %collective-permute-start.48) | collective-permute-done | bytes 32800 | tf_op jit(solution)/shard_map/ppermute | solution.py:270
  60.0 16.5 %collective-permute-done.13 = bf16[1024,512]{1,0:T(8,128)(2,1)S(1)} collective-permute-done((bf16[1024,512]{1,0:T(8,128)(2,1)S(1)}, bf16[1024,512]{1,0:T(8,128)(2,1)S(1)}, u32[]{:S(2)}, u32[]{:S(2)}) %collective-permute-start.13) | collective-permute-done | bytes 1048608 | tf_op jit(solution)/shard_map/ppermute | solution.py:246
  80.8 18.1 %collective-permute-done.21 = bf16[256,2048]{1,0:T(8,128)(2,1)S(1)} collective-permute-done((bf16[256,2048]{1,0:T(8,128)(2,1)S(1)}, bf16[256,2048]{1,0:T(8,128)(2,1)S(1)}, u32[]{:S(2)}, u32[]{:S(2)}) %collective-permute-start.21) | collective-permute-done | bytes 1048608 | tf_op jit(solution)/shard_map/ppermute | solution.py:246
  102.8 18.7 %collective-permute-done.6 = bf16[1024,512]{1,0:T(8,128)(2,1)S(1)} collective-permute-done((bf16[1024,512]{1,0:T(8,128)(2,1)}, bf16[1024,512]{1,0:T(8,128)(2,1)S(1)}, u32[]{:S(2)}, u32[]{:S(2)}) %collective-permute-start.6) | collective-permute-done | bytes 1048608 | tf_op jit(solution)/shard_map/ppermute | solution.py:246
  125.5 18.4 %collective-permute-done.14 = bf16[1024,512]{1,0:T(8,128)(2,1)S(1)} collective-permute-done((bf16[1024,512]{1,0:T(8,128)(2,1)S(1)}, bf16[1024,512]{1,0:T(8,128)(2,1)S(1)}, u32[]{:S(2)}, u32[]{:S(2)}) %collective-permute-start.14) | collective-permute-done | bytes 1048608 | tf_op jit(solution)/shard_map/ppermute | solution.py:246
  147.8 18.5 %collective-permute-done.22 = bf16[256,2048]{1,0:T(8,128)(2,1)S(1)} collective-permute-done((bf16[256,2048]{1,0:T(8,128)(2,1)S(1)}, bf16[256,2048]{1,0:T(8,128)(2,1)S(1)}, u32[]{:S(2)}, u32[]{:S(2)}) %collective-permute-start.22) | collective-permute-done | bytes 1048608 | tf_op jit(solution)/shard_map/ppermute | solution.py:246
  170.3 18.5 %collective-permute-done.7 = bf16[1024,512]{1,0:T(8,128)(2,1)S(1)} collective-permute-done((bf16[1024,512]{1,0:T(8,128)(2,1)S(1)}, bf16[1024,512]{1,0:T(8,128)(2,1)S(1)}, u32[]{:S(2)}, u32[]{:S(2)}) %collective-permute-start.7) | collective-permute-done | bytes 1048608 | tf_op jit(solution)/shard_map/ppermute | solution.py:246
  192.7 18.5 %collective-permute-done.15 = bf16[1024,512]{1,0:T(8,128)(2,1)S(1)} collective-permute-done((bf16[1024,512]{1,0:T(8,128)(2,1)S(1)}, bf16[1024,512]{1,0:T(8,128)(2,1)S(1)}, u32[]{:S(2)}, u32[]{:S(2)}) %collective-permute-start.15) | collective-permute-done | bytes 1048608 | tf_op jit(solution)/shard_map/ppermute | solution.py:246
  215.2 18.5 %collective-permute-done.23 = bf16[256,2048]{1,0:T(8,128)(2,1)S(1)} collective-permute-done((bf16[256,2048]{1,0:T(8,128)(2,1)S(1)}, bf16[256,2048]{1,0:T(8,128)(2,1)S(1)}, u32[]{:S(2)}, u32[]{:S(2)}) %collective-permute-start.23) | collective-permute-done | bytes 1048608 | tf_op jit(solution)/shard_map/ppermute | solution.py:246
  237.7 18.5 %collective-permute-done.8 = bf16[1024,512]{1,0:T(8,128)(2,1)S(1)} collective-permute-done((bf16[1024,512]{1,0:T(8,128)(2,1)S(1)}, bf16[1024,512]{1,0:T(8,128)(2,1)S(1)}, u32[]{:S(2)}, u32[]{:S(2)}) %collective-permute-start.8) | collective-permute-done | bytes 1048608 | tf_op jit(solution)/shard_map/ppermute | solution.py:246
  260.1 18.5 %collective-permute-done.16 = bf16[1024,512]{1,0:T(8,128)(2,1)S(1)} collective-permute-done((bf16[1024,512]{1,0:T(8,128)(2,1)S(1)}, bf16[1024,512]{1,0:T(8,128)(2,1)S(1)}, u32[]{:S(2)}, u32[]{:S(2)}) %collective-permute-start.16) | collective-permute-done | bytes 1048608 | tf_op jit(solution)/shard_map/ppermute | solution.py:246
  282.6 18.5 %collective-permute-done.24 = bf16[256,2048]{1,0:T(8,128)(2,1)S(1)} collective-permute-done((bf16[256,2048]{1,0:T(8,128)(2,1)S(1)}, bf16[256,2048]{1,0:T(8,128)(2,1)S(1)}, u32[]{:S(2)}, u32[]{:S(2)}) %collective-permute-start.24) | collective-permute-done | bytes 1048608 | tf_op jit(solution)/shard_map/ppermute | solution.py:246
  305.3 18.3 %collective-permute-done.9 = bf16[1024,512]{1,0:T(8,128)(2,1)S(1)} collective-permute-done((bf16[1024,512]{1,0:T(8,128)(2,1)S(1)}, bf16[1024,512]{1,0:T(8,128)(2,1)S(1)}, u32[]{:S(2)}, u32[]{:S(2)}) %collective-permute-start.9) | collective-permute-done | bytes 1048608 | tf_op jit(solution)/shard_map/ppermute | solution.py:246
  327.5 18.5 %collective-permute-done.17 = bf16[1024,512]{1,0:T(8,128)(2,1)S(1)} collective-permute-done((bf16[1024,512]{1,0:T(8,128)(2,1)S(1)}, bf16[1024,512]{1,0:T(8,128)(2,1)S(1)}, u32[]{:S(2)}, u32[]{:S(2)}) %collective-permute-start.17) | collective-permute-done | bytes 1048608 | tf_op jit(solution)/shard_map/ppermute | solution.py:246
  350.0 18.5 %collective-permute-done.25 = bf16[256,2048]{1,0:T(8,128)(2,1)} collective-permute-done((bf16[256,2048]{1,0:T(8,128)(2,1)S(1)}, bf16[256,2048]{1,0:T(8,128)(2,1)}, u32[]{:S(2)}, u32[]{:S(2)}) %collective-permute-start.25) | collective-permute-done | bytes 1048608 | tf_op jit(solution)/shard_map/ppermute | solution.py:246
  372.6 18.4 %collective-permute-done.10 = bf16[1024,512]{1,0:T(8,128)(2,1)} collective-permute-done((bf16[1024,512]{1,0:T(8,128)(2,1)S(1)}, bf16[1024,512]{1,0:T(8,128)(2,1)}, u32[]{:S(2)}, u32[]{:S(2)}) %collective-permute-start.10) | collective-permute-done | bytes 1048608 | tf_op jit(solution)/shard_map/ppermute | solution.py:246
  396.5 17.0 %collective-permute-done.18 = bf16[1024,512]{1,0:T(8,128)(2,1)} collective-permute-done((bf16[1024,512]{1,0:T(8,128)(2,1)S(1)}, bf16[1024,512]{1,0:T(8,128)(2,1)}, u32[]{:S(2)}, u32[]{:S(2)}) %collective-permute-start.18) | collective-permute-done | bytes 1048608 | tf_op jit(solution)/shard_map/ppermute | solution.py:246
  417.5 18.6 %collective-permute-done.26 = bf16[256,2048]{1,0:T(8,128)(2,1)} collective-permute-done((bf16[256,2048]{1,0:T(8,128)(2,1)}, bf16[256,2048]{1,0:T(8,128)(2,1)}, u32[]{:S(2)}, u32[]{:S(2)}) %collective-permute-start.26) | collective-permute-done | bytes 1048608 | tf_op jit(solution)/shard_map/ppermute | solution.py:246
  440.0 18.6 %collective-permute-done.11 = bf16[1024,512]{1,0:T(8,128)(2,1)} collective-permute-done((bf16[1024,512]{1,0:T(8,128)(2,1)}, bf16[1024,512]{1,0:T(8,128)(2,1)}, u32[]{:S(2)}, u32[]{:S(2)}) %collective-permute-start.11) | collective-permute-done | bytes 1048608 | tf_op jit(solution)/shard_map/ppermute | solution.py:246
  462.9 18.1 %collective-permute-done.19 = bf16[1024,512]{1,0:T(8,128)(2,1)} collective-permute-done((bf16[1024,512]{1,0:T(8,128)(2,1)}, bf16[1024,512]{1,0:T(8,128)(2,1)}, u32[]{:S(2)}, u32[]{:S(2)}) %collective-permute-start.19) | collective-permute-done | bytes 1048608 | tf_op jit(solution)/shard_map/ppermute | solution.py:246
  484.9 18.6 %collective-permute-done.27 = bf16[256,2048]{1,0:T(8,128)(2,1)} collective-permute-done((bf16[256,2048]{1,0:T(8,128)(2,1)}, bf16[256,2048]{1,0:T(8,128)(2,1)}, u32[]{:S(2)}, u32[]{:S(2)}) %collective-permute-start.27) | collective-permute-done | bytes 1048608 | tf_op jit(solution)/shard_map/ppermute | solution.py:246
  509.1 486.0 %while.17 = (s32[]{:T(128)}, bf16[64,2048]{1,0:T(8,128)(2,1)S(1)}, f32[64,2048]{1,0:T(8,128)}, f32[64,2048]{1,0:T(8,128)}, s32[]{:T(128)}, /*index=5*/s32[]{:T(1...) while((s32[]{:T(128)}, bf16[64,2048]{1,0:T(8,128)(2,1)S(1)}, ...), condition=%wide.region_1.2_spmd, body=%wide.region_0.1_spmd.sunk | while | flops 10 | bytes 135267728 | solution.py:310
  510.0 5.9 collective-permute-done.mine_ref
  533.2 10.0 collective-permute-start
  565.1 5.5 collective-permute-start
  571.5 4.4 collective-permute-done.mine_ref
  592.5 5.5 collective-permute-start
  619.9 5.5 collective-permute-start
  626.3 4.4 collective-permute-done.mine_ref
  647.3 5.5 collective-permute-start
  674.7 5.5 collective-permute-start
  681.1 4.4 collective-permute-done.mine_ref
  702.1 5.5 collective-permute-start
  729.5 5.5 collective-permute-start
  756.9 5.5 collective-permute-start
  784.3 5.5 collective-permute-start
  811.7 5.5 collective-permute-start
  839.1 5.5 collective-permute-start
  866.5 5.5 collective-permute-start
  894.0 5.5 collective-permute-start
  921.4 5.5 collective-permute-start
  927.0 8.6 eval_jaxpr.20
  935.5 36.6 %collective-permute-done.mine_ref = bf16[64,2048]{1,0:T(8,128)(2,1)S(1)} collective-permute-done((bf16[64,2048]{1,0:T(8,128)(2,1)S(1)}, bf16[64,2048]{1,0:T(8,128)(2,1)S(1)}, u32[]{:S(2)}, u32[]{:S(2)}) %collective-permute-start) | collective-permute-done | bytes 262176 | tf_op jit(solution)/shard_map/while/body/eval_jaxpr/ppermute | solution.py:297
  974.3 6.3 eval_jaxpr.21
  982.9 7.7 eval_jaxpr.22
  998.1 10.2 %collective-permute-done.49 = bf16[64,2048]{1,0:T(8,128)(2,1)S(1)} collective-permute-done((bf16[64,2048]{1,0:T(8,128)(2,1)S(1)}, bf16[64,2048]{1,0:T(8,128)(2,1)S(1)}, u32[]{:S(2)}, u32[]{:S(2)}) %collective-permute-start.49) | collective-permute-done | bytes 262176 | tf_op jit(solution)/shard_map/ppermute | solution.py:313
  (1121 shorter events, 421.0 us)
Async XLA Ops:
  3.2 54.0 %collective-permute-start.5 = (bf16[1024,512]{1,0:T(8,128)(2,1)}, bf16[1024,512]{1,0:T(8,128)(2,1)}, u32[]{:S(2)}, u32[]{:S(2)}) collective-permute-start(bf16[1024,512]{1,0:T(8,128)(2,1)} %get-tuple-element.987), channel_id=1, source_target_pairs={{0,14},{1,15},{2,0},{3,1},{4,2},{5,3},{6,4},{7,5},{8,6},{9,7},{10,... | collective-permute-start | bytes 3145736 | tf_op jit(solution)/shard_map/ppermute | solution.py:246
  8.8 49.9 %collective-permute-start.4 = (bf16[1024,512]{1,0:T(8,128)(2,1)}, bf16[1024,512]{1,0:T(8,128)(2,1)}, u32[]{:S(2)}, u32[]{:S(2)}) collective-permute-start(bf16[1024,512]{1,0:T(8,128)(2,1)} %get-tuple-element.988), channel_id=1, source_target_pairs={{0,2},{1,3},{2,4},{3,5},{4,6},{5,7},{6,8},{7,9},{8,10},{9,11},{10,... | collective-permute-start | bytes 3145736 | tf_op jit(solution)/shard_map/ppermute | solution.py:246
  8.8 25.9 %collective-permute-start.47 = (s32[8,128,2]{1,2,0:T(2,128)S(1)}, s32[8,128,2]{1,2,0:T(2,128)S(1)}, u32[]{:S(2)}, u32[]{:S(2)}) collective-permute-start(s32[8,128,2]{1,2,0:T(2,128)S(1)} %bitcast.45), channel_id=1, source_target_pairs={{0,8},{8,0},{16,24},{24,16},{32,40},{40,32},{48,56},{56,48},{64,72... | collective-permute-start | bytes 24584 | tf_op jit(solution)/shard_map/ppermute | solution.py:270
  11.6 23.4 %collective-permute-start.46 = (f32[1,2048]{1,0:T(1,128)S(1)}, f32[1,2048]{1,0:T(1,128)S(1)}, u32[]{:S(2)}, u32[]{:S(2)}) collective-permute-start(f32[1,2048]{1,0:T(1,128)S(1)} %copy-done.59), channel_id=1, source_target_pairs={{0,8},{8,0},{16,24},{24,16},{32,40},{40,32},{48,56},{56,48},{64,72... | collective-permute-start | bytes 24584 | tf_op jit(solution)/shard_map/ppermute | solution.py:270
  14.6 42.6 %collective-permute-start.48 = (bf16[2048,8]{1,0:T(8,128)(2,1)S(1)}, bf16[2048,8]{1,0:T(8,128)(2,1)S(1)}, u32[]{:S(2)}, u32[]{:S(2)}) collective-permute-start(bf16[2048,8]{1,0:T(8,128)(2,1)S(1)} %bitcast.43), channel_id=1, source_target_pairs={{0,8},{8,0},{16,24},{24,16},{32,40},{40,32},{48,56},{56,48},{64,72... | collective-permute-start | bytes 98312 | tf_op jit(solution)/shard_map/ppermute | solution.py:270
  34.6 41.8 %collective-permute-start.13 = (bf16[1024,512]{1,0:T(8,128)(2,1)S(1)}, bf16[1024,512]{1,0:T(8,128)(2,1)S(1)}, u32[]{:S(2)}, u32[]{:S(2)}) collective-permute-start(bf16[1024,512]{1,0:T(8,128)(2,1)S(1)} %get-tuple-element.985), channel_id=1, source_target_pairs={{0,14},{1,15},{2,0},{3,1},{4,2},{5,3},{6,4},{7,5},{8,6},{9,7},{10,... | collective-permute-start | bytes 3145736 | tf_op jit(solution)/shard_map/ppermute | solution.py:246
  35.0 45.4 %collective-permute-start.12 = (bf16[1024,512]{1,0:T(8,128)(2,1)S(1)}, bf16[1024,512]{1,0:T(8,128)(2,1)S(1)}, u32[]{:S(2)}, u32[]{:S(2)}) collective-permute-start(bf16[1024,512]{1,0:T(8,128)(2,1)S(1)} %get-tuple-element.986), channel_id=1, source_target_pairs={{0,2},{1,3},{2,4},{3,5},{4,6},{5,7},{6,8},{7,9},{8,10},{9,11},{10,... | collective-permute-start | bytes 3145736 | tf_op jit(solution)/shard_map/ppermute | solution.py:246
  57.2 41.7 %collective-permute-start.21 = (bf16[256,2048]{1,0:T(8,128)(2,1)S(1)}, bf16[256,2048]{1,0:T(8,128)(2,1)S(1)}, u32[]{:S(2)}, u32[]{:S(2)}) collective-permute-start(bf16[256,2048]{1,0:T(8,128)(2,1)S(1)} %get-tuple-element.983), channel_id=1, source_target_pairs={{0,14},{1,15},{2,0},{3,1},{4,2},{5,3},{6,4},{7,5},{8,6},{9,7},{10,... | collective-permute-start | bytes 3145736 | tf_op jit(solution)/shard_map/ppermute | solution.py:246
  57.2 45.6 %collective-permute-start.20 = (bf16[256,2048]{1,0:T(8,128)(2,1)S(1)}, bf16[256,2048]{1,0:T(8,128)(2,1)S(1)}, u32[]{:S(2)}, u32[]{:S(2)}) collective-permute-start(bf16[256,2048]{1,0:T(8,128)(2,1)S(1)} %get-tuple-element.984), channel_id=1, source_target_pairs={{0,2},{1,3},{2,4},{3,5},{4,6},{5,7},{6,8},{7,9},{8,10},{9,11},{10,... | collective-permute-start | bytes 3145736 | tf_op jit(solution)/shard_map/ppermute | solution.py:246
  58.7 62.8 %collective-permute-start.6 = (bf16[1024,512]{1,0:T(8,128)(2,1)}, bf16[1024,512]{1,0:T(8,128)(2,1)S(1)}, u32[]{:S(2)}, u32[]{:S(2)}) collective-permute-start(bf16[1024,512]{1,0:T(8,128)(2,1)} %collective-permute-done.5), channel_id=1, source_target_pairs={{0,14},{1,15},{2,0},{3,1},{4,2},{5,3},{6,4},{7,5},{8,6},{9,7},{10,... | collective-permute-start | bytes 3145736 | tf_op jit(solution)/shard_map/ppermute | solution.py:246
  76.4 48.8 %collective-permute-start.28 = (bf16[1024,512]{1,0:T(8,128)(2,1)}, bf16[1024,512]{1,0:T(8,128)(2,1)S(1)}, u32[]{:S(2)}, u32[]{:S(2)}) collective-permute-start(bf16[1024,512]{1,0:T(8,128)(2,1)} %collective-permute-done.4), channel_id=1, source_target_pairs={{0,2},{1,3},{2,4},{3,5},{4,6},{5,7},{6,8},{7,9},{8,10},{9,11},{10,... | collective-permute-start | bytes 3145736 | tf_op jit(solution)/shard_map/ppermute | solution.py:246
  80.4 63.5 %collective-permute-start.14 = (bf16[1024,512]{1,0:T(8,128)(2,1)S(1)}, bf16[1024,512]{1,0:T(8,128)(2,1)S(1)}, u32[]{:S(2)}, u32[]{:S(2)}) collective-permute-start(bf16[1024,512]{1,0:T(8,128)(2,1)S(1)} %collective-permute-done.13), channel_id=1, source_target_pairs={{0,14},{1,15},{2,0},{3,1},{4,2},{5,3},{6,4},{7,5},{8,6},{9,7},{10,... | collective-permute-start | bytes 3145736 | tf_op jit(solution)/shard_map/ppermute | solution.py:246
  98.9 48.8 %collective-permute-start.29 = (bf16[1024,512]{1,0:T(8,128)(2,1)S(1)}, bf16[1024,512]{1,0:T(8,128)(2,1)S(1)}, u32[]{:S(2)}, u32[]{:S(2)}) collective-permute-start(bf16[1024,512]{1,0:T(8,128)(2,1)S(1)} %collective-permute-done.12), channel_id=1, source_target_pairs={{0,2},{1,3},{2,4},{3,5},{4,6},{5,7},{6,8},{7,9},{8,10},{9,11},{10,... | collective-permute-start | bytes 3145736 | tf_op jit(solution)/shard_map/ppermute | solution.py:246
  102.8 63.5 %collective-permute-start.22 = (bf16[256,2048]{1,0:T(8,128)(2,1)S(1)}, bf16[256,2048]{1,0:T(8,128)(2,1)S(1)}, u32[]{:S(2)}, u32[]{:S(2)}) collective-permute-start(bf16[256,2048]{1,0:T(8,128)(2,1)S(1)} %collective-permute-done.21), channel_id=1, source_target_pairs={{0,14},{1,15},{2,0},{3,1},{4,2},{5,3},{6,4},{7,5},{8,6},{9,7},{10,... | collective-permute-start | bytes 3145736 | tf_op jit(solution)/shard_map/ppermute | solution.py:246
  121.5 48.7 %collective-permute-start.30 = (bf16[256,2048]{1,0:T(8,128)(2,1)S(1)}, bf16[256,2048]{1,0:T(8,128)(2,1)S(1)}, u32[]{:S(2)}, u32[]{:S(2)}) collective-permute-start(bf16[256,2048]{1,0:T(8,128)(2,1)S(1)} %collective-permute-done.20), channel_id=1, source_target_pairs={{0,2},{1,3},{2,4},{3,5},{4,6},{5,7},{6,8},{7,9},{8,10},{9,11},{10,... | collective-permute-start | bytes 3145736 | tf_op jit(solution)/shard_map/ppermute | solution.py:246
  125.3 63.5 %collective-permute-start.7 = (bf16[1024,512]{1,0:T(8,128)(2,1)S(1)}, bf16[1024,512]{1,0:T(8,128)(2,1)S(1)}, u32[]{:S(2)}, u32[]{:S(2)}) collective-permute-start(bf16[1024,512]{1,0:T(8,128)(2,1)S(1)} %collective-permute-done.6), channel_id=1, source_target_pairs={{0,14},{1,15},{2,0},{3,1},{4,2},{5,3},{6,4},{7,5},{8,6},{9,7},{10,... | collective-permute-start | bytes 3145736 | tf_op jit(solution)/shard_map/ppermute | solution.py:246
  143.9 48.8 %collective-permute-start.31 = (bf16[1024,512]{1,0:T(8,128)(2,1)S(1)}, bf16[1024,512]{1,0:T(8,128)(2,1)S(1)}, u32[]{:S(2)}, u32[]{:S(2)}) collective-permute-start(bf16[1024,512]{1,0:T(8,128)(2,1)S(1)} %collective-permute-done.28), channel_id=1, source_target_pairs={{0,2},{1,3},{2,4},{3,5},{4,6},{5,7},{6,8},{7,9},{8,10},{9,11},{10,... | collective-permute-start | bytes 3145736 | tf_op jit(solution)/shard_map/ppermute | solution.py:246
  147.8 63.5 %collective-permute-start.15 = (bf16[1024,512]{1,0:T(8,128)(2,1)S(1)}, bf16[1024,512]{1,0:T(8,128)(2,1)S(1)}, u32[]{:S(2)}, u32[]{:S(2)}) collective-permute-start(bf16[1024,512]{1,0:T(8,128)(2,1)S(1)} %collective-permute-done.14), channel_id=1, source_target_pairs={{0,14},{1,15},{2,0},{3,1},{4,2},{5,3},{6,4},{7,5},{8,6},{9,7},{10,... | collective-permute-start | bytes 3145736 | tf_op jit(solution)/shard_map/ppermute | solution.py:246
  166.3 48.8 %collective-permute-start.32 = (bf16[1024,512]{1,0:T(8,128)(2,1)S(1)}, bf16[1024,512]{1,0:T(8,128)(2,1)S(1)}, u32[]{:S(2)}, u32[]{:S(2)}) collective-permute-start(bf16[1024,512]{1,0:T(8,128)(2,1)S(1)} %collective-permute-done.29), channel_id=1, source_target_pairs={{0,2},{1,3},{2,4},{3,5},{4,6},{5,7},{6,8},{7,9},{8,10},{9,11},{10,... | collective-permute-start | bytes 3145736 | tf_op jit(solution)/shard_map/ppermute | solution.py:246
  170.2 63.5 %collective-permute-start.23 = (bf16[256,2048]{1,0:T(8,128)(2,1)S(1)}, bf16[256,2048]{1,0:T(8,128)(2,1)S(1)}, u32[]{:S(2)}, u32[]{:S(2)}) collective-permute-start(bf16[256,2048]{1,0:T(8,128)(2,1)S(1)} %collective-permute-done.22), channel_id=1, source_target_pairs={{0,14},{1,15},{2,0},{3,1},{4,2},{5,3},{6,4},{7,5},{8,6},{9,7},{10,... | collective-permute-start | bytes 3145736 | tf_op jit(solution)/shard_map/ppermute | solution.py:246
  188.8 48.8 %collective-permute-start.33 = (bf16[256,2048]{1,0:T(8,128)(2,1)S(1)}, bf16[256,2048]{1,0:T(8,128)(2,1)S(1)}, u32[]{:S(2)}, u32[]{:S(2)}) collective-permute-start(bf16[256,2048]{1,0:T(8,128)(2,1)S(1)} %collective-permute-done.30), channel_id=1, source_target_pairs={{0,2},{1,3},{2,4},{3,5},{4,6},{5,7},{6,8},{7,9},{8,10},{9,11},{10,... | collective-permute-start | bytes 3145736 | tf_op jit(solution)/shard_map/ppermute | solution.py:246
  192.7 63.5 %collective-permute-start.8 = (bf16[1024,512]{1,0:T(8,128)(2,1)S(1)}, bf16[1024,512]{1,0:T(8,128)(2,1)S(1)}, u32[]{:S(2)}, u32[]{:S(2)}) collective-permute-start(bf16[1024,512]{1,0:T(8,128)(2,1)S(1)} %collective-permute-done.7), channel_id=1, source_target_pairs={{0,14},{1,15},{2,0},{3,1},{4,2},{5,3},{6,4},{7,5},{8,6},{9,7},{10,... | collective-permute-start | bytes 3145736 | tf_op jit(solution)/shard_map/ppermute | solution.py:246
  211.3 48.8 %collective-permute-start.34 = (bf16[1024,512]{1,0:T(8,128)(2,1)S(1)}, bf16[1024,512]{1,0:T(8,128)(2,1)S(1)}, u32[]{:S(2)}, u32[]{:S(2)}) collective-permute-start(bf16[1024,512]{1,0:T(8,128)(2,1)S(1)} %collective-permute-done.31), channel_id=1, source_target_pairs={{0,2},{1,3},{2,4},{3,5},{4,6},{5,7},{6,8},{7,9},{8,10},{9,11},{10,... | collective-permute-start | bytes 3145736 | tf_op jit(solution)/shard_map/ppermute | solution.py:246
  215.2 63.5 %collective-permute-start.16 = (bf16[1024,512]{1,0:T(8,128)(2,1)S(1)}, bf16[1024,512]{1,0:T(8,128)(2,1)S(1)}, u32[]{:S(2)}, u32[]{:S(2)}) collective-permute-start(bf16[1024,512]{1,0:T(8,128)(2,1)S(1)} %collective-permute-done.15), channel_id=1, source_target_pairs={{0,14},{1,15},{2,0},{3,1},{4,2},{5,3},{6,4},{7,5},{8,6},{9,7},{10,... | collective-permute-start | bytes 3145736 | tf_op jit(solution)/shard_map/ppermute | solution.py:246
  233.7 48.8 %collective-permute-start.35 = (bf16[1024,512]{1,0:T(8,128)(2,1)S(1)}, bf16[1024,512]{1,0:T(8,128)(2,1)S(1)}, u32[]{:S(2)}, u32[]{:S(2)}) collective-permute-start(bf16[1024,512]{1,0:T(8,128)(2,1)S(1)} %collective-permute-done.32), channel_id=1, source_target_pairs={{0,2},{1,3},{2,4},{3,5},{4,6},{5,7},{6,8},{7,9},{8,10},{9,11},{10,... | collective-permute-start | bytes 3145736 | tf_op jit(solution)/shard_map/ppermute | solution.py:246
  237.7 63.5 %collective-permute-start.24 = (bf16[256,2048]{1,0:T(8,128)(2,1)S(1)}, bf16[256,2048]{1,0:T(8,128)(2,1)S(1)}, u32[]{:S(2)}, u32[]{:S(2)}) collective-permute-start(bf16[256,2048]{1,0:T(8,128)(2,1)S(1)} %collective-permute-done.23), channel_id=1, source_target_pairs={{0,14},{1,15},{2,0},{3,1},{4,2},{5,3},{6,4},{7,5},{8,6},{9,7},{10,... | collective-permute-start | bytes 3145736 | tf_op jit(solution)/shard_map/ppermute | solution.py:246
  256.2 48.8 %collective-permute-start.36 = (bf16[256,2048]{1,0:T(8,128)(2,1)S(1)}, bf16[256,2048]{1,0:T(8,128)(2,1)S(1)}, u32[]{:S(2)}, u32[]{:S(2)}) collective-permute-start(bf16[256,2048]{1,0:T(8,128)(2,1)S(1)} %collective-permute-done.33), channel_id=1, source_target_pairs={{0,2},{1,3},{2,4},{3,5},{4,6},{5,7},{6,8},{7,9},{8,10},{9,11},{10,... | collective-permute-start | bytes 3145736 | tf_op jit(solution)/shard_map/ppermute | solution.py:246
  260.1 63.5 %collective-permute-start.9 = (bf16[1024,512]{1,0:T(8,128)(2,1)S(1)}, bf16[1024,512]{1,0:T(8,128)(2,1)S(1)}, u32[]{:S(2)}, u32[]{:S(2)}) collective-permute-start(bf16[1024,512]{1,0:T(8,128)(2,1)S(1)} %collective-permute-done.8), channel_id=1, source_target_pairs={{0,14},{1,15},{2,0},{3,1},{4,2},{5,3},{6,4},{7,5},{8,6},{9,7},{10,... | collective-permute-start | bytes 3145736 | tf_op jit(solution)/shard_map/ppermute | solution.py:246
  278.7 48.8 %collective-permute-start.37 = (bf16[1024,512]{1,0:T(8,128)(2,1)S(1)}, bf16[1024,512]{1,0:T(8,128)(2,1)S(1)}, u32[]{:S(2)}, u32[]{:S(2)}) collective-permute-start(bf16[1024,512]{1,0:T(8,128)(2,1)S(1)} %collective-permute-done.34), channel_id=1, source_target_pairs={{0,2},{1,3},{2,4},{3,5},{4,6},{5,7},{6,8},{7,9},{8,10},{9,11},{10,... | collective-permute-start | bytes 3145736 | tf_op jit(solution)/shard_map/ppermute | solution.py:246
  282.6 63.5 %collective-permute-start.17 = (bf16[1024,512]{1,0:T(8,128)(2,1)S(1)}, bf16[1024,512]{1,0:T(8,128)(2,1)S(1)}, u32[]{:S(2)}, u32[]{:S(2)}) collective-permute-start(bf16[1024,512]{1,0:T(8,128)(2,1)S(1)} %collective-permute-done.16), channel_id=1, source_target_pairs={{0,14},{1,15},{2,0},{3,1},{4,2},{5,3},{6,4},{7,5},{8,6},{9,7},{10,... | collective-permute-start | bytes 3145736 | tf_op jit(solution)/shard_map/ppermute | solution.py:246
  301.2 48.8 %collective-permute-start.38 = (bf16[1024,512]{1,0:T(8,128)(2,1)S(1)}, bf16[1024,512]{1,0:T(8,128)(2,1)S(1)}, u32[]{:S(2)}, u32[]{:S(2)}) collective-permute-start(bf16[1024,512]{1,0:T(8,128)(2,1)S(1)} %collective-permute-done.35), channel_id=1, source_target_pairs={{0,2},{1,3},{2,4},{3,5},{4,6},{5,7},{6,8},{7,9},{8,10},{9,11},{10,... | collective-permute-start | bytes 3145736 | tf_op jit(solution)/shard_map/ppermute | solution.py:246
  305.1 63.5 %collective-permute-start.25 = (bf16[256,2048]{1,0:T(8,128)(2,1)S(1)}, bf16[256,2048]{1,0:T(8,128)(2,1)}, u32[]{:S(2)}, u32[]{:S(2)}) collective-permute-start(bf16[256,2048]{1,0:T(8,128)(2,1)S(1)} %collective-permute-done.24), channel_id=1, source_target_pairs={{0,14},{1,15},{2,0},{3,1},{4,2},{5,3},{6,4},{7,5},{8,6},{9,7},{10,... | collective-permute-start | bytes 3145736 | tf_op jit(solution)/shard_map/ppermute | solution.py:246
  323.6 49.0 %collective-permute-start.39 = (bf16[256,2048]{1,0:T(8,128)(2,1)S(1)}, bf16[256,2048]{1,0:T(8,128)(2,1)}, u32[]{:S(2)}, u32[]{:S(2)}) collective-permute-start(bf16[256,2048]{1,0:T(8,128)(2,1)S(1)} %collective-permute-done.36), channel_id=1, source_target_pairs={{0,2},{1,3},{2,4},{3,5},{4,6},{5,7},{6,8},{7,9},{8,10},{9,11},{10,... | collective-permute-start | bytes 3145736 | tf_op jit(solution)/shard_map/ppermute | solution.py:246
  327.5 63.5 %collective-permute-start.10 = (bf16[1024,512]{1,0:T(8,128)(2,1)S(1)}, bf16[1024,512]{1,0:T(8,128)(2,1)}, u32[]{:S(2)}, u32[]{:S(2)}) collective-permute-start(bf16[1024,512]{1,0:T(8,128)(2,1)S(1)} %collective-permute-done.9), channel_id=1, source_target_pairs={{0,14},{1,15},{2,0},{3,1},{4,2},{5,3},{6,4},{7,5},{8,6},{9,7},{10,... | collective-permute-start | bytes 3145736 | tf_op jit(solution)/shard_map/ppermute | solution.py:246
  346.1 48.8 %collective-permute-start.40 = (bf16[1024,512]{1,0:T(8,128)(2,1)S(1)}, bf16[1024,512]{1,0:T(8,128)(2,1)S(1)}, u32[]{:S(2)}, u32[]{:S(2)}) collective-permute-start(bf16[1024,512]{1,0:T(8,128)(2,1)S(1)} %collective-permute-done.37), channel_id=1, source_target_pairs={{0,2},{1,3},{2,4},{3,5},{4,6},{5,7},{6,8},{7,9},{8,10},{9,11},{10,... | collective-permute-start | bytes 3145736 | tf_op jit(solution)/shard_map/ppermute | solution.py:246
  350.0 63.5 %collective-permute-start.18 = (bf16[1024,512]{1,0:T(8,128)(2,1)S(1)}, bf16[1024,512]{1,0:T(8,128)(2,1)}, u32[]{:S(2)}, u32[]{:S(2)}) collective-permute-start(bf16[1024,512]{1,0:T(8,128)(2,1)S(1)} %collective-permute-done.17), channel_id=1, source_target_pairs={{0,14},{1,15},{2,0},{3,1},{4,2},{5,3},{6,4},{7,5},{8,6},{9,7},{10,... | collective-permute-start | bytes 3145736 | tf_op jit(solution)/shard_map/ppermute | solution.py:246
  368.6 49.0 %collective-permute-start.41 = (bf16[1024,512]{1,0:T(8,128)(2,1)S(1)}, bf16[1024,512]{1,0:T(8,128)(2,1)}, u32[]{:S(2)}, u32[]{:S(2)}) collective-permute-start(bf16[1024,512]{1,0:T(8,128)(2,1)S(1)} %collective-permute-done.38), channel_id=1, source_target_pairs={{0,2},{1,3},{2,4},{3,5},{4,6},{5,7},{6,8},{7,9},{8,10},{9,11},{10,... | collective-permute-start | bytes 3145736 | tf_op jit(solution)/shard_map/ppermute | solution.py:246
  372.6 63.5 %collective-permute-start.26 = (bf16[256,2048]{1,0:T(8,128)(2,1)}, bf16[256,2048]{1,0:T(8,128)(2,1)}, u32[]{:S(2)}, u32[]{:S(2)}) collective-permute-start(bf16[256,2048]{1,0:T(8,128)(2,1)} %collective-permute-done.25), channel_id=1, source_target_pairs={{0,14},{1,15},{2,0},{3,1},{4,2},{5,3},{6,4},{7,5},{8,6},{9,7},{10,... | collective-permute-start | bytes 3145736 | tf_op jit(solution)/shard_map/ppermute | solution.py:246
  391.0 49.0 %collective-permute-start.42 = (bf16[256,2048]{1,0:T(8,128)(2,1)}, bf16[256,2048]{1,0:T(8,128)(2,1)}, u32[]{:S(2)}, u32[]{:S(2)}) collective-permute-start(bf16[256,2048]{1,0:T(8,128)(2,1)} %collective-permute-done.39), channel_id=1, source_target_pairs={{0,2},{1,3},{2,4},{3,5},{4,6},{5,7},{6,8},{7,9},{8,10},{9,11},{10,... | collective-permute-start | bytes 3145736 | tf_op jit(solution)/shard_map/ppermute | solution.py:246
  395.9 62.6 %collective-permute-start.11 = (bf16[1024,512]{1,0:T(8,128)(2,1)}, bf16[1024,512]{1,0:T(8,128)(2,1)}, u32[]{:S(2)}, u32[]{:S(2)}) collective-permute-start(bf16[1024,512]{1,0:T(8,128)(2,1)} %collective-permute-done.10), channel_id=1, source_target_pairs={{0,14},{1,15},{2,0},{3,1},{4,2},{5,3},{6,4},{7,5},{8,6},{9,7},{10,... | collective-permute-start | bytes 3145736 | tf_op jit(solution)/shard_map/ppermute | solution.py:246
  413.5 49.4 %collective-permute-start.43 = (bf16[1024,512]{1,0:T(8,128)(2,1)}, bf16[1024,512]{1,0:T(8,128)(2,1)}, u32[]{:S(2)}, u32[]{:S(2)}) collective-permute-start(bf16[1024,512]{1,0:T(8,128)(2,1)} %copy-done.53), channel_id=1, source_target_pairs={{0,2},{1,3},{2,4},{3,5},{4,6},{5,7},{6,8},{7,9},{8,10},{9,11},{10,... | collective-permute-start | bytes 3145736 | tf_op jit(solution)/shard_map/ppermute | solution.py:246
  417.5 63.5 %collective-permute-start.19 = (bf16[1024,512]{1,0:T(8,128)(2,1)}, bf16[1024,512]{1,0:T(8,128)(2,1)}, u32[]{:S(2)}, u32[]{:S(2)}) collective-permute-start(bf16[1024,512]{1,0:T(8,128)(2,1)} %collective-permute-done.18), channel_id=1, source_target_pairs={{0,14},{1,15},{2,0},{3,1},{4,2},{5,3},{6,4},{7,5},{8,6},{9,7},{10,... | collective-permute-start | bytes 3145736 | tf_op jit(solution)/shard_map/ppermute | solution.py:246
  436.1 48.9 %collective-permute-start.44 = (bf16[1024,512]{1,0:T(8,128)(2,1)}, bf16[1024,512]{1,0:T(8,128)(2,1)}, u32[]{:S(2)}, u32[]{:S(2)}) collective-permute-start(bf16[1024,512]{1,0:T(8,128)(2,1)} %collective-permute-done.41), channel_id=1, source_target_pairs={{0,2},{1,3},{2,4},{3,5},{4,6},{5,7},{6,8},{7,9},{8,10},{9,11},{10,... | collective-permute-start | bytes 3145736 | tf_op jit(solution)/shard_map/ppermute | solution.py:246
  440.0 63.5 %collective-permute-start.27 = (bf16[256,2048]{1,0:T(8,128)(2,1)}, bf16[256,2048]{1,0:T(8,128)(2,1)}, u32[]{:S(2)}, u32[]{:S(2)}) collective-permute-start(bf16[256,2048]{1,0:T(8,128)(2,1)} %collective-permute-done.26), channel_id=1, source_target_pairs={{0,14},{1,15},{2,0},{3,1},{4,2},{5,3},{6,4},{7,5},{8,6},{9,7},{10,... | collective-permute-start | bytes 3145736 | tf_op jit(solution)/shard_map/ppermute | solution.py:246
  458.6 48.9 %collective-permute-start.45 = (bf16[256,2048]{1,0:T(8,128)(2,1)}, bf16[256,2048]{1,0:T(8,128)(2,1)}, u32[]{:S(2)}, u32[]{:S(2)}) collective-permute-start(bf16[256,2048]{1,0:T(8,128)(2,1)} %collective-permute-done.42), channel_id=1, source_target_pairs={{0,2},{1,3},{2,4},{3,5},{4,6},{5,7},{6,8},{7,9},{8,10},{9,11},{10,... | collective-permute-start | bytes 3145736 | tf_op jit(solution)/shard_map/ppermute | solution.py:246
  533.2 15.4 %collective-permute-start = (bf16[64,2048]{1,0:T(8,128)(2,1)S(1)}, bf16[64,2048]{1,0:T(8,128)(2,1)S(1)}, u32[]{:S(2)}, u32[]{:S(2)}) collective-permute-start(bf16[64,2048]{1,0:T(8,128)(2,1)S(1)} %get-tuple-element.1440), channel_id=1, source_target_pairs={{0,16},{8,24},{16,32},{24,40},{32,48},{40,56},{48,64},{56,72},{64,... | collective-permute-start | bytes 786440 | tf_op jit(solution)/shard_map/while/body/eval_jaxpr/ppermute | solution.py:297
  921.4 50.7 %collective-permute-start = (bf16[64,2048]{1,0:T(8,128)(2,1)S(1)}, bf16[64,2048]{1,0:T(8,128)(2,1)S(1)}, u32[]{:S(2)}, u32[]{:S(2)}) collective-permute-start(bf16[64,2048]{1,0:T(8,128)(2,1)S(1)} %get-tuple-element.1440), channel_id=1, source_target_pairs={{0,16},{8,24},{16,32},{24,40},{32,48},{40,56},{48,64},{56,72},{64,... | collective-permute-start | bytes 786440 | tf_op jit(solution)/shard_map/while/body/eval_jaxpr/ppermute | solution.py:297
  996.2 12.1 %collective-permute-start.49 = (bf16[64,2048]{1,0:T(8,128)(2,1)S(1)}, bf16[64,2048]{1,0:T(8,128)(2,1)S(1)}, u32[]{:S(2)}, u32[]{:S(2)}) collective-permute-start(bf16[64,2048]{1,0:T(8,128)(2,1)S(1)} %select_convert_fusion), channel_id=1, source_target_pairs={{0,8},{8,0},{16,24},{24,16},{32,40},{40,32},{48,56},{56,48},{64,72... | collective-permute-start | bytes 786440 | tf_op jit(solution)/shard_map/ppermute | solution.py:313
  (482 other events, 4704.6 us)

commit v3 on v2

--- a/solution.py
+++ b/solution.py
@@ -11,6 +11,8 @@
 both = ("section", "expert")
 z_size = 8
 source_count = 3 + (z_size - 1) * 6
+early = 3
+ready_count = 3 if early else 0
 lanes = 128
 
 
@@ -19,9 +21,9 @@
     return (hidden * lax.rsqrt(mean_square + norm_epsilon) * norm_scale).astype(jnp.bfloat16)
 
 
-def layer_copies(layer_half, my_z, refs, loaded, sems):
+def layer_copies(layer_half, experts, my_z, refs, loaded, sems):
     kept, arrived = refs[:3], refs[3:]
-    held = z_size // 2
+    first, count = experts
 
     def halves_of(ref, *before):
         middle = ref.shape[len(before)] // 2
@@ -33,9 +35,10 @@
     sources = [half for ref in kept for half in halves_of(ref)] + list(arrived)
 
     def start():
-        @pl.loop(0, held)
+        @pl.loop(0, count)
         def _(i):
-            offset = lax.rem(my_z - (layer_half * held + i) + 2 * z_size, z_size)
+            owner = layer_half * (z_size // 2) + first + i
+            offset = lax.rem(my_z - owner + 2 * z_size, z_size)
             for r in range(z_size):
 
                 @pl.when(offset == r)
@@ -51,16 +54,34 @@
 
 
 def load_kernel(place_ref, *refs):
-    sources, loaded, sems = refs[:source_count], refs[source_count:-1], refs[-1]
-    start, wait = layer_copies(0, place_ref[1], sources, loaded, sems)
+    sources, (middle_ref, last_ref) = refs[:source_count], refs[source_count : source_count + 2]
+    loaded, (first_out, second_out) = refs[source_count + 4 : -5], refs[-5:-3]
+    first_sems, second_sems, out_sems = refs[-3:]
+    held = z_size // 2
+    copies = [layer_copies(0, (0, held), place_ref[1], sources, loaded[:3], first_sems)]
+    if early:
+        copies.append(layer_copies(1, (0, early), place_ref[1], sources, loaded[3:], second_sems))
 
     @pl.when(place_ref[0] == 1)
     def _():
-        start()
-        pl.loop(0, z_size // 2)(wait)
-
-
-def experts_sum(my_core, rows, ids_ref, router_ref, gates, ups, downs, total, wait=None):
+        for start, _ in copies:
+            start()
+        for (_, wait), count in zip(copies, (held, early)):
+            pl.loop(0, count)(wait)
+
+    @pl.when(place_ref[3] == 1)
+    def _():
+        away = [
+            pltpu.make_async_copy(middle_ref, first_out, out_sems.at[0]),
+            pltpu.make_async_copy(last_ref, second_out, out_sems.at[1]),
+        ]
+        for copy in away:
+            copy.start()
+        for copy in away:
+            copy.wait()
+
+
+def experts_sum(my_core, rows, ids_ref, router_ref, experts, total):
     logits = jnp.dot(rows[...], router_ref[...], preferred_element_type=jnp.float32)
     lane = lax.broadcasted_iota(jnp.int32, logits.shape, 1)
     first = lane == ids_ref[:, 0:1]
@@ -72,18 +93,22 @@
     table = jnp.where(first, score_first / score_sum, zero) + jnp.where(
         second, score_second / score_sum, zero
     )
-    total[...] = jnp.zeros_like(total)
-
-    @pl.loop(0, gates.shape[0])
-    def _(i):
-        if wait is not None:
-            wait(i)
+    for i, (gates, ups, downs, wait) in enumerate(experts):
+        wait()
         weight = jnp.sum(jnp.where(lane == 2 * i + my_core, table, zero), axis=1, keepdims=True)
-        gate_part = jnp.dot(rows[...], gates[i], preferred_element_type=jnp.float32)
-        up_part = jnp.dot(rows[...], ups[i], preferred_element_type=jnp.float32)
+        gate_part = jnp.dot(rows[...], gates[...], preferred_element_type=jnp.float32)
+        up_part = jnp.dot(rows[...], ups[...], preferred_element_type=jnp.float32)
         act = (jax.nn.silu(gate_part) * up_part).astype(jnp.bfloat16)
-        produced = jnp.dot(act, downs[i], preferred_element_type=jnp.float32)
-        total[...] += produced.astype(jnp.bfloat16).astype(jnp.float32) * weight
+        produced = jnp.dot(act, downs[...], preferred_element_type=jnp.float32)
+        part = produced.astype(jnp.bfloat16).astype(jnp.float32) * weight
+        if i == 0:
+            total[...] = part
+        else:
+            total[...] += part
+
+
+def at_once(refs):
+    return [tuple(ref.at[i] for ref in refs) + (lambda: None,) for i in range(refs[0].shape[0])]
 
 
 def first_kernel(
@@ -96,17 +121,20 @@
     def _():
         rows[pl.ds(0, count)] = normed_of(mine_ref[...].astype(jnp.float32), scale_ref[...])
         rows[pl.ds(count, count)] = normed_of(other_ref[...].astype(jnp.float32), scale_ref[...])
-        experts_sum(place_ref[2], rows, ids_ref, router_ref, gates, ups, downs, part_ref)
+        experts = at_once((gates, ups, downs))
+        experts_sum(place_ref[2], rows, ids_ref, router_ref, experts, part_ref)
         lent_ref[...] = part_ref[...].astype(jnp.bfloat16)
 
 
 def second_kernel(
-    place_ref, mine_ref, other_ref, part_ref, back_ref, scale_ref, ids_ref, router_ref, stored_ref, *refs
+    place_ref, mine_ref, other_ref, part_ref, back_ref, scale_ref, ids_ref, router_ref, *refs
 ):
-    sources = refs[:source_count]
-    middle_ref, own_ref, lent_ref, gates, ups, downs, rows, total, sems = refs[source_count:]
-    count = mine_ref.shape[0]
-    start, wait = layer_copies(1, place_ref[1], sources, (gates, ups, downs), sems)
+    ready, sources, refs = refs[:ready_count], refs[ready_count:][:source_count], refs[ready_count + source_count :]
+    middle_ref, own_ref, lent_ref, gates, ups, downs, rows, total, sems = refs
+    count, late = mine_ref.shape[0], gates.shape[0]
+    start, wait = layer_copies(
+        1, (early, late), place_ref[1], sources, (gates, ups, downs), sems
+    )
 
     @pl.when(place_ref[0] == 1)
     def _():
@@ -120,26 +148,21 @@
             part_ref[count:] + back_ref[:count].astype(jnp.float32)
         )
         rows[pl.ds(count, count)] = normed_of(beside, scale_ref[...])
-        experts_sum(place_ref[2], rows, ids_ref, router_ref, gates, ups, downs, total, wait)
+        experts = (at_once(ready) if early else []) + [
+            (gates.at[i], ups.at[i], downs.at[i], functools.partial(wait, i)) for i in range(late)
+        ]
+        experts_sum(place_ref[2], rows, ids_ref, router_ref, experts, total)
         own_ref[...] = total[:count]
         lent_ref[...] = total[count:].astype(jnp.bfloat16)
 
-    @pl.when(place_ref[0] == 0)
-    def _():
-        middle_ref[...] = stored_ref[...]
-
-
-def add_kernel(place_ref, middle_ref, own_ref, back_ref, stored_ref, sum_ref, sent_ref):
+
+def add_kernel(place_ref, middle_ref, own_ref, back_ref, sum_ref, sent_ref):
     @pl.when(place_ref[0] == 1)
     def _():
         total = middle_ref[...] + (own_ref[...] + back_ref[...].astype(jnp.float32))
         sum_ref[...] = total
         sent_ref[...] = total.astype(jnp.bfloat16)
 
-    @pl.when(place_ref[0] == 0)
-    def _():
-        sum_ref[...] = stored_ref[...]
-
 
 def vmem(count):
     return [pl.BlockSpec(memory_space=pltpu.VMEM)] * count
@@ -149,33 +172,40 @@
     return jax.ShapeDtypeStruct(shape, kind)
 
 
-def layer_shapes(sources):
+def layer_shapes(sources, count):
+    width, units = sources[0].shape
+    return [(count, width, units), (count, width, units), (count, units, width)]
+
+
+def copy_sems(count):
+    return pltpu.SemaphoreType.DMA((max(count, 1), 6))
+
+
+def in_hbm(count):
+    return [pl.BlockSpec(memory_space=pltpu.HBM)] * count
+
+
+def load_ahead(place, sources, middle, last, stored):
     width, units = sources[0].shape
     held = z_size // 2
-    return [(held, width, units), (held, width, units), (held, units, width)]
-
-
-def copy_sems():
-    return pltpu.SemaphoreType.DMA((z_size // 2, 6))
-
-
-def in_hbm(sources):
-    return [pl.BlockSpec(memory_space=pltpu.HBM)] * len(sources)
-
-
-def load_first(place, sources):
-    width, units = sources[0].shape
-    return pl.pallas_call(
+    shapes = layer_shapes(sources, held) + (layer_shapes(sources, early) if early else [])
+    results = pl.pallas_call(
         load_kernel,
-        out_shape=tuple(pltpu.VMEM(shape, jnp.bfloat16) for shape in layer_shapes(sources)),
-        in_specs=[pl.BlockSpec(memory_space=pltpu.SMEM)] + in_hbm(sources),
-        out_specs=tuple(vmem(3)),
-        scratch_shapes=[copy_sems()],
+        out_shape=tuple(pltpu.VMEM(shape, jnp.bfloat16) for shape in shapes)
+        + tuple(like(array.shape, array.dtype) for array in stored),
+        in_specs=[pl.BlockSpec(memory_space=pltpu.SMEM)]
+        + in_hbm(len(sources))
+        + [pl.BlockSpec(memory_space=pl.ANY)] * 2
+        + in_hbm(2),
+        out_specs=tuple(vmem(len(shapes)) + in_hbm(2)),
+        scratch_shapes=[copy_sems(held), copy_sems(early), pltpu.SemaphoreType.DMA((2,))],
+        input_output_aliases={source_count + 3 + i: len(shapes) + i for i in range(2)},
         compiler_params=pltpu.CompilerParams(vmem_limit_bytes=1 << 20),
         cost_estimate=pl.CostEstimate(
-            flops=0, bytes_accessed=3 * z_size * width * units, transcendentals=0
+            flops=0, bytes_accessed=6 * (held + early) * width * units, transcendentals=0
         ),
-    )(place, *sources)
+    )(place, *sources, middle, last, *stored)
+    return results[:3], results[3:-2], results[-2:]
 
 
 def run_first(place, mine, other, scale, ids, router, weights):
@@ -190,7 +220,7 @@
     )(place, mine, other, scale, ids, router, *weights)
 
 
-def run_second(place, mine, other, part, back, scale, ids, router, stored, sources):
+def run_second(place, mine, other, part, back, scale, ids, router, ready, sources):
     count, width = mine.shape
     return pl.pallas_call(
         second_kernel,
@@ -199,28 +229,32 @@
             like((count, width), jnp.float32),
             like((count, width), jnp.bfloat16),
         ),
-        in_specs=[pl.BlockSpec(memory_space=pltpu.SMEM)] + vmem(8) + in_hbm(sources),
+        in_specs=[pl.BlockSpec(memory_space=pltpu.SMEM)]
+        + vmem(7 + len(ready))
+        + in_hbm(len(sources)),
         out_specs=tuple(vmem(3)),
-        scratch_shapes=[pltpu.VMEM(shape, jnp.bfloat16) for shape in layer_shapes(sources)]
+        scratch_shapes=[
+            pltpu.VMEM(shape, jnp.bfloat16) for shape in layer_shapes(sources, z_size // 2 - early)
+        ]
         + [
             pltpu.VMEM((2 * count, width), jnp.bfloat16),
             pltpu.VMEM((2 * count, width), jnp.float32),
-            copy_sems(),
+            copy_sems(z_size // 2 - early),
         ],
-        input_output_aliases={8: 0},
-        compiler_params=pltpu.CompilerParams(vmem_limit_bytes=34 << 20),
-    )(place, mine, other, part, back, scale, ids, router, stored, *sources)
-
-
-def run_add(place, middle, own, back, stored):
+        compiler_params=pltpu.CompilerParams(
+            vmem_limit_bytes=(10 + 6 * (z_size // 2 - early)) << 20
+        ),
+    )(place, mine, other, part, back, scale, ids, router, *ready, *sources)
+
+
+def run_add(place, middle, own, back):
     return pl.pallas_call(
         add_kernel,
         out_shape=(like(middle.shape, jnp.float32), like(middle.shape, jnp.bfloat16)),
-        in_specs=[pl.BlockSpec(memory_space=pltpu.SMEM)] + vmem(4),
+        in_specs=[pl.BlockSpec(memory_space=pltpu.SMEM)] + vmem(3),
         out_specs=tuple(vmem(2)),
-        input_output_aliases={4: 0},
         compiler_params=pltpu.CompilerParams(vmem_limit_bytes=4 << 20),
-    )(place, middle, own, back, stored)
+    )(place, middle, own, back)
 
 
 def device_at(ring, z, core):
@@ -292,22 +326,27 @@
         return lax.ppermute(value, "expert", other_core)
 
     def ring_step(step, state):
-        sent, stored_first, stored_second = state
-        place = jnp.stack([(ring_id == step).astype(jnp.int32), my_z, my_core])
+        sent, middle, last, stored = state
+        flags = [(ring_id == step).astype(jnp.int32), my_z, my_core]
+        place = jnp.stack(flags + [(ring_id == step - 1).astype(jnp.int32)])
         mine = lax.ppermute(sent, "section", next_ring)
-        mine, weights = lax.optimization_barrier((mine, load_first(place, sources)))
+        ahead = load_ahead(place, sources, middle, last, stored)
+        mine, (weights, ready, stored) = lax.optimization_barrier((mine, ahead))
         other = exchange(mine)
         part, lent = run_first(place, mine, other, scales[0], ids[0], routers[0], weights)
         back = exchange(lent)
-        stored_first, own, lent = run_second(
-            place, mine, other, part, back, scales[1], ids[1], routers[1], stored_first, sources
+        middle, own, lent = run_second(
+            place, mine, other, part, back, scales[1], ids[1], routers[1], ready, sources
         )
-        back = exchange(lent)
-        stored_second, sent = run_add(place, stored_first, own, back, stored_second)
-        return sent, stored_first, stored_second
+        last, sent = run_add(place, middle, own, exchange(lent))
+        return sent, middle, last, stored
 
     blank = jnp.zeros(entering.shape, jnp.float32)
-    _, stored_first, stored_second = lax.fori_loop(0, rings, ring_step, (entering, blank, blank))
+    state = (entering, blank, blank, (blank, blank + 0))
+    _, middle, last, stored = lax.fori_loop(0, rings, ring_step, state)
+    final = ring_id == rings - 1
+    stored_first = jnp.where(final, middle, stored[0])
+    stored_second = jnp.where(final, last, stored[1])
     kept = jnp.where(upper == 0, stored_first, stored_second)
     given = jnp.where(upper == 0, stored_second, stored_first)
     taken = lax.ppermute(given.astype(jnp.bfloat16), "section", other_half).astype(jnp.float32)

time: 1030 us -> 1050 us (1.019)
  the two profiles are of different devices: /device:TPU:31 before, /device:TPU:119 now
where the time goes in v3:
time: 1050 us; the launch traced here: 1040 us
  waiting for transfers between devices  642 us (61%)
  starting transfers between devices  217 us (21%)
  Pallas kernels  152 us (14%)
  local copies, waits for them, and re-layouts  20.7 us (2%)
    ppermute x42, waiting for transfers between devices, gather_ring(): lax.ppermute(travelling[m], both, forward if m % 2 == 0 else backward)  413 us
    ppermute x16, starting transfers between devices, ring_step(): mine = lax.ppermute(sent, 'section', next_ring)  109 us
    ppermute x16, waiting for transfers between devices, ring_step(): mine = lax.ppermute(sent, 'section', next_ring)  94.7 us
    ppermute x48, waiting for transfers between devices, exchange(): return lax.ppermute(value, 'expert', other_core)  65.1 us
    pallas_call x16, Pallas kernels, load_ahead(): pl.pallas_call(load_kernel, out_shape=tuple((pltpu.VMEM(shape, jnp.bfloat...  61.7 us
    ppermute x3, waiting for transfers between devices, both_layers(): theirs = lax.ppermute(value, 'section', other_half)  57.3 us
    ppermute x42, starting transfers between devices, gather_ring(): lax.ppermute(travelling[m], both, forward if m % 2 == 0 else backward)  53.1 us
    pallas_call x16, Pallas kernels, run_second(): pl.pallas_call(second_kernel, out_shape=(like((count, width), jnp.float32...  36.7 us
  transfers between devices with their start and end apart: 110, of which 87 were waited for; matrix products, arithmetic and copies ran while one was open for 1% of the time, Pallas kernels for 6%

profile of v3, /device:TPU:119, one launch (start us, length us, event | category | flops | bytes accessed | tf_op | source)
XLA Modules:
  0.0 1038.3 jit_solution(2194372030278276972)
XLA Ops:
  6.4 5.7 collective-permute-start.48
  12.3 5.3 collective-permute-start.46
  19.2 57.1 %collective-permute-done.47 = s32[8,128,2]{1,2,0:T(2,128)S(1)} collective-permute-done((s32[8,128,2]{1,2,0:T(2,128)S(1)}, s32[8,128,2]{1,2,0:T(2,128)S(1)}, u32[]{:S(2)}, u32[]{:S(2)}) %collective-permute-start.47) | collective-permute-done | bytes 8224 | tf_op jit(solution)/shard_map/ppermute | solution.py:304
  80.6 19.9 %collective-permute-done.21 = bf16[256,2048]{1,0:T(8,128)(2,1)S(1)} collective-permute-done((bf16[256,2048]{1,0:T(8,128)(2,1)S(1)}, bf16[256,2048]{1,0:T(8,128)(2,1)S(1)}, u32[]{:S(2)}, u32[]{:S(2)}) %collective-permute-start.21) | collective-permute-done | bytes 1048608 | tf_op jit(solution)/shard_map/ppermute | solution.py:280
  101.4 20.8 %collective-permute-done.12 = bf16[1024,512]{1,0:T(8,128)(2,1)S(1)} collective-permute-done((bf16[1024,512]{1,0:T(8,128)(2,1)}, bf16[1024,512]{1,0:T(8,128)(2,1)S(1)}, u32[]{:S(2)}, u32[]{:S(2)}) %collective-permute-start.12) | collective-permute-done | bytes 1048608 | tf_op jit(solution)/shard_map/ppermute | solution.py:280
  125.5 19.1 %collective-permute-done.20 = bf16[256,2048]{1,0:T(8,128)(2,1)S(1)} collective-permute-done((bf16[256,2048]{1,0:T(8,128)(2,1)S(1)}, bf16[256,2048]{1,0:T(8,128)(2,1)S(1)}, u32[]{:S(2)}, u32[]{:S(2)}) %collective-permute-start.20) | collective-permute-done | bytes 1048608 | tf_op jit(solution)/shard_map/ppermute | solution.py:280
  149.6 18.2 %collective-permute-done.22 = bf16[256,2048]{1,0:T(8,128)(2,1)S(1)} collective-permute-done((bf16[256,2048]{1,0:T(8,128)(2,1)S(1)}, bf16[256,2048]{1,0:T(8,128)(2,1)S(1)}, u32[]{:S(2)}, u32[]{:S(2)}) %collective-permute-start.22) | collective-permute-done | bytes 1048608 | tf_op jit(solution)/shard_map/ppermute | solution.py:280
  168.0 21.6 %collective-permute-done.29 = bf16[1024,512]{1,0:T(8,128)(2,1)S(1)} collective-permute-done((bf16[1024,512]{1,0:T(8,128)(2,1)S(1)}, bf16[1024,512]{1,0:T(8,128)(2,1)S(1)}, u32[]{:S(2)}, u32[]{:S(2)}) %collective-permute-start.29) | collective-permute-done | bytes 1048608 | tf_op jit(solution)/shard_map/ppermute | solution.py:280
  192.9 19.1 %collective-permute-done.30 = bf16[256,2048]{1,0:T(8,128)(2,1)S(1)} collective-permute-done((bf16[256,2048]{1,0:T(8,128)(2,1)S(1)}, bf16[256,2048]{1,0:T(8,128)(2,1)S(1)}, u32[]{:S(2)}, u32[]{:S(2)}) %collective-permute-start.30) | collective-permute-done | bytes 1048608 | tf_op jit(solution)/shard_map/ppermute | solution.py:280
  217.0 18.2 %collective-permute-done.23 = bf16[256,2048]{1,0:T(8,128)(2,1)S(1)} collective-permute-done((bf16[256,2048]{1,0:T(8,128)(2,1)S(1)}, bf16[256,2048]{1,0:T(8,128)(2,1)S(1)}, u32[]{:S(2)}, u32[]{:S(2)}) %collective-permute-start.23) | collective-permute-done | bytes 1048608 | tf_op jit(solution)/shard_map/ppermute | solution.py:280
  235.4 21.6 %collective-permute-done.32 = bf16[1024,512]{1,0:T(8,128)(2,1)S(1)} collective-permute-done((bf16[1024,512]{1,0:T(8,128)(2,1)S(1)}, bf16[1024,512]{1,0:T(8,128)(2,1)S(1)}, u32[]{:S(2)}, u32[]{:S(2)}) %collective-permute-start.32) | collective-permute-done | bytes 1048608 | tf_op jit(solution)/shard_map/ppermute | solution.py:280
  260.3 19.1 %collective-permute-done.33 = bf16[256,2048]{1,0:T(8,128)(2,1)S(1)} collective-permute-done((bf16[256,2048]{1,0:T(8,128)(2,1)S(1)}, bf16[256,2048]{1,0:T(8,128)(2,1)S(1)}, u32[]{:S(2)}, u32[]{:S(2)}) %collective-permute-start.33) | collective-permute-done | bytes 1048608 | tf_op jit(solution)/shard_map/ppermute | solution.py:280
  284.4 18.2 %collective-permute-done.24 = bf16[256,2048]{1,0:T(8,128)(2,1)S(1)} collective-permute-done((bf16[256,2048]{1,0:T(8,128)(2,1)S(1)}, bf16[256,2048]{1,0:T(8,128)(2,1)S(1)}, u32[]{:S(2)}, u32[]{:S(2)}) %collective-permute-start.24) | collective-permute-done | bytes 1048608 | tf_op jit(solution)/shard_map/ppermute | solution.py:280
  302.8 21.6 %collective-permute-done.35 = bf16[1024,512]{1,0:T(8,128)(2,1)S(1)} collective-permute-done((bf16[1024,512]{1,0:T(8,128)(2,1)S(1)}, bf16[1024,512]{1,0:T(8,128)(2,1)S(1)}, u32[]{:S(2)}, u32[]{:S(2)}) %collective-permute-start.35) | collective-permute-done | bytes 1048608 | tf_op jit(solution)/shard_map/ppermute | solution.py:280
  327.7 19.1 %collective-permute-done.36 = bf16[256,2048]{1,0:T(8,128)(2,1)S(1)} collective-permute-done((bf16[256,2048]{1,0:T(8,128)(2,1)S(1)}, bf16[256,2048]{1,0:T(8,128)(2,1)S(1)}, u32[]{:S(2)}, u32[]{:S(2)}) %collective-permute-start.36) | collective-permute-done | bytes 1048608 | tf_op jit(solution)/shard_map/ppermute | solution.py:280
  352.2 17.9 %collective-permute-done.25 = bf16[256,2048]{1,0:T(8,128)(2,1)} collective-permute-done((bf16[256,2048]{1,0:T(8,128)(2,1)S(1)}, bf16[256,2048]{1,0:T(8,128)(2,1)}, u32[]{:S(2)}, u32[]{:S(2)}) %collective-permute-start.25) | collective-permute-done | bytes 1048608 | tf_op jit(solution)/shard_map/ppermute | solution.py:280
  370.3 21.6 %collective-permute-done.38 = bf16[1024,512]{1,0:T(8,128)(2,1)} collective-permute-done((bf16[1024,512]{1,0:T(8,128)(2,1)S(1)}, bf16[1024,512]{1,0:T(8,128)(2,1)}, u32[]{:S(2)}, u32[]{:S(2)}) %collective-permute-start.38) | collective-permute-done | bytes 1048608 | tf_op jit(solution)/shard_map/ppermute | solution.py:280
  395.3 19.1 %collective-permute-done.39 = bf16[256,2048]{1,0:T(8,128)(2,1)} collective-permute-done((bf16[256,2048]{1,0:T(8,128)(2,1)S(1)}, bf16[256,2048]{1,0:T(8,128)(2,1)}, u32[]{:S(2)}, u32[]{:S(2)}) %collective-permute-start.39) | collective-permute-done | bytes 1048608 | tf_op jit(solution)/shard_map/ppermute | solution.py:280
  420.9 16.7 %collective-permute-done.26 = bf16[256,2048]{1,0:T(8,128)(2,1)} collective-permute-done((bf16[256,2048]{1,0:T(8,128)(2,1)}, bf16[256,2048]{1,0:T(8,128)(2,1)}, u32[]{:S(2)}, u32[]{:S(2)}) %collective-permute-start.26) | collective-permute-done | bytes 1048608 | tf_op jit(solution)/shard_map/ppermute | solution.py:280
  437.6 21.7 %collective-permute-done.41 = bf16[1024,512]{1,0:T(8,128)(2,1)} collective-permute-done((bf16[1024,512]{1,0:T(8,128)(2,1)}, bf16[1024,512]{1,0:T(8,128)(2,1)}, u32[]{:S(2)}, u32[]{:S(2)}) %collective-permute-start.41) | collective-permute-done | bytes 1048608 | tf_op jit(solution)/shard_map/ppermute | solution.py:280
  462.7 19.1 %collective-permute-done.42 = bf16[256,2048]{1,0:T(8,128)(2,1)} collective-permute-done((bf16[256,2048]{1,0:T(8,128)(2,1)}, bf16[256,2048]{1,0:T(8,128)(2,1)}, u32[]{:S(2)}, u32[]{:S(2)}) %collective-permute-start.42) | collective-permute-done | bytes 1048608 | tf_op jit(solution)/shard_map/ppermute | solution.py:280
  489.3 15.7 %collective-permute-done.27 = bf16[256,2048]{1,0:T(8,128)(2,1)} collective-permute-done((bf16[256,2048]{1,0:T(8,128)(2,1)}, bf16[256,2048]{1,0:T(8,128)(2,1)}, u32[]{:S(2)}, u32[]{:S(2)}) %collective-permute-start.27) | collective-permute-done | bytes 1048608 | tf_op jit(solution)/shard_map/ppermute | solution.py:280
  505.0 21.7 %collective-permute-done.44 = bf16[1024,512]{1,0:T(8,128)(2,1)} collective-permute-done((bf16[1024,512]{1,0:T(8,128)(2,1)}, bf16[1024,512]{1,0:T(8,128)(2,1)}, u32[]{:S(2)}, u32[]{:S(2)}) %collective-permute-start.44) | collective-permute-done | bytes 1048608 | tf_op jit(solution)/shard_map/ppermute | solution.py:280
  526.7 22.5 %collective-permute-done.45 = bf16[256,2048]{1,0:T(8,128)(2,1)} collective-permute-done((bf16[256,2048]{1,0:T(8,128)(2,1)}, bf16[256,2048]{1,0:T(8,128)(2,1)}, u32[]{:S(2)}, u32[]{:S(2)}) %collective-permute-start.45) | collective-permute-done | bytes 1048608 | tf_op jit(solution)/shard_map/ppermute | solution.py:280
  552.6 463.4 %while.23 = (s32[]{:T(128)}, bf16[64,2048]{1,0:T(8,128)(2,1)S(1)}, f32[64,2048]{1,0:T(8,128)}, f32[64,2048]{1,0:T(8,128)}, f32[64,2048]{1,0:T(8,128)}, /*index=5...) while((s32[]{:T(128)}, bf16[64,2048]{1,0:T(8,128)(2,1)S(1)}, ...), condition=%wide.region_1.2_spmd, body=%wide.region_0.1_spmd.sunk | while | flops 19 | bytes 82838424 | solution.py:346
  574.3 5.4 collective-permute-done.mine_ref
  591.4 16.8 %collective-permute-start = (bf16[64,2048]{1,0:T(8,128)(2,1)S(1)}, bf16[64,2048]{1,0:T(8,128)(2,1)S(1)}, u32[]{:S(2)}, u32[]{:S(2)}) collective-permute-start(bf16[64,2048]{1,0:T(8,128)(2,1)S(1)} %get-tuple-element.1964), channel_id=1, source_target_pairs={{0,16},{8,24},{16,32},{24,40},{32,48},{40,56},{48,64},{56,72},{64,... | collective-permute-start | bytes 786440 | tf_op jit(solution)/shard_map/while/body/eval_jaxpr/ppermute | solution.py:332
  609.3 4.2 collective-permute-done.mine_ref
  625.2 27.9 %collective-permute-start = (bf16[64,2048]{1,0:T(8,128)(2,1)S(1)}, bf16[64,2048]{1,0:T(8,128)(2,1)S(1)}, u32[]{:S(2)}, u32[]{:S(2)}) collective-permute-start(bf16[64,2048]{1,0:T(8,128)(2,1)S(1)} %get-tuple-element.1964), channel_id=1, source_target_pairs={{0,16},{8,24},{16,32},{24,40},{32,48},{40,56},{48,64},{56,72},{64,... | collective-permute-start | bytes 786440 | tf_op jit(solution)/shard_map/while/body/eval_jaxpr/ppermute | solution.py:332
  654.1 4.2 collective-permute-done.mine_ref
  670.0 5.5 collective-permute-start
  692.5 5.5 collective-permute-start
  715.0 5.5 collective-permute-start
  737.4 5.5 collective-permute-start
  759.9 5.5 collective-permute-start
  782.4 5.5 collective-permute-start
  804.8 5.5 collective-permute-start
  827.3 7.1 collective-permute-start
  851.4 5.5 collective-permute-start
  873.9 5.5 collective-permute-start
  896.3 5.5 collective-permute-start
  901.9 14.1 %eval_jaxpr.32 = (bf16[4,2048,512]{2,1,0:T(8,128)(2,1)S(1)}, bf16[4,2048,512]{2,1,0:T(8,128)(2,1)S(1)}, bf16[4,512,2048]{2,1,0:T(8,128)(2,1)S(1)}, bf16[3,2048,5...) custom-call(s32[4]{0:T(128)S(1)} %pad_add_fusion.4.place_ref, ...), custom_call_target="tpu_custom_call", output_to_operand_aliasing={{6}: (48, {}), {7}: (49, {})} | custom-call | bytes 44040192 | tf_op jit(solution)/shard_map/while/body/eval_jaxpr/pallas_call | solution.py:192
  916.0 35.2 %collective-permute-done.mine_ref = bf16[64,2048]{1,0:T(8,128)(2,1)S(1)} collective-permute-done((bf16[64,2048]{1,0:T(8,128)(2,1)S(1)}, bf16[64,2048]{1,0:T(8,128)(2,1)S(1)}, u32[]{:S(2)}, u32[]{:S(2)}) %collective-permute-start) | collective-permute-done | bytes 262176 | tf_op jit(solution)/shard_map/while/body/eval_jaxpr/ppermute | solution.py:332
  953.2 5.5 eval_jaxpr.33
  960.7 6.7 eval_jaxpr.34
  971.3 33.8 %eval_jaxpr.32 = (bf16[4,2048,512]{2,1,0:T(8,128)(2,1)S(1)}, bf16[4,2048,512]{2,1,0:T(8,128)(2,1)S(1)}, bf16[4,512,2048]{2,1,0:T(8,128)(2,1)S(1)}, bf16[3,2048,5...) custom-call(s32[4]{0:T(128)S(1)} %pad_add_fusion.4.place_ref, ...), custom_call_target="tpu_custom_call", output_to_operand_aliasing={{6}: (48, {}), {7}: (49, {})} | custom-call | bytes 44040192 | tf_op jit(solution)/shard_map/while/body/eval_jaxpr/pallas_call | solution.py:192
  1017.4 7.6 collective-permute-start.49
  1025.1 11.9 %collective-permute-done.49 = bf16[64,2048]{1,0:T(8,128)(2,1)S(1)} collective-permute-done((bf16[64,2048]{1,0:T(8,128)(2,1)S(1)}, bf16[64,2048]{1,0:T(8,128)(2,1)S(1)}, u32[]{:S(2)}, u32[]{:S(2)}) %collective-permute-start.49) | collective-permute-done | bytes 262176 | tf_op jit(solution)/shard_map/ppermute | solution.py:352
  (541 shorter events, 320.4 us)
Async XLA Ops:
  3.1 76.0 %collective-permute-start.5 = (bf16[1024,512]{1,0:T(8,128)(2,1)}, bf16[1024,512]{1,0:T(8,128)(2,1)}, u32[]{:S(2)}, u32[]{:S(2)}) collective-permute-start(bf16[1024,512]{1,0:T(8,128)(2,1)} %get-tuple-element.1476), channel_id=1, source_target_pairs={{0,14},{1,15},{2,0},{3,1},{4,2},{5,3},{6,4},{7,5},{8,6},{9,7},{10,... | collective-permute-start | bytes 3145736 | tf_op jit(solution)/shard_map/ppermute | solution.py:280
  6.1 73.1 %collective-permute-start.13 = (bf16[1024,512]{1,0:T(8,128)(2,1)}, bf16[1024,512]{1,0:T(8,128)(2,1)}, u32[]{:S(2)}, u32[]{:S(2)}) collective-permute-start(bf16[1024,512]{1,0:T(8,128)(2,1)} %get-tuple-element.1474), channel_id=1, source_target_pairs={{0,14},{1,15},{2,0},{3,1},{4,2},{5,3},{6,4},{7,5},{8,6},{9,7},{10,... | collective-permute-start | bytes 3145736 | tf_op jit(solution)/shard_map/ppermute | solution.py:280
  6.4 72.6 %collective-permute-start.48 = (bf16[2048,8]{1,0:T(8,128)(2,1)S(1)}, bf16[2048,8]{1,0:T(8,128)(2,1)S(1)}, u32[]{:S(2)}, u32[]{:S(2)}) collective-permute-start(bf16[2048,8]{1,0:T(8,128)(2,1)S(1)} %bitcast.46), channel_id=1, source_target_pairs={{0,8},{8,0},{16,24},{24,16},{32,40},{40,32},{48,56},{56,48},{64,72... | collective-permute-start | bytes 98312 | tf_op jit(solution)/shard_map/ppermute | solution.py:304
  12.1 64.1 %collective-permute-start.47 = (s32[8,128,2]{1,2,0:T(2,128)S(1)}, s32[8,128,2]{1,2,0:T(2,128)S(1)}, u32[]{:S(2)}, u32[]{:S(2)}) collective-permute-start(s32[8,128,2]{1,2,0:T(2,128)S(1)} %bitcast.48), channel_id=1, source_target_pairs={{0,8},{8,0},{16,24},{24,16},{32,40},{40,32},{48,56},{56,48},{64,72... | collective-permute-start | bytes 24584 | tf_op jit(solution)/shard_map/ppermute | solution.py:304
  12.3 64.2 %collective-permute-start.46 = (f32[1,2048]{1,0:T(1,128)S(1)}, f32[1,2048]{1,0:T(1,128)S(1)}, u32[]{:S(2)}, u32[]{:S(2)}) collective-permute-start(f32[1,2048]{1,0:T(1,128)S(1)} %copy-done.37), channel_id=1, source_target_pairs={{0,8},{8,0},{16,24},{24,16},{32,40},{40,32},{48,56},{56,48},{64,72... | collective-permute-start | bytes 24584 | tf_op jit(solution)/shard_map/ppermute | solution.py:304
  76.3 24.1 %collective-permute-start.21 = (bf16[256,2048]{1,0:T(8,128)(2,1)S(1)}, bf16[256,2048]{1,0:T(8,128)(2,1)S(1)}, u32[]{:S(2)}, u32[]{:S(2)}) collective-permute-start(bf16[256,2048]{1,0:T(8,128)(2,1)S(1)} %get-tuple-element.1472), channel_id=1, source_target_pairs={{0,14},{1,15},{2,0},{3,1},{4,2},{5,3},{6,4},{7,5},{8,6},{9,7},{10,... | collective-permute-start | bytes 3145736 | tf_op jit(solution)/shard_map/ppermute | solution.py:280
  76.5 24.0 %collective-permute-start.4 = (bf16[1024,512]{1,0:T(8,128)(2,1)}, bf16[1024,512]{1,0:T(8,128)(2,1)S(1)}, u32[]{:S(2)}, u32[]{:S(2)}) collective-permute-start(bf16[1024,512]{1,0:T(8,128)(2,1)} %get-tuple-element.1477), channel_id=1, source_target_pairs={{0,2},{1,3},{2,4},{3,5},{4,6},{5,7},{6,8},{7,9},{8,10},{9,11},{10,... | collective-permute-start | bytes 3145736 | tf_op jit(solution)/shard_map/ppermute | solution.py:280
  79.0 43.2 %collective-permute-start.12 = (bf16[1024,512]{1,0:T(8,128)(2,1)}, bf16[1024,512]{1,0:T(8,128)(2,1)S(1)}, u32[]{:S(2)}, u32[]{:S(2)}) collective-permute-start(bf16[1024,512]{1,0:T(8,128)(2,1)} %get-tuple-element.1475), channel_id=1, source_target_pairs={{0,2},{1,3},{2,4},{3,5},{4,6},{5,7},{6,8},{7,9},{8,10},{9,11},{10,... | collective-permute-start | bytes 3145736 | tf_op jit(solution)/shard_map/ppermute | solution.py:280
  79.1 65.5 %collective-permute-start.20 = (bf16[256,2048]{1,0:T(8,128)(2,1)S(1)}, bf16[256,2048]{1,0:T(8,128)(2,1)S(1)}, u32[]{:S(2)}, u32[]{:S(2)}) collective-permute-start(bf16[256,2048]{1,0:T(8,128)(2,1)S(1)} %get-tuple-element.1473), channel_id=1, source_target_pairs={{0,2},{1,3},{2,4},{3,5},{4,6},{5,7},{6,8},{7,9},{8,10},{9,11},{10,... | collective-permute-start | bytes 3145736 | tf_op jit(solution)/shard_map/ppermute | solution.py:280
  79.2 68.8 %collective-permute-start.6 = (bf16[1024,512]{1,0:T(8,128)(2,1)}, bf16[1024,512]{1,0:T(8,128)(2,1)S(1)}, u32[]{:S(2)}, u32[]{:S(2)}) collective-permute-start(bf16[1024,512]{1,0:T(8,128)(2,1)} %collective-permute-done.5), channel_id=1, source_target_pairs={{0,14},{1,15},{2,0},{3,1},{4,2},{5,3},{6,4},{7,5},{8,6},{9,7},{10,... | collective-permute-start | bytes 3145736 | tf_op jit(solution)/shard_map/ppermute | solution.py:280
  100.4 47.7 %collective-permute-start.14 = (bf16[1024,512]{1,0:T(8,128)(2,1)}, bf16[1024,512]{1,0:T(8,128)(2,1)S(1)}, u32[]{:S(2)}, u32[]{:S(2)}) collective-permute-start(bf16[1024,512]{1,0:T(8,128)(2,1)} %collective-permute-done.13), channel_id=1, source_target_pairs={{0,14},{1,15},{2,0},{3,1},{4,2},{5,3},{6,4},{7,5},{8,6},{9,7},{10,... | collective-permute-start | bytes 3145736 | tf_op jit(solution)/shard_map/ppermute | solution.py:280
  101.4 66.4 %collective-permute-start.22 = (bf16[256,2048]{1,0:T(8,128)(2,1)S(1)}, bf16[256,2048]{1,0:T(8,128)(2,1)S(1)}, u32[]{:S(2)}, u32[]{:S(2)}) collective-permute-start(bf16[256,2048]{1,0:T(8,128)(2,1)S(1)} %collective-permute-done.21), channel_id=1, source_target_pairs={{0,14},{1,15},{2,0},{3,1},{4,2},{5,3},{6,4},{7,5},{8,6},{9,7},{10,... | collective-permute-start | bytes 3145736 | tf_op jit(solution)/shard_map/ppermute | solution.py:280
  122.2 45.6 %collective-permute-start.28 = (bf16[1024,512]{1,0:T(8,128)(2,1)S(1)}, bf16[1024,512]{1,0:T(8,128)(2,1)S(1)}, u32[]{:S(2)}, u32[]{:S(2)}) collective-permute-start(bf16[1024,512]{1,0:T(8,128)(2,1)S(1)} %collective-permute-done.4), channel_id=1, source_target_pairs={{0,2},{1,3},{2,4},{3,5},{4,6},{5,7},{6,8},{7,9},{8,10},{9,11},{10,... | collective-permute-start | bytes 3145736 | tf_op jit(solution)/shard_map/ppermute | solution.py:280
  144.6 44.9 %collective-permute-start.29 = (bf16[1024,512]{1,0:T(8,128)(2,1)S(1)}, bf16[1024,512]{1,0:T(8,128)(2,1)S(1)}, u32[]{:S(2)}, u32[]{:S(2)}) collective-permute-start(bf16[1024,512]{1,0:T(8,128)(2,1)S(1)} %collective-permute-done.12), channel_id=1, source_target_pairs={{0,2},{1,3},{2,4},{3,5},{4,6},{5,7},{6,8},{7,9},{8,10},{9,11},{10,... | collective-permute-start | bytes 3145736 | tf_op jit(solution)/shard_map/ppermute | solution.py:280
  148.0 64.1 %collective-permute-start.30 = (bf16[256,2048]{1,0:T(8,128)(2,1)S(1)}, bf16[256,2048]{1,0:T(8,128)(2,1)S(1)}, u32[]{:S(2)}, u32[]{:S(2)}) collective-permute-start(bf16[256,2048]{1,0:T(8,128)(2,1)S(1)} %collective-permute-done.20), channel_id=1, source_target_pairs={{0,2},{1,3},{2,4},{3,5},{4,6},{5,7},{6,8},{7,9},{8,10},{9,11},{10,... | collective-permute-start | bytes 3145736 | tf_op jit(solution)/shard_map/ppermute | solution.py:280
  148.1 67.3 %collective-permute-start.7 = (bf16[1024,512]{1,0:T(8,128)(2,1)S(1)}, bf16[1024,512]{1,0:T(8,128)(2,1)S(1)}, u32[]{:S(2)}, u32[]{:S(2)}) collective-permute-start(bf16[1024,512]{1,0:T(8,128)(2,1)S(1)} %collective-permute-done.6), channel_id=1, source_target_pairs={{0,14},{1,15},{2,0},{3,1},{4,2},{5,3},{6,4},{7,5},{8,6},{9,7},{10,... | collective-permute-start | bytes 3145736 | tf_op jit(solution)/shard_map/ppermute | solution.py:280
  167.8 47.7 %collective-permute-start.15 = (bf16[1024,512]{1,0:T(8,128)(2,1)S(1)}, bf16[1024,512]{1,0:T(8,128)(2,1)S(1)}, u32[]{:S(2)}, u32[]{:S(2)}) collective-permute-start(bf16[1024,512]{1,0:T(8,128)(2,1)S(1)} %collective-permute-done.14), channel_id=1, source_target_pairs={{0,14},{1,15},{2,0},{3,1},{4,2},{5,3},{6,4},{7,5},{8,6},{9,7},{10,... | collective-permute-start | bytes 3145736 | tf_op jit(solution)/shard_map/ppermute | solution.py:280
  167.9 67.4 %collective-permute-start.23 = (bf16[256,2048]{1,0:T(8,128)(2,1)S(1)}, bf16[256,2048]{1,0:T(8,128)(2,1)S(1)}, u32[]{:S(2)}, u32[]{:S(2)}) collective-permute-start(bf16[256,2048]{1,0:T(8,128)(2,1)S(1)} %collective-permute-done.22), channel_id=1, source_target_pairs={{0,14},{1,15},{2,0},{3,1},{4,2},{5,3},{6,4},{7,5},{8,6},{9,7},{10,... | collective-permute-start | bytes 3145736 | tf_op jit(solution)/shard_map/ppermute | solution.py:280
  189.6 45.7 %collective-permute-start.31 = (bf16[1024,512]{1,0:T(8,128)(2,1)S(1)}, bf16[1024,512]{1,0:T(8,128)(2,1)S(1)}, u32[]{:S(2)}, u32[]{:S(2)}) collective-permute-start(bf16[1024,512]{1,0:T(8,128)(2,1)S(1)} %collective-permute-done.28), channel_id=1, source_target_pairs={{0,2},{1,3},{2,4},{3,5},{4,6},{5,7},{6,8},{7,9},{8,10},{9,11},{10,... | collective-permute-start | bytes 3145736 | tf_op jit(solution)/shard_map/ppermute | solution.py:280
  212.0 44.9 %collective-permute-start.32 = (bf16[1024,512]{1,0:T(8,128)(2,1)S(1)}, bf16[1024,512]{1,0:T(8,128)(2,1)S(1)}, u32[]{:S(2)}, u32[]{:S(2)}) collective-permute-start(bf16[1024,512]{1,0:T(8,128)(2,1)S(1)} %collective-permute-done.29), channel_id=1, source_target_pairs={{0,2},{1,3},{2,4},{3,5},{4,6},{5,7},{6,8},{7,9},{8,10},{9,11},{10,... | collective-permute-start | bytes 3145736 | tf_op jit(solution)/shard_map/ppermute | solution.py:280
  215.4 64.0 %collective-permute-start.33 = (bf16[256,2048]{1,0:T(8,128)(2,1)S(1)}, bf16[256,2048]{1,0:T(8,128)(2,1)S(1)}, u32[]{:S(2)}, u32[]{:S(2)}) collective-permute-start(bf16[256,2048]{1,0:T(8,128)(2,1)S(1)} %collective-permute-done.30), channel_id=1, source_target_pairs={{0,2},{1,3},{2,4},{3,5},{4,6},{5,7},{6,8},{7,9},{8,10},{9,11},{10,... | collective-permute-start | bytes 3145736 | tf_op jit(solution)/shard_map/ppermute | solution.py:280
  215.5 67.3 %collective-permute-start.8 = (bf16[1024,512]{1,0:T(8,128)(2,1)S(1)}, bf16[1024,512]{1,0:T(8,128)(2,1)S(1)}, u32[]{:S(2)}, u32[]{:S(2)}) collective-permute-start(bf16[1024,512]{1,0:T(8,128)(2,1)S(1)} %collective-permute-done.7), channel_id=1, source_target_pairs={{0,14},{1,15},{2,0},{3,1},{4,2},{5,3},{6,4},{7,5},{8,6},{9,7},{10,... | collective-permute-start | bytes 3145736 | tf_op jit(solution)/shard_map/ppermute | solution.py:280
  235.2 47.7 %collective-permute-start.16 = (bf16[1024,512]{1,0:T(8,128)(2,1)S(1)}, bf16[1024,512]{1,0:T(8,128)(2,1)S(1)}, u32[]{:S(2)}, u32[]{:S(2)}) collective-permute-start(bf16[1024,512]{1,0:T(8,128)(2,1)S(1)} %collective-permute-done.15), channel_id=1, source_target_pairs={{0,14},{1,15},{2,0},{3,1},{4,2},{5,3},{6,4},{7,5},{8,6},{9,7},{10,... | collective-permute-start | bytes 3145736 | tf_op jit(solution)/shard_map/ppermute | solution.py:280
  235.3 67.4 %collective-permute-start.24 = (bf16[256,2048]{1,0:T(8,128)(2,1)S(1)}, bf16[256,2048]{1,0:T(8,128)(2,1)S(1)}, u32[]{:S(2)}, u32[]{:S(2)}) collective-permute-start(bf16[256,2048]{1,0:T(8,128)(2,1)S(1)} %collective-permute-done.23), channel_id=1, source_target_pairs={{0,14},{1,15},{2,0},{3,1},{4,2},{5,3},{6,4},{7,5},{8,6},{9,7},{10,... | collective-permute-start | bytes 3145736 | tf_op jit(solution)/shard_map/ppermute | solution.py:280
  257.0 45.7 %collective-permute-start.34 = (bf16[1024,512]{1,0:T(8,128)(2,1)S(1)}, bf16[1024,512]{1,0:T(8,128)(2,1)S(1)}, u32[]{:S(2)}, u32[]{:S(2)}) collective-permute-start(bf16[1024,512]{1,0:T(8,128)(2,1)S(1)} %collective-permute-done.31), channel_id=1, source_target_pairs={{0,2},{1,3},{2,4},{3,5},{4,6},{5,7},{6,8},{7,9},{8,10},{9,11},{10,... | collective-permute-start | bytes 3145736 | tf_op jit(solution)/shard_map/ppermute | solution.py:280
  279.4 44.9 %collective-permute-start.35 = (bf16[1024,512]{1,0:T(8,128)(2,1)S(1)}, bf16[1024,512]{1,0:T(8,128)(2,1)S(1)}, u32[]{:S(2)}, u32[]{:S(2)}) collective-permute-start(bf16[1024,512]{1,0:T(8,128)(2,1)S(1)} %collective-permute-done.32), channel_id=1, source_target_pairs={{0,2},{1,3},{2,4},{3,5},{4,6},{5,7},{6,8},{7,9},{8,10},{9,11},{10,... | collective-permute-start | bytes 3145736 | tf_op jit(solution)/shard_map/ppermute | solution.py:280
  282.8 64.0 %collective-permute-start.36 = (bf16[256,2048]{1,0:T(8,128)(2,1)S(1)}, bf16[256,2048]{1,0:T(8,128)(2,1)S(1)}, u32[]{:S(2)}, u32[]{:S(2)}) collective-permute-start(bf16[256,2048]{1,0:T(8,128)(2,1)S(1)} %collective-permute-done.33), channel_id=1, source_target_pairs={{0,2},{1,3},{2,4},{3,5},{4,6},{5,7},{6,8},{7,9},{8,10},{9,11},{10,... | collective-permute-start | bytes 3145736 | tf_op jit(solution)/shard_map/ppermute | solution.py:280
  282.9 67.7 %collective-permute-start.9 = (bf16[1024,512]{1,0:T(8,128)(2,1)S(1)}, bf16[1024,512]{1,0:T(8,128)(2,1)S(1)}, u32[]{:S(2)}, u32[]{:S(2)}) collective-permute-start(bf16[1024,512]{1,0:T(8,128)(2,1)S(1)} %collective-permute-done.8), channel_id=1, source_target_pairs={{0,14},{1,15},{2,0},{3,1},{4,2},{5,3},{6,4},{7,5},{8,6},{9,7},{10,... | collective-permute-start | bytes 3145736 | tf_op jit(solution)/shard_map/ppermute | solution.py:280
  302.7 48.1 %collective-permute-start.17 = (bf16[1024,512]{1,0:T(8,128)(2,1)S(1)}, bf16[1024,512]{1,0:T(8,128)(2,1)S(1)}, u32[]{:S(2)}, u32[]{:S(2)}) collective-permute-start(bf16[1024,512]{1,0:T(8,128)(2,1)S(1)} %collective-permute-done.16), channel_id=1, source_target_pairs={{0,14},{1,15},{2,0},{3,1},{4,2},{5,3},{6,4},{7,5},{8,6},{9,7},{10,... | collective-permute-start | bytes 3145736 | tf_op jit(solution)/shard_map/ppermute | solution.py:280
  302.7 67.5 %collective-permute-start.25 = (bf16[256,2048]{1,0:T(8,128)(2,1)S(1)}, bf16[256,2048]{1,0:T(8,128)(2,1)}, u32[]{:S(2)}, u32[]{:S(2)}) collective-permute-start(bf16[256,2048]{1,0:T(8,128)(2,1)S(1)} %collective-permute-done.24), channel_id=1, source_target_pairs={{0,14},{1,15},{2,0},{3,1},{4,2},{5,3},{6,4},{7,5},{8,6},{9,7},{10,... | collective-permute-start | bytes 3145736 | tf_op jit(solution)/shard_map/ppermute | solution.py:280
  324.4 45.8 %collective-permute-start.37 = (bf16[1024,512]{1,0:T(8,128)(2,1)S(1)}, bf16[1024,512]{1,0:T(8,128)(2,1)}, u32[]{:S(2)}, u32[]{:S(2)}) collective-permute-start(bf16[1024,512]{1,0:T(8,128)(2,1)S(1)} %collective-permute-done.34), channel_id=1, source_target_pairs={{0,2},{1,3},{2,4},{3,5},{4,6},{5,7},{6,8},{7,9},{8,10},{9,11},{10,... | collective-permute-start | bytes 3145736 | tf_op jit(solution)/shard_map/ppermute | solution.py:280
  346.9 45.0 %collective-permute-start.38 = (bf16[1024,512]{1,0:T(8,128)(2,1)S(1)}, bf16[1024,512]{1,0:T(8,128)(2,1)}, u32[]{:S(2)}, u32[]{:S(2)}) collective-permute-start(bf16[1024,512]{1,0:T(8,128)(2,1)S(1)} %collective-permute-done.35), channel_id=1, source_target_pairs={{0,2},{1,3},{2,4},{3,5},{4,6},{5,7},{6,8},{7,9},{8,10},{9,11},{10,... | collective-permute-start | bytes 3145736 | tf_op jit(solution)/shard_map/ppermute | solution.py:280
  350.6 63.8 %collective-permute-start.39 = (bf16[256,2048]{1,0:T(8,128)(2,1)S(1)}, bf16[256,2048]{1,0:T(8,128)(2,1)}, u32[]{:S(2)}, u32[]{:S(2)}) collective-permute-start(bf16[256,2048]{1,0:T(8,128)(2,1)S(1)} %collective-permute-done.36), channel_id=1, source_target_pairs={{0,2},{1,3},{2,4},{3,5},{4,6},{5,7},{6,8},{7,9},{8,10},{9,11},{10,... | collective-permute-start | bytes 3145736 | tf_op jit(solution)/shard_map/ppermute | solution.py:280
  350.7 67.0 %collective-permute-start.10 = (bf16[1024,512]{1,0:T(8,128)(2,1)S(1)}, bf16[1024,512]{1,0:T(8,128)(2,1)}, u32[]{:S(2)}, u32[]{:S(2)}) collective-permute-start(bf16[1024,512]{1,0:T(8,128)(2,1)S(1)} %collective-permute-done.9), channel_id=1, source_target_pairs={{0,14},{1,15},{2,0},{3,1},{4,2},{5,3},{6,4},{7,5},{8,6},{9,7},{10,... | collective-permute-start | bytes 3145736 | tf_op jit(solution)/shard_map/ppermute | solution.py:280
  370.2 47.7 %collective-permute-start.18 = (bf16[1024,512]{1,0:T(8,128)(2,1)S(1)}, bf16[1024,512]{1,0:T(8,128)(2,1)S(1)}, u32[]{:S(2)}, u32[]{:S(2)}) collective-permute-start(bf16[1024,512]{1,0:T(8,128)(2,1)S(1)} %collective-permute-done.17), channel_id=1, source_target_pairs={{0,14},{1,15},{2,0},{3,1},{4,2},{5,3},{6,4},{7,5},{8,6},{9,7},{10,... | collective-permute-start | bytes 3145736 | tf_op jit(solution)/shard_map/ppermute | solution.py:280
  370.2 67.4 %collective-permute-start.26 = (bf16[256,2048]{1,0:T(8,128)(2,1)}, bf16[256,2048]{1,0:T(8,128)(2,1)}, u32[]{:S(2)}, u32[]{:S(2)}) collective-permute-start(bf16[256,2048]{1,0:T(8,128)(2,1)} %collective-permute-done.25), channel_id=1, source_target_pairs={{0,14},{1,15},{2,0},{3,1},{4,2},{5,3},{6,4},{7,5},{8,6},{9,7},{10,... | collective-permute-start | bytes 3145736 | tf_op jit(solution)/shard_map/ppermute | solution.py:280
  391.9 45.7 %collective-permute-start.40 = (bf16[1024,512]{1,0:T(8,128)(2,1)}, bf16[1024,512]{1,0:T(8,128)(2,1)}, u32[]{:S(2)}, u32[]{:S(2)}) collective-permute-start(bf16[1024,512]{1,0:T(8,128)(2,1)} %collective-permute-done.37), channel_id=1, source_target_pairs={{0,2},{1,3},{2,4},{3,5},{4,6},{5,7},{6,8},{7,9},{8,10},{9,11},{10,... | collective-permute-start | bytes 3145736 | tf_op jit(solution)/shard_map/ppermute | solution.py:280
  414.4 44.9 %collective-permute-start.41 = (bf16[1024,512]{1,0:T(8,128)(2,1)}, bf16[1024,512]{1,0:T(8,128)(2,1)}, u32[]{:S(2)}, u32[]{:S(2)}) collective-permute-start(bf16[1024,512]{1,0:T(8,128)(2,1)} %collective-permute-done.38), channel_id=1, source_target_pairs={{0,2},{1,3},{2,4},{3,5},{4,6},{5,7},{6,8},{7,9},{8,10},{9,11},{10,... | collective-permute-start | bytes 3145736 | tf_op jit(solution)/shard_map/ppermute | solution.py:280
  417.7 64.0 %collective-permute-start.42 = (bf16[256,2048]{1,0:T(8,128)(2,1)}, bf16[256,2048]{1,0:T(8,128)(2,1)}, u32[]{:S(2)}, u32[]{:S(2)}) collective-permute-start(bf16[256,2048]{1,0:T(8,128)(2,1)} %collective-permute-done.39), channel_id=1, source_target_pairs={{0,2},{1,3},{2,4},{3,5},{4,6},{5,7},{6,8},{7,9},{8,10},{9,11},{10,... | collective-permute-start | bytes 3145736 | tf_op jit(solution)/shard_map/ppermute | solution.py:280
  418.9 66.2 %collective-permute-start.11 = (bf16[1024,512]{1,0:T(8,128)(2,1)}, bf16[1024,512]{1,0:T(8,128)(2,1)}, u32[]{:S(2)}, u32[]{:S(2)}) collective-permute-start(bf16[1024,512]{1,0:T(8,128)(2,1)} %collective-permute-done.10), channel_id=1, source_target_pairs={{0,14},{1,15},{2,0},{3,1},{4,2},{5,3},{6,4},{7,5},{8,6},{9,7},{10,... | collective-permute-start | bytes 3145736 | tf_op jit(solution)/shard_map/ppermute | solution.py:280
  437.6 51.7 %collective-permute-start.19 = (bf16[1024,512]{1,0:T(8,128)(2,1)}, bf16[1024,512]{1,0:T(8,128)(2,1)}, u32[]{:S(2)}, u32[]{:S(2)}) collective-permute-start(bf16[1024,512]{1,0:T(8,128)(2,1)} %copy-done.33), channel_id=1, source_target_pairs={{0,14},{1,15},{2,0},{3,1},{4,2},{5,3},{6,4},{7,5},{8,6},{9,7},{10,... | collective-permute-start | bytes 3145736 | tf_op jit(solution)/shard_map/ppermute | solution.py:280
  437.6 67.4 %collective-permute-start.27 = (bf16[256,2048]{1,0:T(8,128)(2,1)}, bf16[256,2048]{1,0:T(8,128)(2,1)}, u32[]{:S(2)}, u32[]{:S(2)}) collective-permute-start(bf16[256,2048]{1,0:T(8,128)(2,1)} %collective-permute-done.26), channel_id=1, source_target_pairs={{0,14},{1,15},{2,0},{3,1},{4,2},{5,3},{6,4},{7,5},{8,6},{9,7},{10,... | collective-permute-start | bytes 3145736 | tf_op jit(solution)/shard_map/ppermute | solution.py:280
  459.3 45.7 %collective-permute-start.43 = (bf16[1024,512]{1,0:T(8,128)(2,1)}, bf16[1024,512]{1,0:T(8,128)(2,1)}, u32[]{:S(2)}, u32[]{:S(2)}) collective-permute-start(bf16[1024,512]{1,0:T(8,128)(2,1)} %collective-permute-done.40), channel_id=1, source_target_pairs={{0,2},{1,3},{2,4},{3,5},{4,6},{5,7},{6,8},{7,9},{8,10},{9,11},{10,... | collective-permute-start | bytes 3145736 | tf_op jit(solution)/shard_map/ppermute | solution.py:280
  481.8 44.9 %collective-permute-start.44 = (bf16[1024,512]{1,0:T(8,128)(2,1)}, bf16[1024,512]{1,0:T(8,128)(2,1)}, u32[]{:S(2)}, u32[]{:S(2)}) collective-permute-start(bf16[1024,512]{1,0:T(8,128)(2,1)} %collective-permute-done.41), channel_id=1, source_target_pairs={{0,2},{1,3},{2,4},{3,5},{4,6},{5,7},{6,8},{7,9},{8,10},{9,11},{10,... | collective-permute-start | bytes 3145736 | tf_op jit(solution)/shard_map/ppermute | solution.py:280
  485.1 64.1 %collective-permute-start.45 = (bf16[256,2048]{1,0:T(8,128)(2,1)}, bf16[256,2048]{1,0:T(8,128)(2,1)}, u32[]{:S(2)}, u32[]{:S(2)}) collective-permute-start(bf16[256,2048]{1,0:T(8,128)(2,1)} %collective-permute-done.42), channel_id=1, source_target_pairs={{0,2},{1,3},{2,4},{3,5},{4,6},{5,7},{6,8},{7,9},{8,10},{9,11},{10,... | collective-permute-start | bytes 3145736 | tf_op jit(solution)/shard_map/ppermute | solution.py:280
  625.2 33.2 %collective-permute-start = (bf16[64,2048]{1,0:T(8,128)(2,1)S(1)}, bf16[64,2048]{1,0:T(8,128)(2,1)S(1)}, u32[]{:S(2)}, u32[]{:S(2)}) collective-permute-start(bf16[64,2048]{1,0:T(8,128)(2,1)S(1)} %get-tuple-element.1964), channel_id=1, source_target_pairs={{0,16},{8,24},{16,32},{24,40},{32,48},{40,56},{48,64},{56,72},{64,... | collective-permute-start | bytes 786440 | tf_op jit(solution)/shard_map/while/body/eval_jaxpr/ppermute | solution.py:332
  896.3 54.8 %collective-permute-start = (bf16[64,2048]{1,0:T(8,128)(2,1)S(1)}, bf16[64,2048]{1,0:T(8,128)(2,1)S(1)}, u32[]{:S(2)}, u32[]{:S(2)}) collective-permute-start(bf16[64,2048]{1,0:T(8,128)(2,1)S(1)} %get-tuple-element.1964), channel_id=1, source_target_pairs={{0,16},{8,24},{16,32},{24,40},{32,48},{40,56},{48,64},{56,72},{64,... | collective-permute-start | bytes 786440 | tf_op jit(solution)/shard_map/while/body/eval_jaxpr/ppermute | solution.py:332
  971.2 33.9 %collective-permute-start = (bf16[64,2048]{1,0:T(8,128)(2,1)S(1)}, bf16[64,2048]{1,0:T(8,128)(2,1)S(1)}, u32[]{:S(2)}, u32[]{:S(2)}) collective-permute-start(bf16[64,2048]{1,0:T(8,128)(2,1)S(1)} %get-tuple-element.1964), channel_id=1, source_target_pairs={{0,16},{8,24},{16,32},{24,40},{32,48},{40,56},{48,64},{56,72},{64,... | collective-permute-start | bytes 786440 | tf_op jit(solution)/shard_map/while/body/eval_jaxpr/ppermute | solution.py:332
  (191 other events, 3614.1 us)

commit v4 on v3

--- a/solution.py
+++ b/solution.py
@@ -11,7 +11,7 @@
 both = ("section", "expert")
 z_size = 8
 source_count = 3 + (z_size - 1) * 6
-early = 3
+early = 2
 ready_count = 3 if early else 0
 lanes = 128
 
@@ -195,12 +195,12 @@
         + tuple(like(array.shape, array.dtype) for array in stored),
         in_specs=[pl.BlockSpec(memory_space=pltpu.SMEM)]
         + in_hbm(len(sources))
-        + [pl.BlockSpec(memory_space=pl.ANY)] * 2
+        + vmem(2)
         + in_hbm(2),
         out_specs=tuple(vmem(len(shapes)) + in_hbm(2)),
         scratch_shapes=[copy_sems(held), copy_sems(early), pltpu.SemaphoreType.DMA((2,))],
         input_output_aliases={source_count + 3 + i: len(shapes) + i for i in range(2)},
-        compiler_params=pltpu.CompilerParams(vmem_limit_bytes=1 << 20),
+        compiler_params=pltpu.CompilerParams(vmem_limit_bytes=3 << 20),
         cost_estimate=pl.CostEstimate(
             flops=0, bytes_accessed=6 * (held + early) * width * units, transcendentals=0
         ),
@@ -276,9 +276,11 @@
     slots = [[None] * len(pieces) for _ in range(z_size)]
     travelling = list(pieces)
     for step in range(1, z_size):
-        for m in range(len(pieces)):
-            travelling[m] = lax.ppermute(travelling[m], both, forward if m % 2 == 0 else backward)
-            slots[step if m % 2 == 0 else z_size - step][m] = travelling[m]
+        for m in range(0, len(pieces), 2):
+            pair = lax.optimization_barrier((travelling[m], travelling[m + 1]))
+            travelling[m] = lax.ppermute(pair[0], both, forward)
+            travelling[m + 1] = lax.ppermute(pair[1], both, backward)
+            slots[step][m], slots[z_size - step][m + 1] = travelling[m], travelling[m + 1]
     return [piece for slot in slots[1:] for piece in slot]
 
 
@@ -312,13 +314,14 @@
         ]
         return jnp.concatenate([b.reshape(row_count, -1) for b in blocks], axis=0)
 
-    ids = [rows_of(layer) for layer in both_layers(expert_ids[0])]
-    scales = both_layers(norm_gain)
-    routers = [
-        jnp.pad(layer, ((0, 0), (0, lanes - layer.shape[1]))) for layer in both_layers(router[0])
-    ]
     matrices = [w_gate[0, 0], w_up[0, 0], w_down[0, 0]]
     sources = matrices + gather_ring([half for matrix in matrices for half in halves(matrix)], rings)
+    small = lax.optimization_barrier((expert_ids[0], norm_gain, router[0], sources[3 + 6]))
+    ids = [rows_of(layer) for layer in both_layers(small[0])]
+    scales = both_layers(small[1])
+    routers = [
+        jnp.pad(layer, ((0, 0), (0, lanes - layer.shape[1]))) for layer in both_layers(small[2])
+    ]
     entering = lax.dynamic_slice_in_dim(tokens_in, upper * own_micros, own_micros, 0)
     entering = entering.reshape(row_count, width)
 

time: 1050 us -> 989 us (0.942)
  the two profiles are of different devices: /device:TPU:119 before, /device:TPU:31 now
where the time goes in v4:
time: 989 us; the launch traced here: 979 us
  waiting for transfers between devices  606 us (61%)
  starting transfers between devices  230 us (23%)
  Pallas kernels  119 us (12%)
  local copies, waits for them, and re-layouts  15.5 us (2%)
    ppermute x21, waiting for transfers between devices, gather_ring(): travelling[m] = lax.ppermute(pair[0], both, forward)  349 us
    ppermute x16, waiting for transfers between devices, ring_step(): mine = lax.ppermute(sent, 'section', next_ring)  117 us
    ppermute x16, starting transfers between devices, ring_step(): mine = lax.ppermute(sent, 'section', next_ring)  99.7 us
    ppermute x48, waiting for transfers between devices, exchange(): return lax.ppermute(value, 'expert', other_core)  61.8 us
    ppermute x21, starting transfers between devices, gather_ring(): travelling[m + 1] = lax.ppermute(pair[1], both, backward)  42.7 us
    pallas_call x16, Pallas kernels, load_ahead(): pl.pallas_call(load_kernel, out_shape=tuple((pltpu.VMEM(shape, jnp.bfloat...  37.1 us
    ppermute x48, starting transfers between devices, exchange(): return lax.ppermute(value, 'expert', other_core)  37 us
    ppermute x21, waiting for transfers between devices, gather_ring(): travelling[m + 1] = lax.ppermute(pair[1], both, backward)  33.7 us
  transfers between devices with their start and end apart: 110, of which 88 were waited for; matrix products, arithmetic and copies ran while one was open for 1% of the time, Pallas kernels for 4%

profile of v4, /device:TPU:31, one launch (start us, length us, event | category | flops | bytes accessed | tf_op | source)
XLA Modules:
  0.0 978.5 jit_solution(18098283345859504417)
XLA Ops:
  3.6 4.0 collective-permute-start.31
  10.8 19.7 %collective-permute-done.30 = bf16[256,2048]{1,0:T(8,128)(2,1)S(1)} collective-permute-done((bf16[256,2048]{1,0:T(8,128)(2,1)S(1)}, bf16[256,2048]{1,0:T(8,128)(2,1)S(1)}, u32[]{:S(2)}, u32[]{:S(2)}) %collective-permute-start.30) | collective-permute-done | bytes 1048608 | tf_op jit(solution)/shard_map/ppermute | solution.py:281
  32.0 20.9 %collective-permute-done.17 = bf16[1024,512]{1,0:T(8,128)(2,1)S(1)} collective-permute-done((bf16[1024,512]{1,0:T(8,128)(2,1)S(1)}, bf16[1024,512]{1,0:T(8,128)(2,1)S(1)}, u32[]{:S(2)}, u32[]{:S(2)}) %collective-permute-start.17) | collective-permute-done | bytes 1048608 | tf_op jit(solution)/shard_map/ppermute | solution.py:281
  54.4 21.0 %collective-permute-done.4 = bf16[1024,512]{1,0:T(8,128)(2,1)S(1)} collective-permute-done((bf16[1024,512]{1,0:T(8,128)(2,1)S(1)}, bf16[1024,512]{1,0:T(8,128)(2,1)S(1)}, u32[]{:S(2)}, u32[]{:S(2)}) %collective-permute-start.4) | collective-permute-done | bytes 1048608 | tf_op jit(solution)/shard_map/ppermute | solution.py:281
  76.8 21.0 %collective-permute-done.32 = bf16[256,2048]{1,0:T(8,128)(2,1)S(1)} collective-permute-done((bf16[256,2048]{1,0:T(8,128)(2,1)S(1)}, bf16[256,2048]{1,0:T(8,128)(2,1)S(1)}, u32[]{:S(2)}, u32[]{:S(2)}) %collective-permute-start.32) | collective-permute-done | bytes 1048608 | tf_op jit(solution)/shard_map/ppermute | solution.py:281
  99.4 20.9 %collective-permute-done.19 = bf16[1024,512]{1,0:T(8,128)(2,1)S(1)} collective-permute-done((bf16[1024,512]{1,0:T(8,128)(2,1)S(1)}, bf16[1024,512]{1,0:T(8,128)(2,1)S(1)}, u32[]{:S(2)}, u32[]{:S(2)}) %collective-permute-start.19) | collective-permute-done | bytes 1048608 | tf_op jit(solution)/shard_map/ppermute | solution.py:281
  121.9 20.9 %collective-permute-done.6 = bf16[1024,512]{1,0:T(8,128)(2,1)S(1)} collective-permute-done((bf16[1024,512]{1,0:T(8,128)(2,1)S(1)}, bf16[1024,512]{1,0:T(8,128)(2,1)S(1)}, u32[]{:S(2)}, u32[]{:S(2)}) %collective-permute-start.6) | collective-permute-done | bytes 1048608 | tf_op jit(solution)/shard_map/ppermute | solution.py:281
  144.5 20.7 %collective-permute-done.34 = bf16[256,2048]{1,0:T(8,128)(2,1)S(1)} collective-permute-done((bf16[256,2048]{1,0:T(8,128)(2,1)S(1)}, bf16[256,2048]{1,0:T(8,128)(2,1)S(1)}, u32[]{:S(2)}, u32[]{:S(2)}) %collective-permute-start.34) | collective-permute-done | bytes 1048608 | tf_op jit(solution)/shard_map/ppermute | solution.py:281
  166.8 20.9 %collective-permute-done.21 = bf16[1024,512]{1,0:T(8,128)(2,1)S(1)} collective-permute-done((bf16[1024,512]{1,0:T(8,128)(2,1)S(1)}, bf16[1024,512]{1,0:T(8,128)(2,1)S(1)}, u32[]{:S(2)}, u32[]{:S(2)}) %collective-permute-start.21) | collective-permute-done | bytes 1048608 | tf_op jit(solution)/shard_map/ppermute | solution.py:281
  189.3 20.9 %collective-permute-done.8 = bf16[1024,512]{1,0:T(8,128)(2,1)S(1)} collective-permute-done((bf16[1024,512]{1,0:T(8,128)(2,1)S(1)}, bf16[1024,512]{1,0:T(8,128)(2,1)S(1)}, u32[]{:S(2)}, u32[]{:S(2)}) %collective-permute-start.8) | collective-permute-done | bytes 1048608 | tf_op jit(solution)/shard_map/ppermute | solution.py:281
  211.7 20.9 %collective-permute-done.36 = bf16[256,2048]{1,0:T(8,128)(2,1)S(1)} collective-permute-done((bf16[256,2048]{1,0:T(8,128)(2,1)S(1)}, bf16[256,2048]{1,0:T(8,128)(2,1)S(1)}, u32[]{:S(2)}, u32[]{:S(2)}) %collective-permute-start.36) | collective-permute-done | bytes 1048608 | tf_op jit(solution)/shard_map/ppermute | solution.py:281
  234.2 20.9 %collective-permute-done.23 = bf16[1024,512]{1,0:T(8,128)(2,1)S(1)} collective-permute-done((bf16[1024,512]{1,0:T(8,128)(2,1)S(1)}, bf16[1024,512]{1,0:T(8,128)(2,1)S(1)}, u32[]{:S(2)}, u32[]{:S(2)}) %collective-permute-start.23) | collective-permute-done | bytes 1048608 | tf_op jit(solution)/shard_map/ppermute | solution.py:281
  256.7 20.9 %collective-permute-done.10 = bf16[1024,512]{1,0:T(8,128)(2,1)S(1)} collective-permute-done((bf16[1024,512]{1,0:T(8,128)(2,1)S(1)}, bf16[1024,512]{1,0:T(8,128)(2,1)S(1)}, u32[]{:S(2)}, u32[]{:S(2)}) %collective-permute-start.10) | collective-permute-done | bytes 1048608 | tf_op jit(solution)/shard_map/ppermute | solution.py:281
  279.1 21.1 %collective-permute-done.38 = bf16[256,2048]{1,0:T(8,128)(2,1)} collective-permute-done((bf16[256,2048]{1,0:T(8,128)(2,1)S(1)}, bf16[256,2048]{1,0:T(8,128)(2,1)}, u32[]{:S(2)}, u32[]{:S(2)}) %collective-permute-start.38) | collective-permute-done | bytes 1048608 | tf_op jit(solution)/shard_map/ppermute | solution.py:281
  301.7 21.0 %collective-permute-done.25 = bf16[1024,512]{1,0:T(8,128)(2,1)} collective-permute-done((bf16[1024,512]{1,0:T(8,128)(2,1)S(1)}, bf16[1024,512]{1,0:T(8,128)(2,1)}, u32[]{:S(2)}, u32[]{:S(2)}) %collective-permute-start.25) | collective-permute-done | bytes 1048608 | tf_op jit(solution)/shard_map/ppermute | solution.py:281
  324.5 20.5 %collective-permute-done.12 = bf16[1024,512]{1,0:T(8,128)(2,1)S(1)} collective-permute-done((bf16[1024,512]{1,0:T(8,128)(2,1)S(1)}, bf16[1024,512]{1,0:T(8,128)(2,1)S(1)}, u32[]{:S(2)}, u32[]{:S(2)}) %collective-permute-start.12) | collective-permute-done | bytes 1048608 | tf_op jit(solution)/shard_map/ppermute | solution.py:281
  350.1 17.5 %collective-permute-done.40 = bf16[256,2048]{1,0:T(8,128)(2,1)} collective-permute-done((bf16[256,2048]{1,0:T(8,128)(2,1)}, bf16[256,2048]{1,0:T(8,128)(2,1)}, u32[]{:S(2)}, u32[]{:S(2)}) %collective-permute-start.40) | collective-permute-done | bytes 1048608 | tf_op jit(solution)/shard_map/ppermute | solution.py:281
  370.3 21.5 %collective-permute-done.47 = s32[8,128,2]{1,2,0:T(2,128)S(1)} collective-permute-done((s32[8,128,2]{1,2,0:T(2,128)S(1)}, s32[8,128,2]{1,2,0:T(2,128)S(1)}, u32[]{:S(2)}, u32[]{:S(2)}) %collective-permute-start.47) | collective-permute-done | bytes 8224 | tf_op jit(solution)/shard_map/ppermute | solution.py:306
  399.5 13.4 %collective-permute-done.14 = bf16[1024,512]{1,0:T(8,128)(2,1)} collective-permute-done((bf16[1024,512]{1,0:T(8,128)(2,1)}, bf16[1024,512]{1,0:T(8,128)(2,1)}, u32[]{:S(2)}, u32[]{:S(2)}) %collective-permute-start.14) | collective-permute-done | bytes 1048608 | tf_op jit(solution)/shard_map/ppermute | solution.py:281
  415.6 11.4 %collective-permute-done.46 = f32[1,2048]{1,0:T(1,128)S(1)} collective-permute-done((f32[1,2048]{1,0:T(1,128)S(1)}, f32[1,2048]{1,0:T(1,128)S(1)}, u32[]{:S(2)}, u32[]{:S(2)}) %collective-permute-start.46) | collective-permute-done | bytes 8224 | tf_op jit(solution)/shard_map/ppermute | solution.py:306
  427.0 23.8 %collective-permute-start.44 = (bf16[1024,512]{1,0:T(8,128)(2,1)}, bf16[1024,512]{1,0:T(8,128)(2,1)}, u32[]{:S(2)}, u32[]{:S(2)}) collective-permute-start(bf16[1024,512]{1,0:T(8,128)(2,1)} %collective-permute-done.27), channel_id=1, source_target_pairs={{0,2},{1,3},{2,4},{3,5},{4,6},{5,7},{6,8},{7,9},{8,10},{9,11},{10,... | collective-permute-start | bytes 3145736 | tf_op jit(solution)/shard_map/ppermute | solution.py:281
  450.7 10.9 %collective-permute-start.16 = (bf16[1024,512]{1,0:T(8,128)(2,1)}, bf16[1024,512]{1,0:T(8,128)(2,1)}, u32[]{:S(2)}, u32[]{:S(2)}) collective-permute-start(bf16[1024,512]{1,0:T(8,128)(2,1)} %collective-permute-done.15), channel_id=1, source_target_pairs={{0,14},{1,15},{2,0},{3,1},{4,2},{5,3},{6,4},{7,5},{8,6},{9,7},{10,... | collective-permute-start | bytes 3145736 | tf_op jit(solution)/shard_map/ppermute | solution.py:282
  465.6 14.1 %collective-permute-done.29 = bf16[1024,512]{1,0:T(8,128)(2,1)} collective-permute-done((bf16[1024,512]{1,0:T(8,128)(2,1)}, bf16[1024,512]{1,0:T(8,128)(2,1)}, u32[]{:S(2)}, u32[]{:S(2)}) %collective-permute-start.29) | collective-permute-done | bytes 1048608 | tf_op jit(solution)/shard_map/ppermute | solution.py:282
  482.6 19.6 %collective-permute-done.16 = bf16[1024,512]{1,0:T(8,128)(2,1)} collective-permute-done((bf16[1024,512]{1,0:T(8,128)(2,1)}, bf16[1024,512]{1,0:T(8,128)(2,1)}, u32[]{:S(2)}, u32[]{:S(2)}) %collective-permute-start.16) | collective-permute-done | bytes 1048608 | tf_op jit(solution)/shard_map/ppermute | solution.py:282
  508.4 442.7 %while.23 = (s32[]{:T(128)}, bf16[64,2048]{1,0:T(8,128)(2,1)S(1)}, f32[64,2048]{1,0:T(8,128)}, f32[64,2048]{1,0:T(8,128)}, f32[64,2048]{1,0:T(8,128)}, /*index=5...) while((s32[]{:T(128)}, bf16[64,2048]{1,0:T(8,128)(2,1)S(1)}, ...), condition=%wide.region_1.2_spmd, body=%wide.region_0.1_spmd.sunk | while | flops 19 | bytes 78644152 | solution.py:349
  513.9 4.5 collective-permute-start.1
  528.1 17.4 %collective-permute-start = (bf16[64,2048]{1,0:T(8,128)(2,1)S(1)}, bf16[64,2048]{1,0:T(8,128)(2,1)S(1)}, u32[]{:S(2)}, u32[]{:S(2)}) collective-permute-start(bf16[64,2048]{1,0:T(8,128)(2,1)S(1)} %get-tuple-element.2056), channel_id=1, source_target_pairs={{0,16},{8,24},{16,32},{24,40},{32,48},{40,56},{48,64},{56,72},{64,... | collective-permute-start | bytes 786440 | tf_op jit(solution)/shard_map/while/body/eval_jaxpr/ppermute | solution.py:335
  547.3 3.6 collective-permute-done.mine_ref
  561.9 5.5 collective-permute-start
  583.7 5.9 collective-permute-start
  605.9 5.5 collective-permute-start
  627.7 5.9 collective-permute-start
  649.9 5.5 collective-permute-start
  671.7 5.9 collective-permute-start
  693.9 5.5 collective-permute-start
  715.7 8.0 collective-permute-start
  740.0 5.5 collective-permute-start
  761.8 5.9 collective-permute-start
  784.0 5.5 collective-permute-start
  805.8 5.9 collective-permute-start
  828.0 5.5 collective-permute-start
  849.8 5.9 collective-permute-start
  855.8 13.0 %eval_jaxpr.32 = (bf16[4,2048,512]{2,1,0:T(8,128)(2,1)S(1)}, bf16[4,2048,512]{2,1,0:T(8,128)(2,1)S(1)}, bf16[4,512,2048]{2,1,0:T(8,128)(2,1)S(1)}, bf16[2,2048,5...) custom-call(s32[4]{0:T(128)S(1)} %pad_add_fusion.4.place_ref, ...), custom_call_target="tpu_custom_call", output_to_operand_aliasing={{6}: (48, {}), {7}: (49, {})} | custom-call | bytes 37748736 | tf_op jit(solution)/shard_map/while/body/eval_jaxpr/pallas_call | solution.py:192
  868.8 62.5 %collective-permute-done.mine_ref = bf16[64,2048]{1,0:T(8,128)(2,1)S(1)} collective-permute-done((bf16[64,2048]{1,0:T(8,128)(2,1)S(1)}, bf16[64,2048]{1,0:T(8,128)(2,1)S(1)}, u32[]{:S(2)}, u32[]{:S(2)}) %collective-permute-start) | collective-permute-done | bytes 262176 | tf_op jit(solution)/shard_map/while/body/eval_jaxpr/ppermute | solution.py:335
  933.3 5.5 eval_jaxpr.33
  940.9 6.7 eval_jaxpr.34
  952.6 12.4 %collective-permute-start.49 = (bf16[64,2048]{1,0:T(8,128)(2,1)S(1)}, bf16[64,2048]{1,0:T(8,128)(2,1)S(1)}, u32[]{:S(2)}, u32[]{:S(2)}) collective-permute-start(bf16[64,2048]{1,0:T(8,128)(2,1)S(1)} %get-tuple-element.1559), channel_id=1, source_target_pairs={{0,8},{8,0},{16,24},{24,16},{32,40},{40,32},{48,56},{56,48},{64,72... | collective-permute-start | bytes 786440 | tf_op jit(solution)/shard_map/ppermute | solution.py:355
  964.9 12.2 %collective-permute-done.49 = bf16[64,2048]{1,0:T(8,128)(2,1)S(1)} collective-permute-done((bf16[64,2048]{1,0:T(8,128)(2,1)S(1)}, bf16[64,2048]{1,0:T(8,128)(2,1)S(1)}, u32[]{:S(2)}, u32[]{:S(2)}) %collective-permute-start.49) | collective-permute-done | bytes 262176 | tf_op jit(solution)/shard_map/ppermute | solution.py:355
  (573 shorter events, 308.5 us)
Async XLA Ops:
  1.9 28.5 %collective-permute-start.30 = (bf16[256,2048]{1,0:T(8,128)(2,1)S(1)}, bf16[256,2048]{1,0:T(8,128)(2,1)S(1)}, u32[]{:S(2)}, u32[]{:S(2)}) collective-permute-start(bf16[256,2048]{1,0:T(8,128)(2,1)S(1)} %get-tuple-element.1356), channel_id=1, source_target_pairs={{0,2},{1,3},{2,4},{3,5},{4,6},{5,7},{6,8},{7,9},{8,10},{9,11},{10,... | collective-permute-start | bytes 3145736 | tf_op jit(solution)/shard_map/ppermute | solution.py:281
  3.6 28.0 %collective-permute-start.31 = (bf16[256,2048]{1,0:T(8,128)(2,1)S(1)}, bf16[256,2048]{1,0:T(8,128)(2,1)S(1)}, u32[]{:S(2)}, u32[]{:S(2)}) collective-permute-start(bf16[256,2048]{1,0:T(8,128)(2,1)S(1)} %get-tuple-element.1357), channel_id=1, source_target_pairs={{0,14},{1,15},{2,0},{3,1},{4,2},{5,3},{6,4},{7,5},{8,6},{9,7},{10,... | collective-permute-start | bytes 3145736 | tf_op jit(solution)/shard_map/ppermute | solution.py:282
  7.8 45.1 %collective-permute-start.17 = (bf16[1024,512]{1,0:T(8,128)(2,1)S(1)}, bf16[1024,512]{1,0:T(8,128)(2,1)S(1)}, u32[]{:S(2)}, u32[]{:S(2)}) collective-permute-start(bf16[1024,512]{1,0:T(8,128)(2,1)S(1)} %get-tuple-element.1343), channel_id=1, source_target_pairs={{0,2},{1,3},{2,4},{3,5},{4,6},{5,7},{6,8},{7,9},{8,10},{9,11},{10,... | collective-permute-start | bytes 3145736 | tf_op jit(solution)/shard_map/ppermute | solution.py:281
  7.9 46.2 %collective-permute-start.18 = (bf16[1024,512]{1,0:T(8,128)(2,1)S(1)}, bf16[1024,512]{1,0:T(8,128)(2,1)S(1)}, u32[]{:S(2)}, u32[]{:S(2)}) collective-permute-start(bf16[1024,512]{1,0:T(8,128)(2,1)S(1)} %get-tuple-element.1344), channel_id=1, source_target_pairs={{0,14},{1,15},{2,0},{3,1},{4,2},{5,3},{6,4},{7,5},{8,6},{9,7},{10,... | collective-permute-start | bytes 3145736 | tf_op jit(solution)/shard_map/ppermute | solution.py:282
  10.7 64.7 %collective-permute-start.4 = (bf16[1024,512]{1,0:T(8,128)(2,1)S(1)}, bf16[1024,512]{1,0:T(8,128)(2,1)S(1)}, u32[]{:S(2)}, u32[]{:S(2)}) collective-permute-start(bf16[1024,512]{1,0:T(8,128)(2,1)S(1)} %get-tuple-element.1330), channel_id=1, source_target_pairs={{0,2},{1,3},{2,4},{3,5},{4,6},{5,7},{6,8},{7,9},{8,10},{9,11},{10,... | collective-permute-start | bytes 3145736 | tf_op jit(solution)/shard_map/ppermute | solution.py:281
  30.4 46.1 %collective-permute-start.5 = (bf16[1024,512]{1,0:T(8,128)(2,1)S(1)}, bf16[1024,512]{1,0:T(8,128)(2,1)S(1)}, u32[]{:S(2)}, u32[]{:S(2)}) collective-permute-start(bf16[1024,512]{1,0:T(8,128)(2,1)S(1)} %get-tuple-element.1331), channel_id=1, source_target_pairs={{0,14},{1,15},{2,0},{3,1},{4,2},{5,3},{6,4},{7,5},{8,6},{9,7},{10,... | collective-permute-start | bytes 3145736 | tf_op jit(solution)/shard_map/ppermute | solution.py:282
  31.6 66.3 %collective-permute-start.32 = (bf16[256,2048]{1,0:T(8,128)(2,1)S(1)}, bf16[256,2048]{1,0:T(8,128)(2,1)S(1)}, u32[]{:S(2)}, u32[]{:S(2)}) collective-permute-start(bf16[256,2048]{1,0:T(8,128)(2,1)S(1)} %collective-permute-done.30), channel_id=1, source_target_pairs={{0,2},{1,3},{2,4},{3,5},{4,6},{5,7},{6,8},{7,9},{8,10},{9,11},{10,... | collective-permute-start | bytes 3145736 | tf_op jit(solution)/shard_map/ppermute | solution.py:281
  52.9 46.1 %collective-permute-start.33 = (bf16[256,2048]{1,0:T(8,128)(2,1)S(1)}, bf16[256,2048]{1,0:T(8,128)(2,1)S(1)}, u32[]{:S(2)}, u32[]{:S(2)}) collective-permute-start(bf16[256,2048]{1,0:T(8,128)(2,1)S(1)} %collective-permute-done.31), channel_id=1, source_target_pairs={{0,14},{1,15},{2,0},{3,1},{4,2},{5,3},{6,4},{7,5},{8,6},{9,7},{10,... | collective-permute-start | bytes 3145736 | tf_op jit(solution)/shard_map/ppermute | solution.py:282
  54.0 66.3 %collective-permute-start.19 = (bf16[1024,512]{1,0:T(8,128)(2,1)S(1)}, bf16[1024,512]{1,0:T(8,128)(2,1)S(1)}, u32[]{:S(2)}, u32[]{:S(2)}) collective-permute-start(bf16[1024,512]{1,0:T(8,128)(2,1)S(1)} %collective-permute-done.17), channel_id=1, source_target_pairs={{0,2},{1,3},{2,4},{3,5},{4,6},{5,7},{6,8},{7,9},{8,10},{9,11},{10,... | collective-permute-start | bytes 3145736 | tf_op jit(solution)/shard_map/ppermute | solution.py:281
  75.4 46.1 %collective-permute-start.20 = (bf16[1024,512]{1,0:T(8,128)(2,1)S(1)}, bf16[1024,512]{1,0:T(8,128)(2,1)S(1)}, u32[]{:S(2)}, u32[]{:S(2)}) collective-permute-start(bf16[1024,512]{1,0:T(8,128)(2,1)S(1)} %collective-permute-done.18), channel_id=1, source_target_pairs={{0,14},{1,15},{2,0},{3,1},{4,2},{5,3},{6,4},{7,5},{8,6},{9,7},{10,... | collective-permute-start | bytes 3145736 | tf_op jit(solution)/shard_map/ppermute | solution.py:282
  76.5 66.3 %collective-permute-start.6 = (bf16[1024,512]{1,0:T(8,128)(2,1)S(1)}, bf16[1024,512]{1,0:T(8,128)(2,1)S(1)}, u32[]{:S(2)}, u32[]{:S(2)}) collective-permute-start(bf16[1024,512]{1,0:T(8,128)(2,1)S(1)} %collective-permute-done.4), channel_id=1, source_target_pairs={{0,2},{1,3},{2,4},{3,5},{4,6},{5,7},{6,8},{7,9},{8,10},{9,11},{10,... | collective-permute-start | bytes 3145736 | tf_op jit(solution)/shard_map/ppermute | solution.py:281
  97.8 46.3 %collective-permute-start.7 = (bf16[1024,512]{1,0:T(8,128)(2,1)S(1)}, bf16[1024,512]{1,0:T(8,128)(2,1)S(1)}, u32[]{:S(2)}, u32[]{:S(2)}) collective-permute-start(bf16[1024,512]{1,0:T(8,128)(2,1)S(1)} %collective-permute-done.5), channel_id=1, source_target_pairs={{0,14},{1,15},{2,0},{3,1},{4,2},{5,3},{6,4},{7,5},{8,6},{9,7},{10,... | collective-permute-start | bytes 3145736 | tf_op jit(solution)/shard_map/ppermute | solution.py:282
  99.0 66.3 %collective-permute-start.34 = (bf16[256,2048]{1,0:T(8,128)(2,1)S(1)}, bf16[256,2048]{1,0:T(8,128)(2,1)S(1)}, u32[]{:S(2)}, u32[]{:S(2)}) collective-permute-start(bf16[256,2048]{1,0:T(8,128)(2,1)S(1)} %collective-permute-done.32), channel_id=1, source_target_pairs={{0,2},{1,3},{2,4},{3,5},{4,6},{5,7},{6,8},{7,9},{8,10},{9,11},{10,... | collective-permute-start | bytes 3145736 | tf_op jit(solution)/shard_map/ppermute | solution.py:281
  120.3 46.1 %collective-permute-start.35 = (bf16[256,2048]{1,0:T(8,128)(2,1)S(1)}, bf16[256,2048]{1,0:T(8,128)(2,1)S(1)}, u32[]{:S(2)}, u32[]{:S(2)}) collective-permute-start(bf16[256,2048]{1,0:T(8,128)(2,1)S(1)} %collective-permute-done.33), channel_id=1, source_target_pairs={{0,14},{1,15},{2,0},{3,1},{4,2},{5,3},{6,4},{7,5},{8,6},{9,7},{10,... | collective-permute-start | bytes 3145736 | tf_op jit(solution)/shard_map/ppermute | solution.py:282
  121.5 66.3 %collective-permute-start.21 = (bf16[1024,512]{1,0:T(8,128)(2,1)S(1)}, bf16[1024,512]{1,0:T(8,128)(2,1)S(1)}, u32[]{:S(2)}, u32[]{:S(2)}) collective-permute-start(bf16[1024,512]{1,0:T(8,128)(2,1)S(1)} %collective-permute-done.19), channel_id=1, source_target_pairs={{0,2},{1,3},{2,4},{3,5},{4,6},{5,7},{6,8},{7,9},{8,10},{9,11},{10,... | collective-permute-start | bytes 3145736 | tf_op jit(solution)/shard_map/ppermute | solution.py:281
  142.8 46.1 %collective-permute-start.22 = (bf16[1024,512]{1,0:T(8,128)(2,1)S(1)}, bf16[1024,512]{1,0:T(8,128)(2,1)S(1)}, u32[]{:S(2)}, u32[]{:S(2)}) collective-permute-start(bf16[1024,512]{1,0:T(8,128)(2,1)S(1)} %collective-permute-done.20), channel_id=1, source_target_pairs={{0,14},{1,15},{2,0},{3,1},{4,2},{5,3},{6,4},{7,5},{8,6},{9,7},{10,... | collective-permute-start | bytes 3145736 | tf_op jit(solution)/shard_map/ppermute | solution.py:282
  144.2 66.0 %collective-permute-start.8 = (bf16[1024,512]{1,0:T(8,128)(2,1)S(1)}, bf16[1024,512]{1,0:T(8,128)(2,1)S(1)}, u32[]{:S(2)}, u32[]{:S(2)}) collective-permute-start(bf16[1024,512]{1,0:T(8,128)(2,1)S(1)} %collective-permute-done.6), channel_id=1, source_target_pairs={{0,2},{1,3},{2,4},{3,5},{4,6},{5,7},{6,8},{7,9},{8,10},{9,11},{10,... | collective-permute-start | bytes 3145736 | tf_op jit(solution)/shard_map/ppermute | solution.py:281
  165.2 46.1 %collective-permute-start.9 = (bf16[1024,512]{1,0:T(8,128)(2,1)S(1)}, bf16[1024,512]{1,0:T(8,128)(2,1)S(1)}, u32[]{:S(2)}, u32[]{:S(2)}) collective-permute-start(bf16[1024,512]{1,0:T(8,128)(2,1)S(1)} %collective-permute-done.7), channel_id=1, source_target_pairs={{0,14},{1,15},{2,0},{3,1},{4,2},{5,3},{6,4},{7,5},{8,6},{9,7},{10,... | collective-permute-start | bytes 3145736 | tf_op jit(solution)/shard_map/ppermute | solution.py:282
  166.4 66.3 %collective-permute-start.36 = (bf16[256,2048]{1,0:T(8,128)(2,1)S(1)}, bf16[256,2048]{1,0:T(8,128)(2,1)S(1)}, u32[]{:S(2)}, u32[]{:S(2)}) collective-permute-start(bf16[256,2048]{1,0:T(8,128)(2,1)S(1)} %collective-permute-done.34), channel_id=1, source_target_pairs={{0,2},{1,3},{2,4},{3,5},{4,6},{5,7},{6,8},{7,9},{8,10},{9,11},{10,... | collective-permute-start | bytes 3145736 | tf_op jit(solution)/shard_map/ppermute | solution.py:281
  187.7 46.1 %collective-permute-start.37 = (bf16[256,2048]{1,0:T(8,128)(2,1)S(1)}, bf16[256,2048]{1,0:T(8,128)(2,1)S(1)}, u32[]{:S(2)}, u32[]{:S(2)}) collective-permute-start(bf16[256,2048]{1,0:T(8,128)(2,1)S(1)} %collective-permute-done.35), channel_id=1, source_target_pairs={{0,14},{1,15},{2,0},{3,1},{4,2},{5,3},{6,4},{7,5},{8,6},{9,7},{10,... | collective-permute-start | bytes 3145736 | tf_op jit(solution)/shard_map/ppermute | solution.py:282
  188.9 66.3 %collective-permute-start.23 = (bf16[1024,512]{1,0:T(8,128)(2,1)S(1)}, bf16[1024,512]{1,0:T(8,128)(2,1)S(1)}, u32[]{:S(2)}, u32[]{:S(2)}) collective-permute-start(bf16[1024,512]{1,0:T(8,128)(2,1)S(1)} %collective-permute-done.21), channel_id=1, source_target_pairs={{0,2},{1,3},{2,4},{3,5},{4,6},{5,7},{6,8},{7,9},{8,10},{9,11},{10,... | collective-permute-start | bytes 3145736 | tf_op jit(solution)/shard_map/ppermute | solution.py:281
  210.2 46.1 %collective-permute-start.24 = (bf16[1024,512]{1,0:T(8,128)(2,1)S(1)}, bf16[1024,512]{1,0:T(8,128)(2,1)S(1)}, u32[]{:S(2)}, u32[]{:S(2)}) collective-permute-start(bf16[1024,512]{1,0:T(8,128)(2,1)S(1)} %collective-permute-done.22), channel_id=1, source_target_pairs={{0,14},{1,15},{2,0},{3,1},{4,2},{5,3},{6,4},{7,5},{8,6},{9,7},{10,... | collective-permute-start | bytes 3145736 | tf_op jit(solution)/shard_map/ppermute | solution.py:282
  211.3 66.3 %collective-permute-start.10 = (bf16[1024,512]{1,0:T(8,128)(2,1)S(1)}, bf16[1024,512]{1,0:T(8,128)(2,1)S(1)}, u32[]{:S(2)}, u32[]{:S(2)}) collective-permute-start(bf16[1024,512]{1,0:T(8,128)(2,1)S(1)} %collective-permute-done.8), channel_id=1, source_target_pairs={{0,2},{1,3},{2,4},{3,5},{4,6},{5,7},{6,8},{7,9},{8,10},{9,11},{10,... | collective-permute-start | bytes 3145736 | tf_op jit(solution)/shard_map/ppermute | solution.py:281
  232.7 46.2 %collective-permute-start.11 = (bf16[1024,512]{1,0:T(8,128)(2,1)S(1)}, bf16[1024,512]{1,0:T(8,128)(2,1)}, u32[]{:S(2)}, u32[]{:S(2)}) collective-permute-start(bf16[1024,512]{1,0:T(8,128)(2,1)S(1)} %collective-permute-done.9), channel_id=1, source_target_pairs={{0,14},{1,15},{2,0},{3,1},{4,2},{5,3},{6,4},{7,5},{8,6},{9,7},{10,... | collective-permute-start | bytes 3145736 | tf_op jit(solution)/shard_map/ppermute | solution.py:282
  233.8 66.4 %collective-permute-start.38 = (bf16[256,2048]{1,0:T(8,128)(2,1)S(1)}, bf16[256,2048]{1,0:T(8,128)(2,1)}, u32[]{:S(2)}, u32[]{:S(2)}) collective-permute-start(bf16[256,2048]{1,0:T(8,128)(2,1)S(1)} %collective-permute-done.36), channel_id=1, source_target_pairs={{0,2},{1,3},{2,4},{3,5},{4,6},{5,7},{6,8},{7,9},{8,10},{9,11},{10,... | collective-permute-start | bytes 3145736 | tf_op jit(solution)/shard_map/ppermute | solution.py:281
  255.1 46.2 %collective-permute-start.39 = (bf16[256,2048]{1,0:T(8,128)(2,1)S(1)}, bf16[256,2048]{1,0:T(8,128)(2,1)}, u32[]{:S(2)}, u32[]{:S(2)}) collective-permute-start(bf16[256,2048]{1,0:T(8,128)(2,1)S(1)} %collective-permute-done.37), channel_id=1, source_target_pairs={{0,14},{1,15},{2,0},{3,1},{4,2},{5,3},{6,4},{7,5},{8,6},{9,7},{10,... | collective-permute-start | bytes 3145736 | tf_op jit(solution)/shard_map/ppermute | solution.py:282
  256.3 66.4 %collective-permute-start.25 = (bf16[1024,512]{1,0:T(8,128)(2,1)S(1)}, bf16[1024,512]{1,0:T(8,128)(2,1)}, u32[]{:S(2)}, u32[]{:S(2)}) collective-permute-start(bf16[1024,512]{1,0:T(8,128)(2,1)S(1)} %collective-permute-done.23), channel_id=1, source_target_pairs={{0,2},{1,3},{2,4},{3,5},{4,6},{5,7},{6,8},{7,9},{8,10},{9,11},{10,... | collective-permute-start | bytes 3145736 | tf_op jit(solution)/shard_map/ppermute | solution.py:281
  277.6 46.6 %collective-permute-start.26 = (bf16[1024,512]{1,0:T(8,128)(2,1)S(1)}, bf16[1024,512]{1,0:T(8,128)(2,1)}, u32[]{:S(2)}, u32[]{:S(2)}) collective-permute-start(bf16[1024,512]{1,0:T(8,128)(2,1)S(1)} %collective-permute-done.24), channel_id=1, source_target_pairs={{0,14},{1,15},{2,0},{3,1},{4,2},{5,3},{6,4},{7,5},{8,6},{9,7},{10,... | collective-permute-start | bytes 3145736 | tf_op jit(solution)/shard_map/ppermute | solution.py:282
  278.9 66.2 %collective-permute-start.12 = (bf16[1024,512]{1,0:T(8,128)(2,1)S(1)}, bf16[1024,512]{1,0:T(8,128)(2,1)S(1)}, u32[]{:S(2)}, u32[]{:S(2)}) collective-permute-start(bf16[1024,512]{1,0:T(8,128)(2,1)S(1)} %collective-permute-done.10), channel_id=1, source_target_pairs={{0,2},{1,3},{2,4},{3,5},{4,6},{5,7},{6,8},{7,9},{8,10},{9,11},{10,... | collective-permute-start | bytes 3145736 | tf_op jit(solution)/shard_map/ppermute | solution.py:281
  300.2 47.3 %collective-permute-start.13 = (bf16[1024,512]{1,0:T(8,128)(2,1)}, bf16[1024,512]{1,0:T(8,128)(2,1)}, u32[]{:S(2)}, u32[]{:S(2)}) collective-permute-start(bf16[1024,512]{1,0:T(8,128)(2,1)} %collective-permute-done.11), channel_id=1, source_target_pairs={{0,14},{1,15},{2,0},{3,1},{4,2},{5,3},{6,4},{7,5},{8,6},{9,7},{10,... | collective-permute-start | bytes 3145736 | tf_op jit(solution)/shard_map/ppermute | solution.py:282
  301.3 66.3 %collective-permute-start.40 = (bf16[256,2048]{1,0:T(8,128)(2,1)}, bf16[256,2048]{1,0:T(8,128)(2,1)}, u32[]{:S(2)}, u32[]{:S(2)}) collective-permute-start(bf16[256,2048]{1,0:T(8,128)(2,1)} %collective-permute-done.38), channel_id=1, source_target_pairs={{0,2},{1,3},{2,4},{3,5},{4,6},{5,7},{6,8},{7,9},{8,10},{9,11},{10,... | collective-permute-start | bytes 3145736 | tf_op jit(solution)/shard_map/ppermute | solution.py:281
  322.6 44.9 %collective-permute-start.41 = (bf16[256,2048]{1,0:T(8,128)(2,1)}, bf16[256,2048]{1,0:T(8,128)(2,1)}, u32[]{:S(2)}, u32[]{:S(2)}) collective-permute-start(bf16[256,2048]{1,0:T(8,128)(2,1)} %collective-permute-done.39), channel_id=1, source_target_pairs={{0,14},{1,15},{2,0},{3,1},{4,2},{5,3},{6,4},{7,5},{8,6},{9,7},{10,... | collective-permute-start | bytes 3145736 | tf_op jit(solution)/shard_map/ppermute | solution.py:282
  324.2 69.5 %collective-permute-start.27 = (bf16[1024,512]{1,0:T(8,128)(2,1)}, bf16[1024,512]{1,0:T(8,128)(2,1)}, u32[]{:S(2)}, u32[]{:S(2)}) collective-permute-start(bf16[1024,512]{1,0:T(8,128)(2,1)} %collective-permute-done.25), channel_id=1, source_target_pairs={{0,2},{1,3},{2,4},{3,5},{4,6},{5,7},{6,8},{7,9},{8,10},{9,11},{10,... | collective-permute-start | bytes 3145736 | tf_op jit(solution)/shard_map/ppermute | solution.py:281
  346.0 50.3 %collective-permute-start.28 = (bf16[1024,512]{1,0:T(8,128)(2,1)}, bf16[1024,512]{1,0:T(8,128)(2,1)}, u32[]{:S(2)}, u32[]{:S(2)}) collective-permute-start(bf16[1024,512]{1,0:T(8,128)(2,1)} %collective-permute-done.26), channel_id=1, source_target_pairs={{0,14},{1,15},{2,0},{3,1},{4,2},{5,3},{6,4},{7,5},{8,6},{9,7},{10,... | collective-permute-start | bytes 3145736 | tf_op jit(solution)/shard_map/ppermute | solution.py:282
  347.5 44.2 %collective-permute-start.47 = (s32[8,128,2]{1,2,0:T(2,128)S(1)}, s32[8,128,2]{1,2,0:T(2,128)S(1)}, u32[]{:S(2)}, u32[]{:S(2)}) collective-permute-start(s32[8,128,2]{1,2,0:T(2,128)S(1)} %bitcast.51), channel_id=1, source_target_pairs={{0,8},{8,0},{16,24},{24,16},{32,40},{40,32},{48,56},{56,48},{64,72... | collective-permute-start | bytes 24584 | tf_op jit(solution)/shard_map/ppermute | solution.py:306
  367.6 45.3 %collective-permute-start.14 = (bf16[1024,512]{1,0:T(8,128)(2,1)}, bf16[1024,512]{1,0:T(8,128)(2,1)}, u32[]{:S(2)}, u32[]{:S(2)}) collective-permute-start(bf16[1024,512]{1,0:T(8,128)(2,1)} %copy-done.33), channel_id=1, source_target_pairs={{0,2},{1,3},{2,4},{3,5},{4,6},{5,7},{6,8},{7,9},{8,10},{9,11},{10,... | collective-permute-start | bytes 3145736 | tf_op jit(solution)/shard_map/ppermute | solution.py:281
  367.6 45.3 %collective-permute-start.15 = (bf16[1024,512]{1,0:T(8,128)(2,1)}, bf16[1024,512]{1,0:T(8,128)(2,1)}, u32[]{:S(2)}, u32[]{:S(2)}) collective-permute-start(bf16[1024,512]{1,0:T(8,128)(2,1)} %collective-permute-done.13), channel_id=1, source_target_pairs={{0,14},{1,15},{2,0},{3,1},{4,2},{5,3},{6,4},{7,5},{8,6},{9,7},{10,... | collective-permute-start | bytes 3145736 | tf_op jit(solution)/shard_map/ppermute | solution.py:282
  391.7 69.9 %collective-permute-start.42 = (bf16[256,2048]{1,0:T(8,128)(2,1)}, bf16[256,2048]{1,0:T(8,128)(2,1)}, u32[]{:S(2)}, u32[]{:S(2)}) collective-permute-start(bf16[256,2048]{1,0:T(8,128)(2,1)} %collective-permute-done.41), channel_id=1, source_target_pairs={{0,14},{1,15},{2,0},{3,1},{4,2},{5,3},{6,4},{7,5},{8,6},{9,7},{10,... | collective-permute-start | bytes 3145736 | tf_op jit(solution)/shard_map/ppermute | solution.py:282
  393.7 57.1 %collective-permute-start.48 = (bf16[2048,8]{1,0:T(8,128)(2,1)S(1)}, bf16[2048,8]{1,0:T(8,128)(2,1)S(1)}, u32[]{:S(2)}, u32[]{:S(2)}) collective-permute-start(bf16[2048,8]{1,0:T(8,128)(2,1)S(1)} %bitcast.46), channel_id=1, source_target_pairs={{0,8},{8,0},{16,24},{24,16},{32,40},{40,32},{48,56},{56,48},{64,72... | collective-permute-start | bytes 98312 | tf_op jit(solution)/shard_map/ppermute | solution.py:306
  396.3 30.7 %collective-permute-start.46 = (f32[1,2048]{1,0:T(1,128)S(1)}, f32[1,2048]{1,0:T(1,128)S(1)}, u32[]{:S(2)}, u32[]{:S(2)}) collective-permute-start(f32[1,2048]{1,0:T(1,128)S(1)} %copy-done.38), channel_id=1, source_target_pairs={{0,8},{8,0},{16,24},{24,16},{32,40},{40,32},{48,56},{56,48},{64,72... | collective-permute-start | bytes 24584 | tf_op jit(solution)/shard_map/ppermute | solution.py:306
  412.9 52.7 %collective-permute-start.45 = (bf16[256,2048]{1,0:T(8,128)(2,1)}, bf16[256,2048]{1,0:T(8,128)(2,1)}, u32[]{:S(2)}, u32[]{:S(2)}) collective-permute-start(bf16[256,2048]{1,0:T(8,128)(2,1)} %collective-permute-done.40), channel_id=1, source_target_pairs={{0,2},{1,3},{2,4},{3,5},{4,6},{5,7},{6,8},{7,9},{8,10},{9,11},{10,... | collective-permute-start | bytes 3145736 | tf_op jit(solution)/shard_map/ppermute | solution.py:281
  412.9 66.8 %collective-permute-start.29 = (bf16[1024,512]{1,0:T(8,128)(2,1)}, bf16[1024,512]{1,0:T(8,128)(2,1)}, u32[]{:S(2)}, u32[]{:S(2)}) collective-permute-start(bf16[1024,512]{1,0:T(8,128)(2,1)} %collective-permute-done.28), channel_id=1, source_target_pairs={{0,14},{1,15},{2,0},{3,1},{4,2},{5,3},{6,4},{7,5},{8,6},{9,7},{10,... | collective-permute-start | bytes 3145736 | tf_op jit(solution)/shard_map/ppermute | solution.py:282
  427.0 55.6 %collective-permute-start.44 = (bf16[1024,512]{1,0:T(8,128)(2,1)}, bf16[1024,512]{1,0:T(8,128)(2,1)}, u32[]{:S(2)}, u32[]{:S(2)}) collective-permute-start(bf16[1024,512]{1,0:T(8,128)(2,1)} %collective-permute-done.27), channel_id=1, source_target_pairs={{0,2},{1,3},{2,4},{3,5},{4,6},{5,7},{6,8},{7,9},{8,10},{9,11},{10,... | collective-permute-start | bytes 3145736 | tf_op jit(solution)/shard_map/ppermute | solution.py:281
  450.7 51.4 %collective-permute-start.16 = (bf16[1024,512]{1,0:T(8,128)(2,1)}, bf16[1024,512]{1,0:T(8,128)(2,1)}, u32[]{:S(2)}, u32[]{:S(2)}) collective-permute-start(bf16[1024,512]{1,0:T(8,128)(2,1)} %collective-permute-done.15), channel_id=1, source_target_pairs={{0,14},{1,15},{2,0},{3,1},{4,2},{5,3},{6,4},{7,5},{8,6},{9,7},{10,... | collective-permute-start | bytes 3145736 | tf_op jit(solution)/shard_map/ppermute | solution.py:282
  461.6 43.5 %collective-permute-start.43 = (bf16[1024,512]{1,0:T(8,128)(2,1)}, bf16[1024,512]{1,0:T(8,128)(2,1)}, u32[]{:S(2)}, u32[]{:S(2)}) collective-permute-start(bf16[1024,512]{1,0:T(8,128)(2,1)} %collective-permute-done.14), channel_id=1, source_target_pairs={{0,2},{1,3},{2,4},{3,5},{4,6},{5,7},{6,8},{7,9},{8,10},{9,11},{10,... | collective-permute-start | bytes 3145736 | tf_op jit(solution)/shard_map/ppermute | solution.py:281
  528.1 22.8 %collective-permute-start = (bf16[64,2048]{1,0:T(8,128)(2,1)S(1)}, bf16[64,2048]{1,0:T(8,128)(2,1)S(1)}, u32[]{:S(2)}, u32[]{:S(2)}) collective-permute-start(bf16[64,2048]{1,0:T(8,128)(2,1)S(1)} %get-tuple-element.2056), channel_id=1, source_target_pairs={{0,16},{8,24},{16,32},{24,40},{32,48},{40,56},{48,64},{56,72},{64,... | collective-permute-start | bytes 786440 | tf_op jit(solution)/shard_map/while/body/eval_jaxpr/ppermute | solution.py:335
  849.8 81.5 %collective-permute-start = (bf16[64,2048]{1,0:T(8,128)(2,1)S(1)}, bf16[64,2048]{1,0:T(8,128)(2,1)S(1)}, u32[]{:S(2)}, u32[]{:S(2)}) collective-permute-start(bf16[64,2048]{1,0:T(8,128)(2,1)S(1)} %get-tuple-element.2056), channel_id=1, source_target_pairs={{0,16},{8,24},{16,32},{24,40},{32,48},{40,56},{48,64},{56,72},{64,... | collective-permute-start | bytes 786440 | tf_op jit(solution)/shard_map/while/body/eval_jaxpr/ppermute | solution.py:335
  952.6 24.6 %collective-permute-start.49 = (bf16[64,2048]{1,0:T(8,128)(2,1)S(1)}, bf16[64,2048]{1,0:T(8,128)(2,1)S(1)}, u32[]{:S(2)}, u32[]{:S(2)}) collective-permute-start(bf16[64,2048]{1,0:T(8,128)(2,1)S(1)} %get-tuple-element.1559), channel_id=1, source_target_pairs={{0,8},{8,0},{16,24},{24,16},{32,40},{40,32},{48,56},{56,48},{64,72... | collective-permute-start | bytes 786440 | tf_op jit(solution)/shard_map/ppermute | solution.py:355
  (207 other events, 3463.9 us)

commit v5 on v4

--- a/solution.py
+++ b/solution.py
@@ -54,9 +54,9 @@
 
 
 def load_kernel(place_ref, *refs):
-    sources, (middle_ref, last_ref) = refs[:source_count], refs[source_count : source_count + 2]
-    loaded, (first_out, second_out) = refs[source_count + 4 : -5], refs[-5:-3]
-    first_sems, second_sems, out_sems = refs[-3:]
+    sources, (middle_ref, base_ref, back_ref) = refs[:source_count], refs[source_count:][:3]
+    loaded, (first_out, second_out) = refs[source_count + 5 : -6], refs[-6:-4]
+    leaving, first_sems, second_sems, out_sems = refs[-4:]
     held = z_size // 2
     copies = [layer_copies(0, (0, held), place_ref[1], sources, loaded[:3], first_sems)]
     if early:
@@ -71,9 +71,10 @@
 
     @pl.when(place_ref[3] == 1)
     def _():
+        leaving[...] = base_ref[...] + back_ref[...].astype(jnp.float32)
         away = [
             pltpu.make_async_copy(middle_ref, first_out, out_sems.at[0]),
-            pltpu.make_async_copy(last_ref, second_out, out_sems.at[1]),
+            pltpu.make_async_copy(leaving, second_out, out_sems.at[1]),
         ]
         for copy in away:
             copy.start()
@@ -130,7 +131,7 @@
     place_ref, mine_ref, other_ref, part_ref, back_ref, scale_ref, ids_ref, router_ref, *refs
 ):
     ready, sources, refs = refs[:ready_count], refs[ready_count:][:source_count], refs[ready_count + source_count :]
-    middle_ref, own_ref, lent_ref, gates, ups, downs, rows, total, sems = refs
+    middle_out, base_ref, lent_ref, gates, ups, downs, middle_ref, rows, total, sems, out_sem = refs
     count, late = mine_ref.shape[0], gates.shape[0]
     start, wait = layer_copies(
         1, (early, late), place_ref[1], sources, (gates, ups, downs), sems
@@ -143,6 +144,8 @@
             part_ref[:count] + back_ref[count:].astype(jnp.float32)
         )
         middle_ref[...] = middle
+        put_away = pltpu.make_async_copy(middle_ref, middle_out, out_sem)
+        put_away.start()
         rows[pl.ds(0, count)] = normed_of(middle, scale_ref[...])
         beside = other_ref[...].astype(jnp.float32) + (
             part_ref[count:] + back_ref[:count].astype(jnp.float32)
@@ -152,16 +155,13 @@
             (gates.at[i], ups.at[i], downs.at[i], functools.partial(wait, i)) for i in range(late)
         ]
         experts_sum(place_ref[2], rows, ids_ref, router_ref, experts, total)
-        own_ref[...] = total[:count]
+        base_ref[...] = middle_ref[...] + total[:count]
         lent_ref[...] = total[count:].astype(jnp.bfloat16)
-
-
-def add_kernel(place_ref, middle_ref, own_ref, back_ref, sum_ref, sent_ref):
-    @pl.when(place_ref[0] == 1)
-    def _():
-        total = middle_ref[...] + (own_ref[...] + back_ref[...].astype(jnp.float32))
-        sum_ref[...] = total
-        sent_ref[...] = total.astype(jnp.bfloat16)
+        put_away.wait()
+
+
+def add_kernel(base_ref, back_ref, sent_ref):
+    sent_ref[...] = (base_ref[...] + back_ref[...].astype(jnp.float32)).astype(jnp.bfloat16)
 
 
 def vmem(count):
@@ -185,7 +185,7 @@
     return [pl.BlockSpec(memory_space=pltpu.HBM)] * count
 
 
-def load_ahead(place, sources, middle, last, stored):
+def load_ahead(place, sources, middle, base, back, stored):
     width, units = sources[0].shape
     held = z_size // 2
     shapes = layer_shapes(sources, held) + (layer_shapes(sources, early) if early else [])
@@ -195,16 +195,21 @@
         + tuple(like(array.shape, array.dtype) for array in stored),
         in_specs=[pl.BlockSpec(memory_space=pltpu.SMEM)]
         + in_hbm(len(sources))
-        + vmem(2)
+        + vmem(3)
         + in_hbm(2),
         out_specs=tuple(vmem(len(shapes)) + in_hbm(2)),
-        scratch_shapes=[copy_sems(held), copy_sems(early), pltpu.SemaphoreType.DMA((2,))],
-        input_output_aliases={source_count + 3 + i: len(shapes) + i for i in range(2)},
+        scratch_shapes=[
+            pltpu.VMEM(base.shape, jnp.float32),
+            copy_sems(held),
+            copy_sems(early),
+            pltpu.SemaphoreType.DMA((2,)),
+        ],
+        input_output_aliases={source_count + 4 + i: len(shapes) + i for i in range(2)},
         compiler_params=pltpu.CompilerParams(vmem_limit_bytes=3 << 20),
         cost_estimate=pl.CostEstimate(
             flops=0, bytes_accessed=6 * (held + early) * width * units, transcendentals=0
         ),
-    )(place, *sources, middle, last, *stored)
+    )(place, *sources, middle, base, back, *stored)
     return results[:3], results[3:-2], results[-2:]
 
 
@@ -232,14 +237,16 @@
         in_specs=[pl.BlockSpec(memory_space=pltpu.SMEM)]
         + vmem(7 + len(ready))
         + in_hbm(len(sources)),
-        out_specs=tuple(vmem(3)),
+        out_specs=tuple(in_hbm(1) + vmem(2)),
         scratch_shapes=[
             pltpu.VMEM(shape, jnp.bfloat16) for shape in layer_shapes(sources, z_size // 2 - early)
         ]
         + [
+            pltpu.VMEM((count, width), jnp.float32),
             pltpu.VMEM((2 * count, width), jnp.bfloat16),
             pltpu.VMEM((2 * count, width), jnp.float32),
             copy_sems(z_size // 2 - early),
+            pltpu.SemaphoreType.DMA(()),
         ],
         compiler_params=pltpu.CompilerParams(
             vmem_limit_bytes=(10 + 6 * (z_size // 2 - early)) << 20
@@ -247,14 +254,14 @@
     )(place, mine, other, part, back, scale, ids, router, *ready, *sources)
 
 
-def run_add(place, middle, own, back):
+def run_add(base, back):
     return pl.pallas_call(
         add_kernel,
-        out_shape=(like(middle.shape, jnp.float32), like(middle.shape, jnp.bfloat16)),
-        in_specs=[pl.BlockSpec(memory_space=pltpu.SMEM)] + vmem(3),
-        out_specs=tuple(vmem(2)),
-        compiler_params=pltpu.CompilerParams(vmem_limit_bytes=4 << 20),
-    )(place, middle, own, back)
+        out_shape=like(base.shape, jnp.bfloat16),
+        in_specs=vmem(2),
+        out_specs=vmem(1)[0],
+        compiler_params=pltpu.CompilerParams(vmem_limit_bytes=3 << 20),
+    )(base, back)
 
 
 def device_at(ring, z, core):
@@ -329,27 +336,27 @@
         return lax.ppermute(value, "expert", other_core)
 
     def ring_step(step, state):
-        sent, middle, last, stored = state
+        sent, middle, base, back, stored = state
         flags = [(ring_id == step).astype(jnp.int32), my_z, my_core]
         place = jnp.stack(flags + [(ring_id == step - 1).astype(jnp.int32)])
         mine = lax.ppermute(sent, "section", next_ring)
-        ahead = load_ahead(place, sources, middle, last, stored)
+        ahead = load_ahead(place, sources, middle, base, back, stored)
         mine, (weights, ready, stored) = lax.optimization_barrier((mine, ahead))
         other = exchange(mine)
         part, lent = run_first(place, mine, other, scales[0], ids[0], routers[0], weights)
         back = exchange(lent)
-        middle, own, lent = run_second(
+        middle, base, lent = run_second(
             place, mine, other, part, back, scales[1], ids[1], routers[1], ready, sources
         )
-        last, sent = run_add(place, middle, own, exchange(lent))
-        return sent, middle, last, stored
+        back = exchange(lent)
+        return run_add(base, back), middle, base, back, stored
 
     blank = jnp.zeros(entering.shape, jnp.float32)
-    state = (entering, blank, blank, (blank, blank + 0))
-    _, middle, last, stored = lax.fori_loop(0, rings, ring_step, state)
+    state = (entering, blank, blank, entering, (blank, blank + 0))
+    _, middle, base, back, stored = lax.fori_loop(0, rings, ring_step, state)
     final = ring_id == rings - 1
     stored_first = jnp.where(final, middle, stored[0])
-    stored_second = jnp.where(final, last, stored[1])
+    stored_second = jnp.where(final, base + back.astype(jnp.float32), stored[1])
     kept = jnp.where(upper == 0, stored_first, stored_second)
     given = jnp.where(upper == 0, stored_second, stored_first)
     taken = lax.ppermute(given.astype(jnp.bfloat16), "section", other_half).astype(jnp.float32)

time: 989 us -> 978 us (0.989)
  Pallas kernels: 119 us -> 101 us
  local copies, waits for them, and re-layouts: 15.5 us -> 27.5 us
    pallas_call x16, Pallas kernels: 23.7 us -> 13.1 us  [run_first(): pl.pallas_call(first_kernel, out_shape=(like((2 * count, width), jnp.floa...]
    while x226 -> x258, local copies, waits for them, and re-layouts: 6.35 us -> 16.8 us
where the time goes in v5:
time: 978 us; the launch traced here: 968 us
  waiting for transfers between devices  606 us (62%)
  starting transfers between devices  227 us (23%)
  Pallas kernels  101 us (10%)
  local copies, waits for them, and re-layouts  27.5 us (3%)
    ppermute x21, waiting for transfers between devices, gather_ring(): travelling[m] = lax.ppermute(pair[0], both, forward)  347 us
    ppermute x16, waiting for transfers between devices, ring_step(): mine = lax.ppermute(sent, 'section', next_ring)  116 us
    ppermute x16, starting transfers between devices, ring_step(): mine = lax.ppermute(sent, 'section', next_ring)  93.8 us
    ppermute x48, waiting for transfers between devices, exchange(): return lax.ppermute(value, 'expert', other_core)  63.9 us
    ppermute x21, starting transfers between devices, gather_ring(): travelling[m + 1] = lax.ppermute(pair[1], both, backward)  42.7 us
    ppermute x48, starting transfers between devices, exchange(): return lax.ppermute(value, 'expert', other_core)  36.9 us
    pallas_call x16, Pallas kernels, load_ahead(): pl.pallas_call(load_kernel, out_shape=tuple((pltpu.VMEM(shape, jnp.bfloat...  36.5 us
    ppermute x21, waiting for transfers between devices, gather_ring(): travelling[m + 1] = lax.ppermute(pair[1], both, backward)  34.5 us
  transfers between devices with their start and end apart: 110, of which 88 were waited for; matrix products, arithmetic and copies ran while one was open for 1% of the time, Pallas kernels for 4%

profile of v5, /device:TPU:31, one launch (start us, length us, event | category | flops | bytes accessed | tf_op | source)
XLA Modules:
  0.0 968.0 jit_solution(5752138975086371043)
XLA Ops:
  3.6 4.0 collective-permute-start.31
  10.8 19.7 %collective-permute-done.30 = bf16[256,2048]{1,0:T(8,128)(2,1)S(1)} collective-permute-done((bf16[256,2048]{1,0:T(8,128)(2,1)S(1)}, bf16[256,2048]{1,0:T(8,128)(2,1)S(1)}, u32[]{:S(2)}, u32[]{:S(2)}) %collective-permute-start.30) | collective-permute-done | bytes 1048608 | tf_op jit(solution)/shard_map/ppermute | solution.py:288
  32.0 20.9 %collective-permute-done.17 = bf16[1024,512]{1,0:T(8,128)(2,1)S(1)} collective-permute-done((bf16[1024,512]{1,0:T(8,128)(2,1)S(1)}, bf16[1024,512]{1,0:T(8,128)(2,1)S(1)}, u32[]{:S(2)}, u32[]{:S(2)}) %collective-permute-start.17) | collective-permute-done | bytes 1048608 | tf_op jit(solution)/shard_map/ppermute | solution.py:288
  54.4 21.0 %collective-permute-done.4 = bf16[1024,512]{1,0:T(8,128)(2,1)S(1)} collective-permute-done((bf16[1024,512]{1,0:T(8,128)(2,1)S(1)}, bf16[1024,512]{1,0:T(8,128)(2,1)S(1)}, u32[]{:S(2)}, u32[]{:S(2)}) %collective-permute-start.4) | collective-permute-done | bytes 1048608 | tf_op jit(solution)/shard_map/ppermute | solution.py:288
  76.8 21.0 %collective-permute-done.32 = bf16[256,2048]{1,0:T(8,128)(2,1)S(1)} collective-permute-done((bf16[256,2048]{1,0:T(8,128)(2,1)S(1)}, bf16[256,2048]{1,0:T(8,128)(2,1)S(1)}, u32[]{:S(2)}, u32[]{:S(2)}) %collective-permute-start.32) | collective-permute-done | bytes 1048608 | tf_op jit(solution)/shard_map/ppermute | solution.py:288
  99.4 20.9 %collective-permute-done.19 = bf16[1024,512]{1,0:T(8,128)(2,1)S(1)} collective-permute-done((bf16[1024,512]{1,0:T(8,128)(2,1)S(1)}, bf16[1024,512]{1,0:T(8,128)(2,1)S(1)}, u32[]{:S(2)}, u32[]{:S(2)}) %collective-permute-start.19) | collective-permute-done | bytes 1048608 | tf_op jit(solution)/shard_map/ppermute | solution.py:288
  121.9 20.9 %collective-permute-done.6 = bf16[1024,512]{1,0:T(8,128)(2,1)S(1)} collective-permute-done((bf16[1024,512]{1,0:T(8,128)(2,1)S(1)}, bf16[1024,512]{1,0:T(8,128)(2,1)S(1)}, u32[]{:S(2)}, u32[]{:S(2)}) %collective-permute-start.6) | collective-permute-done | bytes 1048608 | tf_op jit(solution)/shard_map/ppermute | solution.py:288
  144.5 20.7 %collective-permute-done.34 = bf16[256,2048]{1,0:T(8,128)(2,1)S(1)} collective-permute-done((bf16[256,2048]{1,0:T(8,128)(2,1)S(1)}, bf16[256,2048]{1,0:T(8,128)(2,1)S(1)}, u32[]{:S(2)}, u32[]{:S(2)}) %collective-permute-start.34) | collective-permute-done | bytes 1048608 | tf_op jit(solution)/shard_map/ppermute | solution.py:288
  166.8 20.9 %collective-permute-done.21 = bf16[1024,512]{1,0:T(8,128)(2,1)S(1)} collective-permute-done((bf16[1024,512]{1,0:T(8,128)(2,1)S(1)}, bf16[1024,512]{1,0:T(8,128)(2,1)S(1)}, u32[]{:S(2)}, u32[]{:S(2)}) %collective-permute-start.21) | collective-permute-done | bytes 1048608 | tf_op jit(solution)/shard_map/ppermute | solution.py:288
  189.3 20.9 %collective-permute-done.8 = bf16[1024,512]{1,0:T(8,128)(2,1)S(1)} collective-permute-done((bf16[1024,512]{1,0:T(8,128)(2,1)S(1)}, bf16[1024,512]{1,0:T(8,128)(2,1)S(1)}, u32[]{:S(2)}, u32[]{:S(2)}) %collective-permute-start.8) | collective-permute-done | bytes 1048608 | tf_op jit(solution)/shard_map/ppermute | solution.py:288
  211.7 20.9 %collective-permute-done.36 = bf16[256,2048]{1,0:T(8,128)(2,1)S(1)} collective-permute-done((bf16[256,2048]{1,0:T(8,128)(2,1)S(1)}, bf16[256,2048]{1,0:T(8,128)(2,1)S(1)}, u32[]{:S(2)}, u32[]{:S(2)}) %collective-permute-start.36) | collective-permute-done | bytes 1048608 | tf_op jit(solution)/shard_map/ppermute | solution.py:288
  234.2 20.9 %collective-permute-done.23 = bf16[1024,512]{1,0:T(8,128)(2,1)S(1)} collective-permute-done((bf16[1024,512]{1,0:T(8,128)(2,1)S(1)}, bf16[1024,512]{1,0:T(8,128)(2,1)S(1)}, u32[]{:S(2)}, u32[]{:S(2)}) %collective-permute-start.23) | collective-permute-done | bytes 1048608 | tf_op jit(solution)/shard_map/ppermute | solution.py:288
  256.7 20.9 %collective-permute-done.10 = bf16[1024,512]{1,0:T(8,128)(2,1)S(1)} collective-permute-done((bf16[1024,512]{1,0:T(8,128)(2,1)S(1)}, bf16[1024,512]{1,0:T(8,128)(2,1)S(1)}, u32[]{:S(2)}, u32[]{:S(2)}) %collective-permute-start.10) | collective-permute-done | bytes 1048608 | tf_op jit(solution)/shard_map/ppermute | solution.py:288
  279.1 21.1 %collective-permute-done.38 = bf16[256,2048]{1,0:T(8,128)(2,1)} collective-permute-done((bf16[256,2048]{1,0:T(8,128)(2,1)S(1)}, bf16[256,2048]{1,0:T(8,128)(2,1)}, u32[]{:S(2)}, u32[]{:S(2)}) %collective-permute-start.38) | collective-permute-done | bytes 1048608 | tf_op jit(solution)/shard_map/ppermute | solution.py:288
  301.7 21.0 %collective-permute-done.25 = bf16[1024,512]{1,0:T(8,128)(2,1)} collective-permute-done((bf16[1024,512]{1,0:T(8,128)(2,1)S(1)}, bf16[1024,512]{1,0:T(8,128)(2,1)}, u32[]{:S(2)}, u32[]{:S(2)}) %collective-permute-start.25) | collective-permute-done | bytes 1048608 | tf_op jit(solution)/shard_map/ppermute | solution.py:288
  324.5 20.5 %collective-permute-done.12 = bf16[1024,512]{1,0:T(8,128)(2,1)S(1)} collective-permute-done((bf16[1024,512]{1,0:T(8,128)(2,1)S(1)}, bf16[1024,512]{1,0:T(8,128)(2,1)S(1)}, u32[]{:S(2)}, u32[]{:S(2)}) %collective-permute-start.12) | collective-permute-done | bytes 1048608 | tf_op jit(solution)/shard_map/ppermute | solution.py:288
  350.1 17.5 %collective-permute-done.40 = bf16[256,2048]{1,0:T(8,128)(2,1)} collective-permute-done((bf16[256,2048]{1,0:T(8,128)(2,1)}, bf16[256,2048]{1,0:T(8,128)(2,1)}, u32[]{:S(2)}, u32[]{:S(2)}) %collective-permute-start.40) | collective-permute-done | bytes 1048608 | tf_op jit(solution)/shard_map/ppermute | solution.py:288
  370.3 21.5 %collective-permute-done.47 = s32[8,128,2]{1,2,0:T(2,128)S(1)} collective-permute-done((s32[8,128,2]{1,2,0:T(2,128)S(1)}, s32[8,128,2]{1,2,0:T(2,128)S(1)}, u32[]{:S(2)}, u32[]{:S(2)}) %collective-permute-start.47) | collective-permute-done | bytes 8224 | tf_op jit(solution)/shard_map/ppermute | solution.py:313
  401.9 11.0 %collective-permute-done.14 = bf16[1024,512]{1,0:T(8,128)(2,1)} collective-permute-done((bf16[1024,512]{1,0:T(8,128)(2,1)}, bf16[1024,512]{1,0:T(8,128)(2,1)}, u32[]{:S(2)}, u32[]{:S(2)}) %collective-permute-start.14) | collective-permute-done | bytes 1048608 | tf_op jit(solution)/shard_map/ppermute | solution.py:288
  415.6 11.4 %collective-permute-done.46 = f32[1,2048]{1,0:T(1,128)S(1)} collective-permute-done((f32[1,2048]{1,0:T(1,128)S(1)}, f32[1,2048]{1,0:T(1,128)S(1)}, u32[]{:S(2)}, u32[]{:S(2)}) %collective-permute-start.46) | collective-permute-done | bytes 8224 | tf_op jit(solution)/shard_map/ppermute | solution.py:313
  427.0 23.8 %collective-permute-start.44 = (bf16[1024,512]{1,0:T(8,128)(2,1)}, bf16[1024,512]{1,0:T(8,128)(2,1)}, u32[]{:S(2)}, u32[]{:S(2)}) collective-permute-start(bf16[1024,512]{1,0:T(8,128)(2,1)} %collective-permute-done.27), channel_id=1, source_target_pairs={{0,2},{1,3},{2,4},{3,5},{4,6},{5,7},{6,8},{7,9},{8,10},{9,11},{10,... | collective-permute-start | bytes 3145736 | tf_op jit(solution)/shard_map/ppermute | solution.py:288
  450.7 10.8 %collective-permute-start.16 = (bf16[1024,512]{1,0:T(8,128)(2,1)}, bf16[1024,512]{1,0:T(8,128)(2,1)}, u32[]{:S(2)}, u32[]{:S(2)}) collective-permute-start(bf16[1024,512]{1,0:T(8,128)(2,1)} %collective-permute-done.15), channel_id=1, source_target_pairs={{0,14},{1,15},{2,0},{3,1},{4,2},{5,3},{6,4},{7,5},{8,6},{9,7},{10,... | collective-permute-start | bytes 3145736 | tf_op jit(solution)/shard_map/ppermute | solution.py:289
  464.8 14.8 %collective-permute-done.29 = bf16[1024,512]{1,0:T(8,128)(2,1)} collective-permute-done((bf16[1024,512]{1,0:T(8,128)(2,1)}, bf16[1024,512]{1,0:T(8,128)(2,1)}, u32[]{:S(2)}, u32[]{:S(2)}) %collective-permute-start.29) | collective-permute-done | bytes 1048608 | tf_op jit(solution)/shard_map/ppermute | solution.py:289
  482.6 19.6 %collective-permute-done.16 = bf16[1024,512]{1,0:T(8,128)(2,1)} collective-permute-done((bf16[1024,512]{1,0:T(8,128)(2,1)}, bf16[1024,512]{1,0:T(8,128)(2,1)}, u32[]{:S(2)}, u32[]{:S(2)}) %collective-permute-start.16) | collective-permute-done | bytes 1048608 | tf_op jit(solution)/shard_map/ppermute | solution.py:289
  507.6 431.1 %while.25 = (s32[]{:T(128)}, bf16[64,2048]{1,0:T(8,128)(2,1)}, f32[64,2048]{1,0:T(8,128)}, f32[64,2048]{1,0:T(8,128)S(1)}, bf16[64,2048]{1,0:T(8,128)(2,1)}, /*i...) while((s32[]{:T(128)}, bf16[64,2048]{1,0:T(8,128)(2,1)}, ...), condition=%wide.region_1.2_spmd, body=%wide.region_0.1_spmd.sunk | while | flops 19 | bytes 82838496 | solution.py:356
  513.3 4.5 collective-permute-start.1
  527.3 16.5 %collective-permute-start = (bf16[64,2048]{1,0:T(8,128)(2,1)}, bf16[64,2048]{1,0:T(8,128)(2,1)S(1)}, u32[]{:S(2)}, u32[]{:S(2)}) collective-permute-start(bf16[64,2048]{1,0:T(8,128)(2,1)} %get-tuple-element.2076), channel_id=1, source_target_pairs={{0,16},{8,24},{16,32},{24,40},{32,48},{40,56},{48,64},{56,72},{64,... | collective-permute-start | bytes 786440 | tf_op jit(solution)/shard_map/while/body/eval_jaxpr/ppermute | solution.py:342
  560.2 5.4 collective-permute-start
  581.9 5.4 collective-permute-start
  603.7 5.4 collective-permute-start
  625.5 5.4 collective-permute-start
  647.2 5.4 collective-permute-start
  654.3 4.0 collective-permute-done.mine_ref
  669.0 5.4 collective-permute-start
  690.8 5.4 collective-permute-start
  712.5 6.8 collective-permute-start
  735.7 5.4 collective-permute-start
  757.5 5.4 collective-permute-start
  779.2 5.4 collective-permute-start
  801.0 5.4 collective-permute-start
  822.8 5.4 collective-permute-start
  844.6 5.4 collective-permute-start
  850.0 12.9 %eval_jaxpr.32 = (bf16[4,2048,512]{2,1,0:T(8,128)(2,1)S(1)}, bf16[4,2048,512]{2,1,0:T(8,128)(2,1)S(1)}, bf16[4,512,2048]{2,1,0:T(8,128)(2,1)S(1)}, bf16[2,2048,5...) custom-call(s32[4]{0:T(128)S(1)} %pad_add_fusion.4.place_ref, ...), custom_call_target="tpu_custom_call", output_to_operand_aliasing={{6}: (49, {}), {7}: (50, {})} | custom-call | bytes 37748736 | tf_op jit(solution)/shard_map/while/body/eval_jaxpr/pallas_call | solution.py:192
  863.0 56.8 %collective-permute-done.mine_ref = bf16[64,2048]{1,0:T(8,128)(2,1)S(1)} collective-permute-done((bf16[64,2048]{1,0:T(8,128)(2,1)}, bf16[64,2048]{1,0:T(8,128)(2,1)S(1)}, u32[]{:S(2)}, u32[]{:S(2)}) %collective-permute-start) | collective-permute-done | bytes 262176 | tf_op jit(solution)/shard_map/while/body/eval_jaxpr/ppermute | solution.py:342
  921.8 4.8 eval_jaxpr.33
  928.7 6.5 eval_jaxpr.34
  940.0 14.5 %collective-permute-start.49 = (bf16[64,2048]{1,0:T(8,128)(2,1)S(1)}, bf16[64,2048]{1,0:T(8,128)(2,1)S(1)}, u32[]{:S(2)}, u32[]{:S(2)}) collective-permute-start(bf16[64,2048]{1,0:T(8,128)(2,1)S(1)} %get-tuple-element.1576), channel_id=1, source_target_pairs={{0,8},{8,0},{16,24},{24,16},{32,40},{40,32},{48,56},{56,48},{64,72... | collective-permute-start | bytes 786440 | tf_op jit(solution)/shard_map/ppermute | solution.py:362
  954.5 12.1 %collective-permute-done.49 = bf16[64,2048]{1,0:T(8,128)(2,1)S(1)} collective-permute-done((bf16[64,2048]{1,0:T(8,128)(2,1)S(1)}, bf16[64,2048]{1,0:T(8,128)(2,1)S(1)}, u32[]{:S(2)}, u32[]{:S(2)}) %collective-permute-start.49) | collective-permute-done | bytes 262176 | tf_op jit(solution)/shard_map/ppermute | solution.py:362
  (604 shorter events, 309.7 us)
Async XLA Ops:
  1.9 28.5 %collective-permute-start.30 = (bf16[256,2048]{1,0:T(8,128)(2,1)S(1)}, bf16[256,2048]{1,0:T(8,128)(2,1)S(1)}, u32[]{:S(2)}, u32[]{:S(2)}) collective-permute-start(bf16[256,2048]{1,0:T(8,128)(2,1)S(1)} %get-tuple-element.1369), channel_id=1, source_target_pairs={{0,2},{1,3},{2,4},{3,5},{4,6},{5,7},{6,8},{7,9},{8,10},{9,11},{10,... | collective-permute-start | bytes 3145736 | tf_op jit(solution)/shard_map/ppermute | solution.py:288
  3.6 28.0 %collective-permute-start.31 = (bf16[256,2048]{1,0:T(8,128)(2,1)S(1)}, bf16[256,2048]{1,0:T(8,128)(2,1)S(1)}, u32[]{:S(2)}, u32[]{:S(2)}) collective-permute-start(bf16[256,2048]{1,0:T(8,128)(2,1)S(1)} %get-tuple-element.1370), channel_id=1, source_target_pairs={{0,14},{1,15},{2,0},{3,1},{4,2},{5,3},{6,4},{7,5},{8,6},{9,7},{10,... | collective-permute-start | bytes 3145736 | tf_op jit(solution)/shard_map/ppermute | solution.py:289
  7.8 45.1 %collective-permute-start.17 = (bf16[1024,512]{1,0:T(8,128)(2,1)S(1)}, bf16[1024,512]{1,0:T(8,128)(2,1)S(1)}, u32[]{:S(2)}, u32[]{:S(2)}) collective-permute-start(bf16[1024,512]{1,0:T(8,128)(2,1)S(1)} %get-tuple-element.1356), channel_id=1, source_target_pairs={{0,2},{1,3},{2,4},{3,5},{4,6},{5,7},{6,8},{7,9},{8,10},{9,11},{10,... | collective-permute-start | bytes 3145736 | tf_op jit(solution)/shard_map/ppermute | solution.py:288
  7.9 46.2 %collective-permute-start.18 = (bf16[1024,512]{1,0:T(8,128)(2,1)S(1)}, bf16[1024,512]{1,0:T(8,128)(2,1)S(1)}, u32[]{:S(2)}, u32[]{:S(2)}) collective-permute-start(bf16[1024,512]{1,0:T(8,128)(2,1)S(1)} %get-tuple-element.1357), channel_id=1, source_target_pairs={{0,14},{1,15},{2,0},{3,1},{4,2},{5,3},{6,4},{7,5},{8,6},{9,7},{10,... | collective-permute-start | bytes 3145736 | tf_op jit(solution)/shard_map/ppermute | solution.py:289
  10.7 64.7 %collective-permute-start.4 = (bf16[1024,512]{1,0:T(8,128)(2,1)S(1)}, bf16[1024,512]{1,0:T(8,128)(2,1)S(1)}, u32[]{:S(2)}, u32[]{:S(2)}) collective-permute-start(bf16[1024,512]{1,0:T(8,128)(2,1)S(1)} %get-tuple-element.1343), channel_id=1, source_target_pairs={{0,2},{1,3},{2,4},{3,5},{4,6},{5,7},{6,8},{7,9},{8,10},{9,11},{10,... | collective-permute-start | bytes 3145736 | tf_op jit(solution)/shard_map/ppermute | solution.py:288
  30.4 46.1 %collective-permute-start.5 = (bf16[1024,512]{1,0:T(8,128)(2,1)S(1)}, bf16[1024,512]{1,0:T(8,128)(2,1)S(1)}, u32[]{:S(2)}, u32[]{:S(2)}) collective-permute-start(bf16[1024,512]{1,0:T(8,128)(2,1)S(1)} %get-tuple-element.1344), channel_id=1, source_target_pairs={{0,14},{1,15},{2,0},{3,1},{4,2},{5,3},{6,4},{7,5},{8,6},{9,7},{10,... | collective-permute-start | bytes 3145736 | tf_op jit(solution)/shard_map/ppermute | solution.py:289
  31.6 66.3 %collective-permute-start.32 = (bf16[256,2048]{1,0:T(8,128)(2,1)S(1)}, bf16[256,2048]{1,0:T(8,128)(2,1)S(1)}, u32[]{:S(2)}, u32[]{:S(2)}) collective-permute-start(bf16[256,2048]{1,0:T(8,128)(2,1)S(1)} %collective-permute-done.30), channel_id=1, source_target_pairs={{0,2},{1,3},{2,4},{3,5},{4,6},{5,7},{6,8},{7,9},{8,10},{9,11},{10,... | collective-permute-start | bytes 3145736 | tf_op jit(solution)/shard_map/ppermute | solution.py:288
  52.9 46.1 %collective-permute-start.33 = (bf16[256,2048]{1,0:T(8,128)(2,1)S(1)}, bf16[256,2048]{1,0:T(8,128)(2,1)S(1)}, u32[]{:S(2)}, u32[]{:S(2)}) collective-permute-start(bf16[256,2048]{1,0:T(8,128)(2,1)S(1)} %collective-permute-done.31), channel_id=1, source_target_pairs={{0,14},{1,15},{2,0},{3,1},{4,2},{5,3},{6,4},{7,5},{8,6},{9,7},{10,... | collective-permute-start | bytes 3145736 | tf_op jit(solution)/shard_map/ppermute | solution.py:289
  54.0 66.3 %collective-permute-start.19 = (bf16[1024,512]{1,0:T(8,128)(2,1)S(1)}, bf16[1024,512]{1,0:T(8,128)(2,1)S(1)}, u32[]{:S(2)}, u32[]{:S(2)}) collective-permute-start(bf16[1024,512]{1,0:T(8,128)(2,1)S(1)} %collective-permute-done.17), channel_id=1, source_target_pairs={{0,2},{1,3},{2,4},{3,5},{4,6},{5,7},{6,8},{7,9},{8,10},{9,11},{10,... | collective-permute-start | bytes 3145736 | tf_op jit(solution)/shard_map/ppermute | solution.py:288
  75.4 46.1 %collective-permute-start.20 = (bf16[1024,512]{1,0:T(8,128)(2,1)S(1)}, bf16[1024,512]{1,0:T(8,128)(2,1)S(1)}, u32[]{:S(2)}, u32[]{:S(2)}) collective-permute-start(bf16[1024,512]{1,0:T(8,128)(2,1)S(1)} %collective-permute-done.18), channel_id=1, source_target_pairs={{0,14},{1,15},{2,0},{3,1},{4,2},{5,3},{6,4},{7,5},{8,6},{9,7},{10,... | collective-permute-start | bytes 3145736 | tf_op jit(solution)/shard_map/ppermute | solution.py:289
  76.5 66.3 %collective-permute-start.6 = (bf16[1024,512]{1,0:T(8,128)(2,1)S(1)}, bf16[1024,512]{1,0:T(8,128)(2,1)S(1)}, u32[]{:S(2)}, u32[]{:S(2)}) collective-permute-start(bf16[1024,512]{1,0:T(8,128)(2,1)S(1)} %collective-permute-done.4), channel_id=1, source_target_pairs={{0,2},{1,3},{2,4},{3,5},{4,6},{5,7},{6,8},{7,9},{8,10},{9,11},{10,... | collective-permute-start | bytes 3145736 | tf_op jit(solution)/shard_map/ppermute | solution.py:288
  97.8 46.3 %collective-permute-start.7 = (bf16[1024,512]{1,0:T(8,128)(2,1)S(1)}, bf16[1024,512]{1,0:T(8,128)(2,1)S(1)}, u32[]{:S(2)}, u32[]{:S(2)}) collective-permute-start(bf16[1024,512]{1,0:T(8,128)(2,1)S(1)} %collective-permute-done.5), channel_id=1, source_target_pairs={{0,14},{1,15},{2,0},{3,1},{4,2},{5,3},{6,4},{7,5},{8,6},{9,7},{10,... | collective-permute-start | bytes 3145736 | tf_op jit(solution)/shard_map/ppermute | solution.py:289
  99.0 66.3 %collective-permute-start.34 = (bf16[256,2048]{1,0:T(8,128)(2,1)S(1)}, bf16[256,2048]{1,0:T(8,128)(2,1)S(1)}, u32[]{:S(2)}, u32[]{:S(2)}) collective-permute-start(bf16[256,2048]{1,0:T(8,128)(2,1)S(1)} %collective-permute-done.32), channel_id=1, source_target_pairs={{0,2},{1,3},{2,4},{3,5},{4,6},{5,7},{6,8},{7,9},{8,10},{9,11},{10,... | collective-permute-start | bytes 3145736 | tf_op jit(solution)/shard_map/ppermute | solution.py:288
  120.3 46.1 %collective-permute-start.35 = (bf16[256,2048]{1,0:T(8,128)(2,1)S(1)}, bf16[256,2048]{1,0:T(8,128)(2,1)S(1)}, u32[]{:S(2)}, u32[]{:S(2)}) collective-permute-start(bf16[256,2048]{1,0:T(8,128)(2,1)S(1)} %collective-permute-done.33), channel_id=1, source_target_pairs={{0,14},{1,15},{2,0},{3,1},{4,2},{5,3},{6,4},{7,5},{8,6},{9,7},{10,... | collective-permute-start | bytes 3145736 | tf_op jit(solution)/shard_map/ppermute | solution.py:289
  121.5 66.3 %collective-permute-start.21 = (bf16[1024,512]{1,0:T(8,128)(2,1)S(1)}, bf16[1024,512]{1,0:T(8,128)(2,1)S(1)}, u32[]{:S(2)}, u32[]{:S(2)}) collective-permute-start(bf16[1024,512]{1,0:T(8,128)(2,1)S(1)} %collective-permute-done.19), channel_id=1, source_target_pairs={{0,2},{1,3},{2,4},{3,5},{4,6},{5,7},{6,8},{7,9},{8,10},{9,11},{10,... | collective-permute-start | bytes 3145736 | tf_op jit(solution)/shard_map/ppermute | solution.py:288
  142.8 46.1 %collective-permute-start.22 = (bf16[1024,512]{1,0:T(8,128)(2,1)S(1)}, bf16[1024,512]{1,0:T(8,128)(2,1)S(1)}, u32[]{:S(2)}, u32[]{:S(2)}) collective-permute-start(bf16[1024,512]{1,0:T(8,128)(2,1)S(1)} %collective-permute-done.20), channel_id=1, source_target_pairs={{0,14},{1,15},{2,0},{3,1},{4,2},{5,3},{6,4},{7,5},{8,6},{9,7},{10,... | collective-permute-start | bytes 3145736 | tf_op jit(solution)/shard_map/ppermute | solution.py:289
  144.2 66.0 %collective-permute-start.8 = (bf16[1024,512]{1,0:T(8,128)(2,1)S(1)}, bf16[1024,512]{1,0:T(8,128)(2,1)S(1)}, u32[]{:S(2)}, u32[]{:S(2)}) collective-permute-start(bf16[1024,512]{1,0:T(8,128)(2,1)S(1)} %collective-permute-done.6), channel_id=1, source_target_pairs={{0,2},{1,3},{2,4},{3,5},{4,6},{5,7},{6,8},{7,9},{8,10},{9,11},{10,... | collective-permute-start | bytes 3145736 | tf_op jit(solution)/shard_map/ppermute | solution.py:288
  165.2 46.1 %collective-permute-start.9 = (bf16[1024,512]{1,0:T(8,128)(2,1)S(1)}, bf16[1024,512]{1,0:T(8,128)(2,1)S(1)}, u32[]{:S(2)}, u32[]{:S(2)}) collective-permute-start(bf16[1024,512]{1,0:T(8,128)(2,1)S(1)} %collective-permute-done.7), channel_id=1, source_target_pairs={{0,14},{1,15},{2,0},{3,1},{4,2},{5,3},{6,4},{7,5},{8,6},{9,7},{10,... | collective-permute-start | bytes 3145736 | tf_op jit(solution)/shard_map/ppermute | solution.py:289
  166.4 66.3 %collective-permute-start.36 = (bf16[256,2048]{1,0:T(8,128)(2,1)S(1)}, bf16[256,2048]{1,0:T(8,128)(2,1)S(1)}, u32[]{:S(2)}, u32[]{:S(2)}) collective-permute-start(bf16[256,2048]{1,0:T(8,128)(2,1)S(1)} %collective-permute-done.34), channel_id=1, source_target_pairs={{0,2},{1,3},{2,4},{3,5},{4,6},{5,7},{6,8},{7,9},{8,10},{9,11},{10,... | collective-permute-start | bytes 3145736 | tf_op jit(solution)/shard_map/ppermute | solution.py:288
  187.7 46.1 %collective-permute-start.37 = (bf16[256,2048]{1,0:T(8,128)(2,1)S(1)}, bf16[256,2048]{1,0:T(8,128)(2,1)S(1)}, u32[]{:S(2)}, u32[]{:S(2)}) collective-permute-start(bf16[256,2048]{1,0:T(8,128)(2,1)S(1)} %collective-permute-done.35), channel_id=1, source_target_pairs={{0,14},{1,15},{2,0},{3,1},{4,2},{5,3},{6,4},{7,5},{8,6},{9,7},{10,... | collective-permute-start | bytes 3145736 | tf_op jit(solution)/shard_map/ppermute | solution.py:289
  188.9 66.3 %collective-permute-start.23 = (bf16[1024,512]{1,0:T(8,128)(2,1)S(1)}, bf16[1024,512]{1,0:T(8,128)(2,1)S(1)}, u32[]{:S(2)}, u32[]{:S(2)}) collective-permute-start(bf16[1024,512]{1,0:T(8,128)(2,1)S(1)} %collective-permute-done.21), channel_id=1, source_target_pairs={{0,2},{1,3},{2,4},{3,5},{4,6},{5,7},{6,8},{7,9},{8,10},{9,11},{10,... | collective-permute-start | bytes 3145736 | tf_op jit(solution)/shard_map/ppermute | solution.py:288
  210.2 46.1 %collective-permute-start.24 = (bf16[1024,512]{1,0:T(8,128)(2,1)S(1)}, bf16[1024,512]{1,0:T(8,128)(2,1)S(1)}, u32[]{:S(2)}, u32[]{:S(2)}) collective-permute-start(bf16[1024,512]{1,0:T(8,128)(2,1)S(1)} %collective-permute-done.22), channel_id=1, source_target_pairs={{0,14},{1,15},{2,0},{3,1},{4,2},{5,3},{6,4},{7,5},{8,6},{9,7},{10,... | collective-permute-start | bytes 3145736 | tf_op jit(solution)/shard_map/ppermute | solution.py:289
  211.3 66.3 %collective-permute-start.10 = (bf16[1024,512]{1,0:T(8,128)(2,1)S(1)}, bf16[1024,512]{1,0:T(8,128)(2,1)S(1)}, u32[]{:S(2)}, u32[]{:S(2)}) collective-permute-start(bf16[1024,512]{1,0:T(8,128)(2,1)S(1)} %collective-permute-done.8), channel_id=1, source_target_pairs={{0,2},{1,3},{2,4},{3,5},{4,6},{5,7},{6,8},{7,9},{8,10},{9,11},{10,... | collective-permute-start | bytes 3145736 | tf_op jit(solution)/shard_map/ppermute | solution.py:288
  232.7 46.2 %collective-permute-start.11 = (bf16[1024,512]{1,0:T(8,128)(2,1)S(1)}, bf16[1024,512]{1,0:T(8,128)(2,1)}, u32[]{:S(2)}, u32[]{:S(2)}) collective-permute-start(bf16[1024,512]{1,0:T(8,128)(2,1)S(1)} %collective-permute-done.9), channel_id=1, source_target_pairs={{0,14},{1,15},{2,0},{3,1},{4,2},{5,3},{6,4},{7,5},{8,6},{9,7},{10,... | collective-permute-start | bytes 3145736 | tf_op jit(solution)/shard_map/ppermute | solution.py:289
  233.8 66.4 %collective-permute-start.38 = (bf16[256,2048]{1,0:T(8,128)(2,1)S(1)}, bf16[256,2048]{1,0:T(8,128)(2,1)}, u32[]{:S(2)}, u32[]{:S(2)}) collective-permute-start(bf16[256,2048]{1,0:T(8,128)(2,1)S(1)} %collective-permute-done.36), channel_id=1, source_target_pairs={{0,2},{1,3},{2,4},{3,5},{4,6},{5,7},{6,8},{7,9},{8,10},{9,11},{10,... | collective-permute-start | bytes 3145736 | tf_op jit(solution)/shard_map/ppermute | solution.py:288
  255.1 46.2 %collective-permute-start.39 = (bf16[256,2048]{1,0:T(8,128)(2,1)S(1)}, bf16[256,2048]{1,0:T(8,128)(2,1)}, u32[]{:S(2)}, u32[]{:S(2)}) collective-permute-start(bf16[256,2048]{1,0:T(8,128)(2,1)S(1)} %collective-permute-done.37), channel_id=1, source_target_pairs={{0,14},{1,15},{2,0},{3,1},{4,2},{5,3},{6,4},{7,5},{8,6},{9,7},{10,... | collective-permute-start | bytes 3145736 | tf_op jit(solution)/shard_map/ppermute | solution.py:289
  256.3 66.4 %collective-permute-start.25 = (bf16[1024,512]{1,0:T(8,128)(2,1)S(1)}, bf16[1024,512]{1,0:T(8,128)(2,1)}, u32[]{:S(2)}, u32[]{:S(2)}) collective-permute-start(bf16[1024,512]{1,0:T(8,128)(2,1)S(1)} %collective-permute-done.23), channel_id=1, source_target_pairs={{0,2},{1,3},{2,4},{3,5},{4,6},{5,7},{6,8},{7,9},{8,10},{9,11},{10,... | collective-permute-start | bytes 3145736 | tf_op jit(solution)/shard_map/ppermute | solution.py:288
  277.6 46.6 %collective-permute-start.26 = (bf16[1024,512]{1,0:T(8,128)(2,1)S(1)}, bf16[1024,512]{1,0:T(8,128)(2,1)}, u32[]{:S(2)}, u32[]{:S(2)}) collective-permute-start(bf16[1024,512]{1,0:T(8,128)(2,1)S(1)} %collective-permute-done.24), channel_id=1, source_target_pairs={{0,14},{1,15},{2,0},{3,1},{4,2},{5,3},{6,4},{7,5},{8,6},{9,7},{10,... | collective-permute-start | bytes 3145736 | tf_op jit(solution)/shard_map/ppermute | solution.py:289
  278.9 66.2 %collective-permute-start.12 = (bf16[1024,512]{1,0:T(8,128)(2,1)S(1)}, bf16[1024,512]{1,0:T(8,128)(2,1)S(1)}, u32[]{:S(2)}, u32[]{:S(2)}) collective-permute-start(bf16[1024,512]{1,0:T(8,128)(2,1)S(1)} %collective-permute-done.10), channel_id=1, source_target_pairs={{0,2},{1,3},{2,4},{3,5},{4,6},{5,7},{6,8},{7,9},{8,10},{9,11},{10,... | collective-permute-start | bytes 3145736 | tf_op jit(solution)/shard_map/ppermute | solution.py:288
  300.2 47.3 %collective-permute-start.13 = (bf16[1024,512]{1,0:T(8,128)(2,1)}, bf16[1024,512]{1,0:T(8,128)(2,1)}, u32[]{:S(2)}, u32[]{:S(2)}) collective-permute-start(bf16[1024,512]{1,0:T(8,128)(2,1)} %collective-permute-done.11), channel_id=1, source_target_pairs={{0,14},{1,15},{2,0},{3,1},{4,2},{5,3},{6,4},{7,5},{8,6},{9,7},{10,... | collective-permute-start | bytes 3145736 | tf_op jit(solution)/shard_map/ppermute | solution.py:289
  301.3 66.3 %collective-permute-start.40 = (bf16[256,2048]{1,0:T(8,128)(2,1)}, bf16[256,2048]{1,0:T(8,128)(2,1)}, u32[]{:S(2)}, u32[]{:S(2)}) collective-permute-start(bf16[256,2048]{1,0:T(8,128)(2,1)} %collective-permute-done.38), channel_id=1, source_target_pairs={{0,2},{1,3},{2,4},{3,5},{4,6},{5,7},{6,8},{7,9},{8,10},{9,11},{10,... | collective-permute-start | bytes 3145736 | tf_op jit(solution)/shard_map/ppermute | solution.py:288
  322.6 44.9 %collective-permute-start.41 = (bf16[256,2048]{1,0:T(8,128)(2,1)}, bf16[256,2048]{1,0:T(8,128)(2,1)}, u32[]{:S(2)}, u32[]{:S(2)}) collective-permute-start(bf16[256,2048]{1,0:T(8,128)(2,1)} %collective-permute-done.39), channel_id=1, source_target_pairs={{0,14},{1,15},{2,0},{3,1},{4,2},{5,3},{6,4},{7,5},{8,6},{9,7},{10,... | collective-permute-start | bytes 3145736 | tf_op jit(solution)/shard_map/ppermute | solution.py:289
  324.2 71.9 %collective-permute-start.27 = (bf16[1024,512]{1,0:T(8,128)(2,1)}, bf16[1024,512]{1,0:T(8,128)(2,1)}, u32[]{:S(2)}, u32[]{:S(2)}) collective-permute-start(bf16[1024,512]{1,0:T(8,128)(2,1)} %collective-permute-done.25), channel_id=1, source_target_pairs={{0,2},{1,3},{2,4},{3,5},{4,6},{5,7},{6,8},{7,9},{8,10},{9,11},{10,... | collective-permute-start | bytes 3145736 | tf_op jit(solution)/shard_map/ppermute | solution.py:288
  346.0 52.7 %collective-permute-start.28 = (bf16[1024,512]{1,0:T(8,128)(2,1)}, bf16[1024,512]{1,0:T(8,128)(2,1)}, u32[]{:S(2)}, u32[]{:S(2)}) collective-permute-start(bf16[1024,512]{1,0:T(8,128)(2,1)} %collective-permute-done.26), channel_id=1, source_target_pairs={{0,14},{1,15},{2,0},{3,1},{4,2},{5,3},{6,4},{7,5},{8,6},{9,7},{10,... | collective-permute-start | bytes 3145736 | tf_op jit(solution)/shard_map/ppermute | solution.py:289
  347.5 44.2 %collective-permute-start.47 = (s32[8,128,2]{1,2,0:T(2,128)S(1)}, s32[8,128,2]{1,2,0:T(2,128)S(1)}, u32[]{:S(2)}, u32[]{:S(2)}) collective-permute-start(s32[8,128,2]{1,2,0:T(2,128)S(1)} %bitcast.50), channel_id=1, source_target_pairs={{0,8},{8,0},{16,24},{24,16},{32,40},{40,32},{48,56},{56,48},{64,72... | collective-permute-start | bytes 24584 | tf_op jit(solution)/shard_map/ppermute | solution.py:313
  367.6 45.3 %collective-permute-start.14 = (bf16[1024,512]{1,0:T(8,128)(2,1)}, bf16[1024,512]{1,0:T(8,128)(2,1)}, u32[]{:S(2)}, u32[]{:S(2)}) collective-permute-start(bf16[1024,512]{1,0:T(8,128)(2,1)} %copy-done.34), channel_id=1, source_target_pairs={{0,2},{1,3},{2,4},{3,5},{4,6},{5,7},{6,8},{7,9},{8,10},{9,11},{10,... | collective-permute-start | bytes 3145736 | tf_op jit(solution)/shard_map/ppermute | solution.py:288
  367.6 45.3 %collective-permute-start.15 = (bf16[1024,512]{1,0:T(8,128)(2,1)}, bf16[1024,512]{1,0:T(8,128)(2,1)}, u32[]{:S(2)}, u32[]{:S(2)}) collective-permute-start(bf16[1024,512]{1,0:T(8,128)(2,1)} %collective-permute-done.13), channel_id=1, source_target_pairs={{0,14},{1,15},{2,0},{3,1},{4,2},{5,3},{6,4},{7,5},{8,6},{9,7},{10,... | collective-permute-start | bytes 3145736 | tf_op jit(solution)/shard_map/ppermute | solution.py:289
  391.7 69.9 %collective-permute-start.42 = (bf16[256,2048]{1,0:T(8,128)(2,1)}, bf16[256,2048]{1,0:T(8,128)(2,1)}, u32[]{:S(2)}, u32[]{:S(2)}) collective-permute-start(bf16[256,2048]{1,0:T(8,128)(2,1)} %collective-permute-done.41), channel_id=1, source_target_pairs={{0,14},{1,15},{2,0},{3,1},{4,2},{5,3},{6,4},{7,5},{8,6},{9,7},{10,... | collective-permute-start | bytes 3145736 | tf_op jit(solution)/shard_map/ppermute | solution.py:289
  396.0 54.7 %collective-permute-start.48 = (bf16[2048,8]{1,0:T(8,128)(2,1)S(1)}, bf16[2048,8]{1,0:T(8,128)(2,1)S(1)}, u32[]{:S(2)}, u32[]{:S(2)}) collective-permute-start(bf16[2048,8]{1,0:T(8,128)(2,1)S(1)} %bitcast.46), channel_id=1, source_target_pairs={{0,8},{8,0},{16,24},{24,16},{32,40},{40,32},{48,56},{56,48},{64,72... | collective-permute-start | bytes 98312 | tf_op jit(solution)/shard_map/ppermute | solution.py:313
  398.7 28.3 %collective-permute-start.46 = (f32[1,2048]{1,0:T(1,128)S(1)}, f32[1,2048]{1,0:T(1,128)S(1)}, u32[]{:S(2)}, u32[]{:S(2)}) collective-permute-start(f32[1,2048]{1,0:T(1,128)S(1)} %copy-done.39), channel_id=1, source_target_pairs={{0,8},{8,0},{16,24},{24,16},{32,40},{40,32},{48,56},{56,48},{64,72... | collective-permute-start | bytes 24584 | tf_op jit(solution)/shard_map/ppermute | solution.py:313
  412.9 52.0 %collective-permute-start.45 = (bf16[256,2048]{1,0:T(8,128)(2,1)}, bf16[256,2048]{1,0:T(8,128)(2,1)}, u32[]{:S(2)}, u32[]{:S(2)}) collective-permute-start(bf16[256,2048]{1,0:T(8,128)(2,1)} %collective-permute-done.40), channel_id=1, source_target_pairs={{0,2},{1,3},{2,4},{3,5},{4,6},{5,7},{6,8},{7,9},{8,10},{9,11},{10,... | collective-permute-start | bytes 3145736 | tf_op jit(solution)/shard_map/ppermute | solution.py:288
  412.9 66.8 %collective-permute-start.29 = (bf16[1024,512]{1,0:T(8,128)(2,1)}, bf16[1024,512]{1,0:T(8,128)(2,1)}, u32[]{:S(2)}, u32[]{:S(2)}) collective-permute-start(bf16[1024,512]{1,0:T(8,128)(2,1)} %collective-permute-done.28), channel_id=1, source_target_pairs={{0,14},{1,15},{2,0},{3,1},{4,2},{5,3},{6,4},{7,5},{8,6},{9,7},{10,... | collective-permute-start | bytes 3145736 | tf_op jit(solution)/shard_map/ppermute | solution.py:289
  427.0 55.6 %collective-permute-start.44 = (bf16[1024,512]{1,0:T(8,128)(2,1)}, bf16[1024,512]{1,0:T(8,128)(2,1)}, u32[]{:S(2)}, u32[]{:S(2)}) collective-permute-start(bf16[1024,512]{1,0:T(8,128)(2,1)} %collective-permute-done.27), channel_id=1, source_target_pairs={{0,2},{1,3},{2,4},{3,5},{4,6},{5,7},{6,8},{7,9},{8,10},{9,11},{10,... | collective-permute-start | bytes 3145736 | tf_op jit(solution)/shard_map/ppermute | solution.py:288
  450.7 51.4 %collective-permute-start.16 = (bf16[1024,512]{1,0:T(8,128)(2,1)}, bf16[1024,512]{1,0:T(8,128)(2,1)}, u32[]{:S(2)}, u32[]{:S(2)}) collective-permute-start(bf16[1024,512]{1,0:T(8,128)(2,1)} %collective-permute-done.15), channel_id=1, source_target_pairs={{0,14},{1,15},{2,0},{3,1},{4,2},{5,3},{6,4},{7,5},{8,6},{9,7},{10,... | collective-permute-start | bytes 3145736 | tf_op jit(solution)/shard_map/ppermute | solution.py:289
  461.6 43.5 %collective-permute-start.43 = (bf16[1024,512]{1,0:T(8,128)(2,1)}, bf16[1024,512]{1,0:T(8,128)(2,1)}, u32[]{:S(2)}, u32[]{:S(2)}) collective-permute-start(bf16[1024,512]{1,0:T(8,128)(2,1)} %collective-permute-done.14), channel_id=1, source_target_pairs={{0,2},{1,3},{2,4},{3,5},{4,6},{5,7},{6,8},{7,9},{8,10},{9,11},{10,... | collective-permute-start | bytes 3145736 | tf_op jit(solution)/shard_map/ppermute | solution.py:288
  527.3 22.2 %collective-permute-start = (bf16[64,2048]{1,0:T(8,128)(2,1)}, bf16[64,2048]{1,0:T(8,128)(2,1)S(1)}, u32[]{:S(2)}, u32[]{:S(2)}) collective-permute-start(bf16[64,2048]{1,0:T(8,128)(2,1)} %get-tuple-element.2076), channel_id=1, source_target_pairs={{0,16},{8,24},{16,32},{24,40},{32,48},{40,56},{48,64},{56,72},{64,... | collective-permute-start | bytes 786440 | tf_op jit(solution)/shard_map/while/body/eval_jaxpr/ppermute | solution.py:342
  844.6 75.2 %collective-permute-start = (bf16[64,2048]{1,0:T(8,128)(2,1)}, bf16[64,2048]{1,0:T(8,128)(2,1)S(1)}, u32[]{:S(2)}, u32[]{:S(2)}) collective-permute-start(bf16[64,2048]{1,0:T(8,128)(2,1)} %get-tuple-element.2076), channel_id=1, source_target_pairs={{0,16},{8,24},{16,32},{24,40},{32,48},{40,56},{48,64},{56,72},{64,... | collective-permute-start | bytes 786440 | tf_op jit(solution)/shard_map/while/body/eval_jaxpr/ppermute | solution.py:342
  940.0 26.6 %collective-permute-start.49 = (bf16[64,2048]{1,0:T(8,128)(2,1)S(1)}, bf16[64,2048]{1,0:T(8,128)(2,1)S(1)}, u32[]{:S(2)}, u32[]{:S(2)}) collective-permute-start(bf16[64,2048]{1,0:T(8,128)(2,1)S(1)} %get-tuple-element.1576), channel_id=1, source_target_pairs={{0,8},{8,0},{16,24},{24,16},{32,40},{40,32},{48,56},{56,48},{64,72... | collective-permute-start | bytes 786440 | tf_op jit(solution)/shard_map/ppermute | solution.py:362
  (222 other events, 3582.7 us)

commit v6 on v5

--- a/solution.py
+++ b/solution.py
@@ -158,10 +158,6 @@
         base_ref[...] = middle_ref[...] + total[:count]
         lent_ref[...] = total[count:].astype(jnp.bfloat16)
         put_away.wait()
-
-
-def add_kernel(base_ref, back_ref, sent_ref):
-    sent_ref[...] = (base_ref[...] + back_ref[...].astype(jnp.float32)).astype(jnp.bfloat16)
 
 
 def vmem(count):
@@ -254,16 +250,6 @@
     )(place, mine, other, part, back, scale, ids, router, *ready, *sources)
 
 
-def run_add(base, back):
-    return pl.pallas_call(
-        add_kernel,
-        out_shape=like(base.shape, jnp.bfloat16),
-        in_specs=vmem(2),
-        out_specs=vmem(1)[0],
-        compiler_params=pltpu.CompilerParams(vmem_limit_bytes=3 << 20),
-    )(base, back)
-
-
 def device_at(ring, z, core):
     half = z_size // 2
     return (ring * 2 + z // half) * z_size + (z % half) * 2 + core
@@ -349,7 +335,8 @@
             place, mine, other, part, back, scales[1], ids[1], routers[1], ready, sources
         )
         back = exchange(lent)
-        return run_add(base, back), middle, base, back, stored
+        sent = (base + back.astype(jnp.float32)).astype(jnp.bfloat16)
+        return sent, middle, base, back, stored
 
     blank = jnp.zeros(entering.shape, jnp.float32)
     state = (entering, blank, blank, entering, (blank, blank + 0))

time: 978 us -> 978 us (level)
  other arithmetic: 4.93 us -> 32.4 us
  Pallas kernels: 101 us -> 73.7 us
    convert_element_type x0 -> x16, other arithmetic: none -> 27.5 us  [ring_step(): sent = (base + back.astype(jnp.float32)).astype(jnp.bfloat16)]
    pallas_call x16 -> x0, Pallas kernels: 27.4 us -> none  [run_add(): pl.pallas_call(add_kernel, out_shape=like(base.shape, jnp.bfloat16), in_s...]
where the time goes in v6:
time: 978 us; the launch traced here: 968 us
  waiting for transfers between devices  606 us (62%)
  starting transfers between devices  227 us (23%)
  Pallas kernels  73.7 us (8%)
  other arithmetic  32.4 us (3%)
  local copies, waits for them, and re-layouts  27.5 us (3%)
    ppermute x21, waiting for transfers between devices, gather_ring(): travelling[m] = lax.ppermute(pair[0], both, forward)  347 us
    ppermute x16, waiting for transfers between devices, ring_step(): mine = lax.ppermute(sent, 'section', next_ring)  116 us
    ppermute x16, starting transfers between devices, ring_step(): mine = lax.ppermute(sent, 'section', next_ring)  93.8 us
    ppermute x48, waiting for transfers between devices, exchange(): return lax.ppermute(value, 'expert', other_core)  63.9 us
    ppermute x21, starting transfers between devices, gather_ring(): travelling[m + 1] = lax.ppermute(pair[1], both, backward)  42.7 us
    ppermute x48, starting transfers between devices, exchange(): return lax.ppermute(value, 'expert', other_core)  36.9 us
    pallas_call x16, Pallas kernels, load_ahead(): pl.pallas_call(load_kernel, out_shape=tuple((pltpu.VMEM(shape, jnp.bfloat...  36.5 us
    ppermute x21, waiting for transfers between devices, gather_ring(): travelling[m + 1] = lax.ppermute(pair[1], both, backward)  34.5 us
  transfers between devices with their start and end apart: 110, of which 88 were waited for; matrix products, arithmetic and copies ran while one was open for 1% of the time, Pallas kernels for 4%

profile of v6, /device:TPU:31, one launch (start us, length us, event | category | flops | bytes accessed | tf_op | source)
XLA Modules:
  0.0 967.9 jit_solution(15862429726290134121)
XLA Ops:
  3.6 4.0 collective-permute-start.31
  10.8 19.7 %collective-permute-done.30 = bf16[256,2048]{1,0:T(8,128)(2,1)S(1)} collective-permute-done((bf16[256,2048]{1,0:T(8,128)(2,1)S(1)}, bf16[256,2048]{1,0:T(8,128)(2,1)S(1)}, u32[]{:S(2)}, u32[]{:S(2)}) %collective-permute-start.30) | collective-permute-done | bytes 1048608 | tf_op jit(solution)/shard_map/ppermute | solution.py:274
  32.0 20.9 %collective-permute-done.17 = bf16[1024,512]{1,0:T(8,128)(2,1)S(1)} collective-permute-done((bf16[1024,512]{1,0:T(8,128)(2,1)S(1)}, bf16[1024,512]{1,0:T(8,128)(2,1)S(1)}, u32[]{:S(2)}, u32[]{:S(2)}) %collective-permute-start.17) | collective-permute-done | bytes 1048608 | tf_op jit(solution)/shard_map/ppermute | solution.py:274
  54.4 21.0 %collective-permute-done.4 = bf16[1024,512]{1,0:T(8,128)(2,1)S(1)} collective-permute-done((bf16[1024,512]{1,0:T(8,128)(2,1)S(1)}, bf16[1024,512]{1,0:T(8,128)(2,1)S(1)}, u32[]{:S(2)}, u32[]{:S(2)}) %collective-permute-start.4) | collective-permute-done | bytes 1048608 | tf_op jit(solution)/shard_map/ppermute | solution.py:274
  76.8 21.0 %collective-permute-done.32 = bf16[256,2048]{1,0:T(8,128)(2,1)S(1)} collective-permute-done((bf16[256,2048]{1,0:T(8,128)(2,1)S(1)}, bf16[256,2048]{1,0:T(8,128)(2,1)S(1)}, u32[]{:S(2)}, u32[]{:S(2)}) %collective-permute-start.32) | collective-permute-done | bytes 1048608 | tf_op jit(solution)/shard_map/ppermute | solution.py:274
  99.4 20.9 %collective-permute-done.19 = bf16[1024,512]{1,0:T(8,128)(2,1)S(1)} collective-permute-done((bf16[1024,512]{1,0:T(8,128)(2,1)S(1)}, bf16[1024,512]{1,0:T(8,128)(2,1)S(1)}, u32[]{:S(2)}, u32[]{:S(2)}) %collective-permute-start.19) | collective-permute-done | bytes 1048608 | tf_op jit(solution)/shard_map/ppermute | solution.py:274
  121.9 20.9 %collective-permute-done.6 = bf16[1024,512]{1,0:T(8,128)(2,1)S(1)} collective-permute-done((bf16[1024,512]{1,0:T(8,128)(2,1)S(1)}, bf16[1024,512]{1,0:T(8,128)(2,1)S(1)}, u32[]{:S(2)}, u32[]{:S(2)}) %collective-permute-start.6) | collective-permute-done | bytes 1048608 | tf_op jit(solution)/shard_map/ppermute | solution.py:274
  144.5 20.7 %collective-permute-done.34 = bf16[256,2048]{1,0:T(8,128)(2,1)S(1)} collective-permute-done((bf16[256,2048]{1,0:T(8,128)(2,1)S(1)}, bf16[256,2048]{1,0:T(8,128)(2,1)S(1)}, u32[]{:S(2)}, u32[]{:S(2)}) %collective-permute-start.34) | collective-permute-done | bytes 1048608 | tf_op jit(solution)/shard_map/ppermute | solution.py:274
  166.8 20.9 %collective-permute-done.21 = bf16[1024,512]{1,0:T(8,128)(2,1)S(1)} collective-permute-done((bf16[1024,512]{1,0:T(8,128)(2,1)S(1)}, bf16[1024,512]{1,0:T(8,128)(2,1)S(1)}, u32[]{:S(2)}, u32[]{:S(2)}) %collective-permute-start.21) | collective-permute-done | bytes 1048608 | tf_op jit(solution)/shard_map/ppermute | solution.py:274
  189.3 20.9 %collective-permute-done.8 = bf16[1024,512]{1,0:T(8,128)(2,1)S(1)} collective-permute-done((bf16[1024,512]{1,0:T(8,128)(2,1)S(1)}, bf16[1024,512]{1,0:T(8,128)(2,1)S(1)}, u32[]{:S(2)}, u32[]{:S(2)}) %collective-permute-start.8) | collective-permute-done | bytes 1048608 | tf_op jit(solution)/shard_map/ppermute | solution.py:274
  211.7 20.9 %collective-permute-done.36 = bf16[256,2048]{1,0:T(8,128)(2,1)S(1)} collective-permute-done((bf16[256,2048]{1,0:T(8,128)(2,1)S(1)}, bf16[256,2048]{1,0:T(8,128)(2,1)S(1)}, u32[]{:S(2)}, u32[]{:S(2)}) %collective-permute-start.36) | collective-permute-done | bytes 1048608 | tf_op jit(solution)/shard_map/ppermute | solution.py:274
  234.2 20.9 %collective-permute-done.23 = bf16[1024,512]{1,0:T(8,128)(2,1)S(1)} collective-permute-done((bf16[1024,512]{1,0:T(8,128)(2,1)S(1)}, bf16[1024,512]{1,0:T(8,128)(2,1)S(1)}, u32[]{:S(2)}, u32[]{:S(2)}) %collective-permute-start.23) | collective-permute-done | bytes 1048608 | tf_op jit(solution)/shard_map/ppermute | solution.py:274
  256.7 20.9 %collective-permute-done.10 = bf16[1024,512]{1,0:T(8,128)(2,1)S(1)} collective-permute-done((bf16[1024,512]{1,0:T(8,128)(2,1)S(1)}, bf16[1024,512]{1,0:T(8,128)(2,1)S(1)}, u32[]{:S(2)}, u32[]{:S(2)}) %collective-permute-start.10) | collective-permute-done | bytes 1048608 | tf_op jit(solution)/shard_map/ppermute | solution.py:274
  279.1 21.1 %collective-permute-done.38 = bf16[256,2048]{1,0:T(8,128)(2,1)} collective-permute-done((bf16[256,2048]{1,0:T(8,128)(2,1)S(1)}, bf16[256,2048]{1,0:T(8,128)(2,1)}, u32[]{:S(2)}, u32[]{:S(2)}) %collective-permute-start.38) | collective-permute-done | bytes 1048608 | tf_op jit(solution)/shard_map/ppermute | solution.py:274
  301.7 21.0 %collective-permute-done.25 = bf16[1024,512]{1,0:T(8,128)(2,1)} collective-permute-done((bf16[1024,512]{1,0:T(8,128)(2,1)S(1)}, bf16[1024,512]{1,0:T(8,128)(2,1)}, u32[]{:S(2)}, u32[]{:S(2)}) %collective-permute-start.25) | collective-permute-done | bytes 1048608 | tf_op jit(solution)/shard_map/ppermute | solution.py:274
  324.5 20.5 %collective-permute-done.12 = bf16[1024,512]{1,0:T(8,128)(2,1)S(1)} collective-permute-done((bf16[1024,512]{1,0:T(8,128)(2,1)S(1)}, bf16[1024,512]{1,0:T(8,128)(2,1)S(1)}, u32[]{:S(2)}, u32[]{:S(2)}) %collective-permute-start.12) | collective-permute-done | bytes 1048608 | tf_op jit(solution)/shard_map/ppermute | solution.py:274
  350.1 17.5 %collective-permute-done.40 = bf16[256,2048]{1,0:T(8,128)(2,1)} collective-permute-done((bf16[256,2048]{1,0:T(8,128)(2,1)}, bf16[256,2048]{1,0:T(8,128)(2,1)}, u32[]{:S(2)}, u32[]{:S(2)}) %collective-permute-start.40) | collective-permute-done | bytes 1048608 | tf_op jit(solution)/shard_map/ppermute | solution.py:274
  370.3 21.5 %collective-permute-done.47 = s32[8,128,2]{1,2,0:T(2,128)S(1)} collective-permute-done((s32[8,128,2]{1,2,0:T(2,128)S(1)}, s32[8,128,2]{1,2,0:T(2,128)S(1)}, u32[]{:S(2)}, u32[]{:S(2)}) %collective-permute-start.47) | collective-permute-done | bytes 8224 | tf_op jit(solution)/shard_map/ppermute | solution.py:299
  401.9 11.0 %collective-permute-done.14 = bf16[1024,512]{1,0:T(8,128)(2,1)} collective-permute-done((bf16[1024,512]{1,0:T(8,128)(2,1)}, bf16[1024,512]{1,0:T(8,128)(2,1)}, u32[]{:S(2)}, u32[]{:S(2)}) %collective-permute-start.14) | collective-permute-done | bytes 1048608 | tf_op jit(solution)/shard_map/ppermute | solution.py:274
  415.6 11.4 %collective-permute-done.46 = f32[1,2048]{1,0:T(1,128)S(1)} collective-permute-done((f32[1,2048]{1,0:T(1,128)S(1)}, f32[1,2048]{1,0:T(1,128)S(1)}, u32[]{:S(2)}, u32[]{:S(2)}) %collective-permute-start.46) | collective-permute-done | bytes 8224 | tf_op jit(solution)/shard_map/ppermute | solution.py:299
  427.0 23.8 %collective-permute-start.44 = (bf16[1024,512]{1,0:T(8,128)(2,1)}, bf16[1024,512]{1,0:T(8,128)(2,1)}, u32[]{:S(2)}, u32[]{:S(2)}) collective-permute-start(bf16[1024,512]{1,0:T(8,128)(2,1)} %collective-permute-done.27), channel_id=1, source_target_pairs={{0,2},{1,3},{2,4},{3,5},{4,6},{5,7},{6,8},{7,9},{8,10},{9,11},{10,... | collective-permute-start | bytes 3145736 | tf_op jit(solution)/shard_map/ppermute | solution.py:274
  450.7 10.8 %collective-permute-start.16 = (bf16[1024,512]{1,0:T(8,128)(2,1)}, bf16[1024,512]{1,0:T(8,128)(2,1)}, u32[]{:S(2)}, u32[]{:S(2)}) collective-permute-start(bf16[1024,512]{1,0:T(8,128)(2,1)} %collective-permute-done.15), channel_id=1, source_target_pairs={{0,14},{1,15},{2,0},{3,1},{4,2},{5,3},{6,4},{7,5},{8,6},{9,7},{10,... | collective-permute-start | bytes 3145736 | tf_op jit(solution)/shard_map/ppermute | solution.py:275
  464.8 14.8 %collective-permute-done.29 = bf16[1024,512]{1,0:T(8,128)(2,1)} collective-permute-done((bf16[1024,512]{1,0:T(8,128)(2,1)}, bf16[1024,512]{1,0:T(8,128)(2,1)}, u32[]{:S(2)}, u32[]{:S(2)}) %collective-permute-start.29) | collective-permute-done | bytes 1048608 | tf_op jit(solution)/shard_map/ppermute | solution.py:275
  482.6 19.6 %collective-permute-done.16 = bf16[1024,512]{1,0:T(8,128)(2,1)} collective-permute-done((bf16[1024,512]{1,0:T(8,128)(2,1)}, bf16[1024,512]{1,0:T(8,128)(2,1)}, u32[]{:S(2)}, u32[]{:S(2)}) %collective-permute-start.16) | collective-permute-done | bytes 1048608 | tf_op jit(solution)/shard_map/ppermute | solution.py:275
  507.6 431.1 %while.25 = (s32[]{:T(128)}, bf16[64,2048]{1,0:T(8,128)(2,1)}, f32[64,2048]{1,0:T(8,128)}, f32[64,2048]{1,0:T(8,128)S(1)}, bf16[64,2048]{1,0:T(8,128)(2,1)}, /*i...) while((s32[]{:T(128)}, bf16[64,2048]{1,0:T(8,128)(2,1)}, ...), condition=%wide.region_1.2_spmd, body=%wide.region_0.1_spmd.sunk | while | flops 393235 | bytes 83887072 | solution.py:343
  513.3 4.5 collective-permute-start.1
  527.3 16.5 %collective-permute-start = (bf16[64,2048]{1,0:T(8,128)(2,1)}, bf16[64,2048]{1,0:T(8,128)(2,1)S(1)}, u32[]{:S(2)}, u32[]{:S(2)}) collective-permute-start(bf16[64,2048]{1,0:T(8,128)(2,1)} %get-tuple-element.2076), channel_id=1, source_target_pairs={{0,16},{8,24},{16,32},{24,40},{32,48},{40,56},{48,64},{56,72},{64,... | collective-permute-start | bytes 786440 | tf_op jit(solution)/shard_map/while/body/eval_jaxpr/ppermute | solution.py:328
  560.2 5.4 collective-permute-start
  581.9 5.4 collective-permute-start
  603.7 5.4 collective-permute-start
  625.5 5.4 collective-permute-start
  647.2 5.4 collective-permute-start
  654.3 4.0 collective-permute-done.mine_ref
  669.0 5.4 collective-permute-start
  690.8 5.4 collective-permute-start
  712.5 6.8 collective-permute-start
  735.7 5.4 collective-permute-start
  757.5 5.4 collective-permute-start
  779.3 5.4 collective-permute-start
  801.0 5.4 collective-permute-start
  822.8 5.4 collective-permute-start
  844.6 5.4 collective-permute-start
  850.1 12.9 %eval_jaxpr.24 = (bf16[4,2048,512]{2,1,0:T(8,128)(2,1)S(1)}, bf16[4,2048,512]{2,1,0:T(8,128)(2,1)S(1)}, bf16[4,512,2048]{2,1,0:T(8,128)(2,1)S(1)}, bf16[2,2048,5...) custom-call(s32[4]{0:T(128)S(1)} %pad_add_fusion.4.place_ref, ...), custom_call_target="tpu_custom_call", output_to_operand_aliasing={{6}: (49, {}), {7}: (50, {})} | custom-call | bytes 37748736 | tf_op jit(solution)/shard_map/while/body/eval_jaxpr/pallas_call | solution.py:188
  863.0 56.8 %collective-permute-done.mine_ref = bf16[64,2048]{1,0:T(8,128)(2,1)S(1)} collective-permute-done((bf16[64,2048]{1,0:T(8,128)(2,1)}, bf16[64,2048]{1,0:T(8,128)(2,1)S(1)}, u32[]{:S(2)}, u32[]{:S(2)}) %collective-permute-start) | collective-permute-done | bytes 262176 | tf_op jit(solution)/shard_map/while/body/eval_jaxpr/ppermute | solution.py:328
  921.9 4.8 eval_jaxpr.25
  928.7 6.5 eval_jaxpr.26
  940.1 14.5 %collective-permute-start.49 = (bf16[64,2048]{1,0:T(8,128)(2,1)S(1)}, bf16[64,2048]{1,0:T(8,128)(2,1)S(1)}, u32[]{:S(2)}, u32[]{:S(2)}) collective-permute-start(bf16[64,2048]{1,0:T(8,128)(2,1)S(1)} %get-tuple-element.1576), channel_id=1, source_target_pairs={{0,8},{8,0},{16,24},{24,16},{32,40},{40,32},{48,56},{56,48},{64,72... | collective-permute-start | bytes 786440 | tf_op jit(solution)/shard_map/ppermute | solution.py:349
  954.5 12.1 %collective-permute-done.49 = bf16[64,2048]{1,0:T(8,128)(2,1)S(1)} collective-permute-done((bf16[64,2048]{1,0:T(8,128)(2,1)S(1)}, bf16[64,2048]{1,0:T(8,128)(2,1)S(1)}, u32[]{:S(2)}, u32[]{:S(2)}) %collective-permute-start.49) | collective-permute-done | bytes 262176 | tf_op jit(solution)/shard_map/ppermute | solution.py:349
  (604 shorter events, 309.7 us)
Async XLA Ops:
  1.9 28.5 %collective-permute-start.30 = (bf16[256,2048]{1,0:T(8,128)(2,1)S(1)}, bf16[256,2048]{1,0:T(8,128)(2,1)S(1)}, u32[]{:S(2)}, u32[]{:S(2)}) collective-permute-start(bf16[256,2048]{1,0:T(8,128)(2,1)S(1)} %get-tuple-element.1369), channel_id=1, source_target_pairs={{0,2},{1,3},{2,4},{3,5},{4,6},{5,7},{6,8},{7,9},{8,10},{9,11},{10,... | collective-permute-start | bytes 3145736 | tf_op jit(solution)/shard_map/ppermute | solution.py:274
  3.6 28.0 %collective-permute-start.31 = (bf16[256,2048]{1,0:T(8,128)(2,1)S(1)}, bf16[256,2048]{1,0:T(8,128)(2,1)S(1)}, u32[]{:S(2)}, u32[]{:S(2)}) collective-permute-start(bf16[256,2048]{1,0:T(8,128)(2,1)S(1)} %get-tuple-element.1370), channel_id=1, source_target_pairs={{0,14},{1,15},{2,0},{3,1},{4,2},{5,3},{6,4},{7,5},{8,6},{9,7},{10,... | collective-permute-start | bytes 3145736 | tf_op jit(solution)/shard_map/ppermute | solution.py:275
  7.8 45.1 %collective-permute-start.17 = (bf16[1024,512]{1,0:T(8,128)(2,1)S(1)}, bf16[1024,512]{1,0:T(8,128)(2,1)S(1)}, u32[]{:S(2)}, u32[]{:S(2)}) collective-permute-start(bf16[1024,512]{1,0:T(8,128)(2,1)S(1)} %get-tuple-element.1356), channel_id=1, source_target_pairs={{0,2},{1,3},{2,4},{3,5},{4,6},{5,7},{6,8},{7,9},{8,10},{9,11},{10,... | collective-permute-start | bytes 3145736 | tf_op jit(solution)/shard_map/ppermute | solution.py:274
  7.9 46.2 %collective-permute-start.18 = (bf16[1024,512]{1,0:T(8,128)(2,1)S(1)}, bf16[1024,512]{1,0:T(8,128)(2,1)S(1)}, u32[]{:S(2)}, u32[]{:S(2)}) collective-permute-start(bf16[1024,512]{1,0:T(8,128)(2,1)S(1)} %get-tuple-element.1357), channel_id=1, source_target_pairs={{0,14},{1,15},{2,0},{3,1},{4,2},{5,3},{6,4},{7,5},{8,6},{9,7},{10,... | collective-permute-start | bytes 3145736 | tf_op jit(solution)/shard_map/ppermute | solution.py:275
  10.7 64.7 %collective-permute-start.4 = (bf16[1024,512]{1,0:T(8,128)(2,1)S(1)}, bf16[1024,512]{1,0:T(8,128)(2,1)S(1)}, u32[]{:S(2)}, u32[]{:S(2)}) collective-permute-start(bf16[1024,512]{1,0:T(8,128)(2,1)S(1)} %get-tuple-element.1343), channel_id=1, source_target_pairs={{0,2},{1,3},{2,4},{3,5},{4,6},{5,7},{6,8},{7,9},{8,10},{9,11},{10,... | collective-permute-start | bytes 3145736 | tf_op jit(solution)/shard_map/ppermute | solution.py:274
  30.4 46.1 %collective-permute-start.5 = (bf16[1024,512]{1,0:T(8,128)(2,1)S(1)}, bf16[1024,512]{1,0:T(8,128)(2,1)S(1)}, u32[]{:S(2)}, u32[]{:S(2)}) collective-permute-start(bf16[1024,512]{1,0:T(8,128)(2,1)S(1)} %get-tuple-element.1344), channel_id=1, source_target_pairs={{0,14},{1,15},{2,0},{3,1},{4,2},{5,3},{6,4},{7,5},{8,6},{9,7},{10,... | collective-permute-start | bytes 3145736 | tf_op jit(solution)/shard_map/ppermute | solution.py:275
  31.6 66.3 %collective-permute-start.32 = (bf16[256,2048]{1,0:T(8,128)(2,1)S(1)}, bf16[256,2048]{1,0:T(8,128)(2,1)S(1)}, u32[]{:S(2)}, u32[]{:S(2)}) collective-permute-start(bf16[256,2048]{1,0:T(8,128)(2,1)S(1)} %collective-permute-done.30), channel_id=1, source_target_pairs={{0,2},{1,3},{2,4},{3,5},{4,6},{5,7},{6,8},{7,9},{8,10},{9,11},{10,... | collective-permute-start | bytes 3145736 | tf_op jit(solution)/shard_map/ppermute | solution.py:274
  52.9 46.1 %collective-permute-start.33 = (bf16[256,2048]{1,0:T(8,128)(2,1)S(1)}, bf16[256,2048]{1,0:T(8,128)(2,1)S(1)}, u32[]{:S(2)}, u32[]{:S(2)}) collective-permute-start(bf16[256,2048]{1,0:T(8,128)(2,1)S(1)} %collective-permute-done.31), channel_id=1, source_target_pairs={{0,14},{1,15},{2,0},{3,1},{4,2},{5,3},{6,4},{7,5},{8,6},{9,7},{10,... | collective-permute-start | bytes 3145736 | tf_op jit(solution)/shard_map/ppermute | solution.py:275
  54.0 66.3 %collective-permute-start.19 = (bf16[1024,512]{1,0:T(8,128)(2,1)S(1)}, bf16[1024,512]{1,0:T(8,128)(2,1)S(1)}, u32[]{:S(2)}, u32[]{:S(2)}) collective-permute-start(bf16[1024,512]{1,0:T(8,128)(2,1)S(1)} %collective-permute-done.17), channel_id=1, source_target_pairs={{0,2},{1,3},{2,4},{3,5},{4,6},{5,7},{6,8},{7,9},{8,10},{9,11},{10,... | collective-permute-start | bytes 3145736 | tf_op jit(solution)/shard_map/ppermute | solution.py:274
  75.4 46.1 %collective-permute-start.20 = (bf16[1024,512]{1,0:T(8,128)(2,1)S(1)}, bf16[1024,512]{1,0:T(8,128)(2,1)S(1)}, u32[]{:S(2)}, u32[]{:S(2)}) collective-permute-start(bf16[1024,512]{1,0:T(8,128)(2,1)S(1)} %collective-permute-done.18), channel_id=1, source_target_pairs={{0,14},{1,15},{2,0},{3,1},{4,2},{5,3},{6,4},{7,5},{8,6},{9,7},{10,... | collective-permute-start | bytes 3145736 | tf_op jit(solution)/shard_map/ppermute | solution.py:275
  76.5 66.3 %collective-permute-start.6 = (bf16[1024,512]{1,0:T(8,128)(2,1)S(1)}, bf16[1024,512]{1,0:T(8,128)(2,1)S(1)}, u32[]{:S(2)}, u32[]{:S(2)}) collective-permute-start(bf16[1024,512]{1,0:T(8,128)(2,1)S(1)} %collective-permute-done.4), channel_id=1, source_target_pairs={{0,2},{1,3},{2,4},{3,5},{4,6},{5,7},{6,8},{7,9},{8,10},{9,11},{10,... | collective-permute-start | bytes 3145736 | tf_op jit(solution)/shard_map/ppermute | solution.py:274
  97.8 46.3 %collective-permute-start.7 = (bf16[1024,512]{1,0:T(8,128)(2,1)S(1)}, bf16[1024,512]{1,0:T(8,128)(2,1)S(1)}, u32[]{:S(2)}, u32[]{:S(2)}) collective-permute-start(bf16[1024,512]{1,0:T(8,128)(2,1)S(1)} %collective-permute-done.5), channel_id=1, source_target_pairs={{0,14},{1,15},{2,0},{3,1},{4,2},{5,3},{6,4},{7,5},{8,6},{9,7},{10,... | collective-permute-start | bytes 3145736 | tf_op jit(solution)/shard_map/ppermute | solution.py:275
  99.0 66.3 %collective-permute-start.34 = (bf16[256,2048]{1,0:T(8,128)(2,1)S(1)}, bf16[256,2048]{1,0:T(8,128)(2,1)S(1)}, u32[]{:S(2)}, u32[]{:S(2)}) collective-permute-start(bf16[256,2048]{1,0:T(8,128)(2,1)S(1)} %collective-permute-done.32), channel_id=1, source_target_pairs={{0,2},{1,3},{2,4},{3,5},{4,6},{5,7},{6,8},{7,9},{8,10},{9,11},{10,... | collective-permute-start | bytes 3145736 | tf_op jit(solution)/shard_map/ppermute | solution.py:274
  120.3 46.1 %collective-permute-start.35 = (bf16[256,2048]{1,0:T(8,128)(2,1)S(1)}, bf16[256,2048]{1,0:T(8,128)(2,1)S(1)}, u32[]{:S(2)}, u32[]{:S(2)}) collective-permute-start(bf16[256,2048]{1,0:T(8,128)(2,1)S(1)} %collective-permute-done.33), channel_id=1, source_target_pairs={{0,14},{1,15},{2,0},{3,1},{4,2},{5,3},{6,4},{7,5},{8,6},{9,7},{10,... | collective-permute-start | bytes 3145736 | tf_op jit(solution)/shard_map/ppermute | solution.py:275
  121.5 66.3 %collective-permute-start.21 = (bf16[1024,512]{1,0:T(8,128)(2,1)S(1)}, bf16[1024,512]{1,0:T(8,128)(2,1)S(1)}, u32[]{:S(2)}, u32[]{:S(2)}) collective-permute-start(bf16[1024,512]{1,0:T(8,128)(2,1)S(1)} %collective-permute-done.19), channel_id=1, source_target_pairs={{0,2},{1,3},{2,4},{3,5},{4,6},{5,7},{6,8},{7,9},{8,10},{9,11},{10,... | collective-permute-start | bytes 3145736 | tf_op jit(solution)/shard_map/ppermute | solution.py:274
  142.8 46.1 %collective-permute-start.22 = (bf16[1024,512]{1,0:T(8,128)(2,1)S(1)}, bf16[1024,512]{1,0:T(8,128)(2,1)S(1)}, u32[]{:S(2)}, u32[]{:S(2)}) collective-permute-start(bf16[1024,512]{1,0:T(8,128)(2,1)S(1)} %collective-permute-done.20), channel_id=1, source_target_pairs={{0,14},{1,15},{2,0},{3,1},{4,2},{5,3},{6,4},{7,5},{8,6},{9,7},{10,... | collective-permute-start | bytes 3145736 | tf_op jit(solution)/shard_map/ppermute | solution.py:275
  144.2 66.0 %collective-permute-start.8 = (bf16[1024,512]{1,0:T(8,128)(2,1)S(1)}, bf16[1024,512]{1,0:T(8,128)(2,1)S(1)}, u32[]{:S(2)}, u32[]{:S(2)}) collective-permute-start(bf16[1024,512]{1,0:T(8,128)(2,1)S(1)} %collective-permute-done.6), channel_id=1, source_target_pairs={{0,2},{1,3},{2,4},{3,5},{4,6},{5,7},{6,8},{7,9},{8,10},{9,11},{10,... | collective-permute-start | bytes 3145736 | tf_op jit(solution)/shard_map/ppermute | solution.py:274
  165.2 46.1 %collective-permute-start.9 = (bf16[1024,512]{1,0:T(8,128)(2,1)S(1)}, bf16[1024,512]{1,0:T(8,128)(2,1)S(1)}, u32[]{:S(2)}, u32[]{:S(2)}) collective-permute-start(bf16[1024,512]{1,0:T(8,128)(2,1)S(1)} %collective-permute-done.7), channel_id=1, source_target_pairs={{0,14},{1,15},{2,0},{3,1},{4,2},{5,3},{6,4},{7,5},{8,6},{9,7},{10,... | collective-permute-start | bytes 3145736 | tf_op jit(solution)/shard_map/ppermute | solution.py:275
  166.4 66.3 %collective-permute-start.36 = (bf16[256,2048]{1,0:T(8,128)(2,1)S(1)}, bf16[256,2048]{1,0:T(8,128)(2,1)S(1)}, u32[]{:S(2)}, u32[]{:S(2)}) collective-permute-start(bf16[256,2048]{1,0:T(8,128)(2,1)S(1)} %collective-permute-done.34), channel_id=1, source_target_pairs={{0,2},{1,3},{2,4},{3,5},{4,6},{5,7},{6,8},{7,9},{8,10},{9,11},{10,... | collective-permute-start | bytes 3145736 | tf_op jit(solution)/shard_map/ppermute | solution.py:274
  187.7 46.1 %collective-permute-start.37 = (bf16[256,2048]{1,0:T(8,128)(2,1)S(1)}, bf16[256,2048]{1,0:T(8,128)(2,1)S(1)}, u32[]{:S(2)}, u32[]{:S(2)}) collective-permute-start(bf16[256,2048]{1,0:T(8,128)(2,1)S(1)} %collective-permute-done.35), channel_id=1, source_target_pairs={{0,14},{1,15},{2,0},{3,1},{4,2},{5,3},{6,4},{7,5},{8,6},{9,7},{10,... | collective-permute-start | bytes 3145736 | tf_op jit(solution)/shard_map/ppermute | solution.py:275
  188.9 66.3 %collective-permute-start.23 = (bf16[1024,512]{1,0:T(8,128)(2,1)S(1)}, bf16[1024,512]{1,0:T(8,128)(2,1)S(1)}, u32[]{:S(2)}, u32[]{:S(2)}) collective-permute-start(bf16[1024,512]{1,0:T(8,128)(2,1)S(1)} %collective-permute-done.21), channel_id=1, source_target_pairs={{0,2},{1,3},{2,4},{3,5},{4,6},{5,7},{6,8},{7,9},{8,10},{9,11},{10,... | collective-permute-start | bytes 3145736 | tf_op jit(solution)/shard_map/ppermute | solution.py:274
  210.2 46.1 %collective-permute-start.24 = (bf16[1024,512]{1,0:T(8,128)(2,1)S(1)}, bf16[1024,512]{1,0:T(8,128)(2,1)S(1)}, u32[]{:S(2)}, u32[]{:S(2)}) collective-permute-start(bf16[1024,512]{1,0:T(8,128)(2,1)S(1)} %collective-permute-done.22), channel_id=1, source_target_pairs={{0,14},{1,15},{2,0},{3,1},{4,2},{5,3},{6,4},{7,5},{8,6},{9,7},{10,... | collective-permute-start | bytes 3145736 | tf_op jit(solution)/shard_map/ppermute | solution.py:275
  211.3 66.3 %collective-permute-start.10 = (bf16[1024,512]{1,0:T(8,128)(2,1)S(1)}, bf16[1024,512]{1,0:T(8,128)(2,1)S(1)}, u32[]{:S(2)}, u32[]{:S(2)}) collective-permute-start(bf16[1024,512]{1,0:T(8,128)(2,1)S(1)} %collective-permute-done.8), channel_id=1, source_target_pairs={{0,2},{1,3},{2,4},{3,5},{4,6},{5,7},{6,8},{7,9},{8,10},{9,11},{10,... | collective-permute-start | bytes 3145736 | tf_op jit(solution)/shard_map/ppermute | solution.py:274
  232.7 46.2 %collective-permute-start.11 = (bf16[1024,512]{1,0:T(8,128)(2,1)S(1)}, bf16[1024,512]{1,0:T(8,128)(2,1)}, u32[]{:S(2)}, u32[]{:S(2)}) collective-permute-start(bf16[1024,512]{1,0:T(8,128)(2,1)S(1)} %collective-permute-done.9), channel_id=1, source_target_pairs={{0,14},{1,15},{2,0},{3,1},{4,2},{5,3},{6,4},{7,5},{8,6},{9,7},{10,... | collective-permute-start | bytes 3145736 | tf_op jit(solution)/shard_map/ppermute | solution.py:275
  233.8 66.4 %collective-permute-start.38 = (bf16[256,2048]{1,0:T(8,128)(2,1)S(1)}, bf16[256,2048]{1,0:T(8,128)(2,1)}, u32[]{:S(2)}, u32[]{:S(2)}) collective-permute-start(bf16[256,2048]{1,0:T(8,128)(2,1)S(1)} %collective-permute-done.36), channel_id=1, source_target_pairs={{0,2},{1,3},{2,4},{3,5},{4,6},{5,7},{6,8},{7,9},{8,10},{9,11},{10,... | collective-permute-start | bytes 3145736 | tf_op jit(solution)/shard_map/ppermute | solution.py:274
  255.1 46.2 %collective-permute-start.39 = (bf16[256,2048]{1,0:T(8,128)(2,1)S(1)}, bf16[256,2048]{1,0:T(8,128)(2,1)}, u32[]{:S(2)}, u32[]{:S(2)}) collective-permute-start(bf16[256,2048]{1,0:T(8,128)(2,1)S(1)} %collective-permute-done.37), channel_id=1, source_target_pairs={{0,14},{1,15},{2,0},{3,1},{4,2},{5,3},{6,4},{7,5},{8,6},{9,7},{10,... | collective-permute-start | bytes 3145736 | tf_op jit(solution)/shard_map/ppermute | solution.py:275
  256.3 66.4 %collective-permute-start.25 = (bf16[1024,512]{1,0:T(8,128)(2,1)S(1)}, bf16[1024,512]{1,0:T(8,128)(2,1)}, u32[]{:S(2)}, u32[]{:S(2)}) collective-permute-start(bf16[1024,512]{1,0:T(8,128)(2,1)S(1)} %collective-permute-done.23), channel_id=1, source_target_pairs={{0,2},{1,3},{2,4},{3,5},{4,6},{5,7},{6,8},{7,9},{8,10},{9,11},{10,... | collective-permute-start | bytes 3145736 | tf_op jit(solution)/shard_map/ppermute | solution.py:274
  277.6 46.6 %collective-permute-start.26 = (bf16[1024,512]{1,0:T(8,128)(2,1)S(1)}, bf16[1024,512]{1,0:T(8,128)(2,1)}, u32[]{:S(2)}, u32[]{:S(2)}) collective-permute-start(bf16[1024,512]{1,0:T(8,128)(2,1)S(1)} %collective-permute-done.24), channel_id=1, source_target_pairs={{0,14},{1,15},{2,0},{3,1},{4,2},{5,3},{6,4},{7,5},{8,6},{9,7},{10,... | collective-permute-start | bytes 3145736 | tf_op jit(solution)/shard_map/ppermute | solution.py:275
  278.9 66.2 %collective-permute-start.12 = (bf16[1024,512]{1,0:T(8,128)(2,1)S(1)}, bf16[1024,512]{1,0:T(8,128)(2,1)S(1)}, u32[]{:S(2)}, u32[]{:S(2)}) collective-permute-start(bf16[1024,512]{1,0:T(8,128)(2,1)S(1)} %collective-permute-done.10), channel_id=1, source_target_pairs={{0,2},{1,3},{2,4},{3,5},{4,6},{5,7},{6,8},{7,9},{8,10},{9,11},{10,... | collective-permute-start | bytes 3145736 | tf_op jit(solution)/shard_map/ppermute | solution.py:274
  300.2 47.3 %collective-permute-start.13 = (bf16[1024,512]{1,0:T(8,128)(2,1)}, bf16[1024,512]{1,0:T(8,128)(2,1)}, u32[]{:S(2)}, u32[]{:S(2)}) collective-permute-start(bf16[1024,512]{1,0:T(8,128)(2,1)} %collective-permute-done.11), channel_id=1, source_target_pairs={{0,14},{1,15},{2,0},{3,1},{4,2},{5,3},{6,4},{7,5},{8,6},{9,7},{10,... | collective-permute-start | bytes 3145736 | tf_op jit(solution)/shard_map/ppermute | solution.py:275
  301.3 66.3 %collective-permute-start.40 = (bf16[256,2048]{1,0:T(8,128)(2,1)}, bf16[256,2048]{1,0:T(8,128)(2,1)}, u32[]{:S(2)}, u32[]{:S(2)}) collective-permute-start(bf16[256,2048]{1,0:T(8,128)(2,1)} %collective-permute-done.38), channel_id=1, source_target_pairs={{0,2},{1,3},{2,4},{3,5},{4,6},{5,7},{6,8},{7,9},{8,10},{9,11},{10,... | collective-permute-start | bytes 3145736 | tf_op jit(solution)/shard_map/ppermute | solution.py:274
  322.6 44.9 %collective-permute-start.41 = (bf16[256,2048]{1,0:T(8,128)(2,1)}, bf16[256,2048]{1,0:T(8,128)(2,1)}, u32[]{:S(2)}, u32[]{:S(2)}) collective-permute-start(bf16[256,2048]{1,0:T(8,128)(2,1)} %collective-permute-done.39), channel_id=1, source_target_pairs={{0,14},{1,15},{2,0},{3,1},{4,2},{5,3},{6,4},{7,5},{8,6},{9,7},{10,... | collective-permute-start | bytes 3145736 | tf_op jit(solution)/shard_map/ppermute | solution.py:275
  324.2 71.9 %collective-permute-start.27 = (bf16[1024,512]{1,0:T(8,128)(2,1)}, bf16[1024,512]{1,0:T(8,128)(2,1)}, u32[]{:S(2)}, u32[]{:S(2)}) collective-permute-start(bf16[1024,512]{1,0:T(8,128)(2,1)} %collective-permute-done.25), channel_id=1, source_target_pairs={{0,2},{1,3},{2,4},{3,5},{4,6},{5,7},{6,8},{7,9},{8,10},{9,11},{10,... | collective-permute-start | bytes 3145736 | tf_op jit(solution)/shard_map/ppermute | solution.py:274
  346.0 52.7 %collective-permute-start.28 = (bf16[1024,512]{1,0:T(8,128)(2,1)}, bf16[1024,512]{1,0:T(8,128)(2,1)}, u32[]{:S(2)}, u32[]{:S(2)}) collective-permute-start(bf16[1024,512]{1,0:T(8,128)(2,1)} %collective-permute-done.26), channel_id=1, source_target_pairs={{0,14},{1,15},{2,0},{3,1},{4,2},{5,3},{6,4},{7,5},{8,6},{9,7},{10,... | collective-permute-start | bytes 3145736 | tf_op jit(solution)/shard_map/ppermute | solution.py:275
  347.5 44.2 %collective-permute-start.47 = (s32[8,128,2]{1,2,0:T(2,128)S(1)}, s32[8,128,2]{1,2,0:T(2,128)S(1)}, u32[]{:S(2)}, u32[]{:S(2)}) collective-permute-start(s32[8,128,2]{1,2,0:T(2,128)S(1)} %bitcast.50), channel_id=1, source_target_pairs={{0,8},{8,0},{16,24},{24,16},{32,40},{40,32},{48,56},{56,48},{64,72... | collective-permute-start | bytes 24584 | tf_op jit(solution)/shard_map/ppermute | solution.py:299
  367.6 45.3 %collective-permute-start.14 = (bf16[1024,512]{1,0:T(8,128)(2,1)}, bf16[1024,512]{1,0:T(8,128)(2,1)}, u32[]{:S(2)}, u32[]{:S(2)}) collective-permute-start(bf16[1024,512]{1,0:T(8,128)(2,1)} %copy-done.34), channel_id=1, source_target_pairs={{0,2},{1,3},{2,4},{3,5},{4,6},{5,7},{6,8},{7,9},{8,10},{9,11},{10,... | collective-permute-start | bytes 3145736 | tf_op jit(solution)/shard_map/ppermute | solution.py:274
  367.6 45.3 %collective-permute-start.15 = (bf16[1024,512]{1,0:T(8,128)(2,1)}, bf16[1024,512]{1,0:T(8,128)(2,1)}, u32[]{:S(2)}, u32[]{:S(2)}) collective-permute-start(bf16[1024,512]{1,0:T(8,128)(2,1)} %collective-permute-done.13), channel_id=1, source_target_pairs={{0,14},{1,15},{2,0},{3,1},{4,2},{5,3},{6,4},{7,5},{8,6},{9,7},{10,... | collective-permute-start | bytes 3145736 | tf_op jit(solution)/shard_map/ppermute | solution.py:275
  391.7 69.9 %collective-permute-start.42 = (bf16[256,2048]{1,0:T(8,128)(2,1)}, bf16[256,2048]{1,0:T(8,128)(2,1)}, u32[]{:S(2)}, u32[]{:S(2)}) collective-permute-start(bf16[256,2048]{1,0:T(8,128)(2,1)} %collective-permute-done.41), channel_id=1, source_target_pairs={{0,14},{1,15},{2,0},{3,1},{4,2},{5,3},{6,4},{7,5},{8,6},{9,7},{10,... | collective-permute-start | bytes 3145736 | tf_op jit(solution)/shard_map/ppermute | solution.py:275
  396.0 54.7 %collective-permute-start.48 = (bf16[2048,8]{1,0:T(8,128)(2,1)S(1)}, bf16[2048,8]{1,0:T(8,128)(2,1)S(1)}, u32[]{:S(2)}, u32[]{:S(2)}) collective-permute-start(bf16[2048,8]{1,0:T(8,128)(2,1)S(1)} %bitcast.46), channel_id=1, source_target_pairs={{0,8},{8,0},{16,24},{24,16},{32,40},{40,32},{48,56},{56,48},{64,72... | collective-permute-start | bytes 98312 | tf_op jit(solution)/shard_map/ppermute | solution.py:299
  398.7 28.3 %collective-permute-start.46 = (f32[1,2048]{1,0:T(1,128)S(1)}, f32[1,2048]{1,0:T(1,128)S(1)}, u32[]{:S(2)}, u32[]{:S(2)}) collective-permute-start(f32[1,2048]{1,0:T(1,128)S(1)} %copy-done.39), channel_id=1, source_target_pairs={{0,8},{8,0},{16,24},{24,16},{32,40},{40,32},{48,56},{56,48},{64,72... | collective-permute-start | bytes 24584 | tf_op jit(solution)/shard_map/ppermute | solution.py:299
  412.9 52.0 %collective-permute-start.45 = (bf16[256,2048]{1,0:T(8,128)(2,1)}, bf16[256,2048]{1,0:T(8,128)(2,1)}, u32[]{:S(2)}, u32[]{:S(2)}) collective-permute-start(bf16[256,2048]{1,0:T(8,128)(2,1)} %collective-permute-done.40), channel_id=1, source_target_pairs={{0,2},{1,3},{2,4},{3,5},{4,6},{5,7},{6,8},{7,9},{8,10},{9,11},{10,... | collective-permute-start | bytes 3145736 | tf_op jit(solution)/shard_map/ppermute | solution.py:274
  412.9 66.8 %collective-permute-start.29 = (bf16[1024,512]{1,0:T(8,128)(2,1)}, bf16[1024,512]{1,0:T(8,128)(2,1)}, u32[]{:S(2)}, u32[]{:S(2)}) collective-permute-start(bf16[1024,512]{1,0:T(8,128)(2,1)} %collective-permute-done.28), channel_id=1, source_target_pairs={{0,14},{1,15},{2,0},{3,1},{4,2},{5,3},{6,4},{7,5},{8,6},{9,7},{10,... | collective-permute-start | bytes 3145736 | tf_op jit(solution)/shard_map/ppermute | solution.py:275
  427.0 55.6 %collective-permute-start.44 = (bf16[1024,512]{1,0:T(8,128)(2,1)}, bf16[1024,512]{1,0:T(8,128)(2,1)}, u32[]{:S(2)}, u32[]{:S(2)}) collective-permute-start(bf16[1024,512]{1,0:T(8,128)(2,1)} %collective-permute-done.27), channel_id=1, source_target_pairs={{0,2},{1,3},{2,4},{3,5},{4,6},{5,7},{6,8},{7,9},{8,10},{9,11},{10,... | collective-permute-start | bytes 3145736 | tf_op jit(solution)/shard_map/ppermute | solution.py:274
  450.7 51.4 %collective-permute-start.16 = (bf16[1024,512]{1,0:T(8,128)(2,1)}, bf16[1024,512]{1,0:T(8,128)(2,1)}, u32[]{:S(2)}, u32[]{:S(2)}) collective-permute-start(bf16[1024,512]{1,0:T(8,128)(2,1)} %collective-permute-done.15), channel_id=1, source_target_pairs={{0,14},{1,15},{2,0},{3,1},{4,2},{5,3},{6,4},{7,5},{8,6},{9,7},{10,... | collective-permute-start | bytes 3145736 | tf_op jit(solution)/shard_map/ppermute | solution.py:275
  461.6 43.5 %collective-permute-start.43 = (bf16[1024,512]{1,0:T(8,128)(2,1)}, bf16[1024,512]{1,0:T(8,128)(2,1)}, u32[]{:S(2)}, u32[]{:S(2)}) collective-permute-start(bf16[1024,512]{1,0:T(8,128)(2,1)} %collective-permute-done.14), channel_id=1, source_target_pairs={{0,2},{1,3},{2,4},{3,5},{4,6},{5,7},{6,8},{7,9},{8,10},{9,11},{10,... | collective-permute-start | bytes 3145736 | tf_op jit(solution)/shard_map/ppermute | solution.py:274
  527.3 22.2 %collective-permute-start = (bf16[64,2048]{1,0:T(8,128)(2,1)}, bf16[64,2048]{1,0:T(8,128)(2,1)S(1)}, u32[]{:S(2)}, u32[]{:S(2)}) collective-permute-start(bf16[64,2048]{1,0:T(8,128)(2,1)} %get-tuple-element.2076), channel_id=1, source_target_pairs={{0,16},{8,24},{16,32},{24,40},{32,48},{40,56},{48,64},{56,72},{64,... | collective-permute-start | bytes 786440 | tf_op jit(solution)/shard_map/while/body/eval_jaxpr/ppermute | solution.py:328
  844.6 75.2 %collective-permute-start = (bf16[64,2048]{1,0:T(8,128)(2,1)}, bf16[64,2048]{1,0:T(8,128)(2,1)S(1)}, u32[]{:S(2)}, u32[]{:S(2)}) collective-permute-start(bf16[64,2048]{1,0:T(8,128)(2,1)} %get-tuple-element.2076), channel_id=1, source_target_pairs={{0,16},{8,24},{16,32},{24,40},{32,48},{40,56},{48,64},{56,72},{64,... | collective-permute-start | bytes 786440 | tf_op jit(solution)/shard_map/while/body/eval_jaxpr/ppermute | solution.py:328
  940.1 26.5 %collective-permute-start.49 = (bf16[64,2048]{1,0:T(8,128)(2,1)S(1)}, bf16[64,2048]{1,0:T(8,128)(2,1)S(1)}, u32[]{:S(2)}, u32[]{:S(2)}) collective-permute-start(bf16[64,2048]{1,0:T(8,128)(2,1)S(1)} %get-tuple-element.1576), channel_id=1, source_target_pairs={{0,8},{8,0},{16,24},{24,16},{32,40},{40,32},{48,56},{56,48},{64,72... | collective-permute-start | bytes 786440 | tf_op jit(solution)/shard_map/ppermute | solution.py:349
  (222 other events, 3582.7 us)
